TPU v7x, 128 devices: a whole 4x4x4 slice. The times are simulated.
128 devices in a mesh: col: 16 (over x, y), row: 8 (over z, core).
Axes of the slice: x: 4, y: 4, z: 4, core: 2. Of those that a mesh axis runs over, the one named last changes fastest.
Arguments:
- right_side: float32 [8, 128, 32, 128], P(None, ('col', 'row')), may hold values from -6 to 6
- lower_inverse: float32 [8, 128, 128, 128], P(None, ('col', 'row')), as said below
- lower_blocks: bfloat16 [7, 16, 8, 8, 4, 128, 128], P(None, 'col', None, 'row'), may hold values from -0.046875 to 0.046875
- lower_pattern: int32 [7, 16, 8, 8, 4], P(None, 'col', None, 'row'), may hold values from 0 to 111, as said below
- upper_inverse: float32 [8, 128, 128, 128], P(None, ('col', 'row')), as said below
- upper_blocks: bfloat16 [7, 16, 8, 8, 4, 128, 128], P(None, 'col', None, 'row'), may hold values from -0.046875 to 0.046875
- upper_pattern: int32 [7, 16, 8, 8, 4], P(None, 'col', None, 'row'), may hold values from 16 to 127, as said below
Outputs:
- forward_solution: float32 [8, 128, 32, 128], P(None, ('col', 'row'))
- solution: float32 [8, 128, 32, 128], P(None, ('col', 'row'))
Inputs may be any that keep to these rules, and one draw needn't show every extreme that they name: `lower_pattern`: an L block of level i + 1 points at a supernode of levels 0 to i. `upper_pattern`: A U block of level i points at a supernode of levels i + 1 to 7. `lower_inverse`: lower triangular. `upper_inverse`: upper triangular.
All inputs are finite; a program needn't handle non-finite values.
Results may differ from a plain program's by a relative error of at most 0.003.
Values may be sent and summed in bfloat16 or wider, within the bound.
No kernel may reach another device: no remote copies, remote signals or barrier semaphores. Data moves between devices by JAX's collectives and lax.ppermute only.
A program may use at most 64 MiB of HBM per device.

v0:
```python
import jax
import jax.numpy as jnp
from jax import lax
from jax.sharding import PartitionSpec as P


def apply_inverse(inverse, vectors):
    return jnp.einsum("xi,oi->xo", vectors, inverse, precision=lax.Precision.HIGHEST)


def level_terms(history, blocks, pattern):
    picked = history[pattern]
    return jnp.einsum("msxj,msoj->mxo", picked, blocks, preferred_element_type=jnp.float32)


def reduce_rows(partial_value):
    return lax.psum_scatter(partial_value, "row", scatter_dimension=0, tiled=True)[0]


def share_solved(solved):
    return lax.all_gather(solved.astype(jnp.bfloat16)[None], "col", axis=0, tiled=True)


def per_device(
    right_side,
    lower_inverse,
    lower_blocks,
    lower_pattern,
    upper_inverse,
    upper_blocks,
    upper_pattern,
):
    col_count = lax.axis_size("col")
    tiers = right_side.shape[0]
    right_rows = right_side[:, 0]
    low_inv = lower_inverse[:, 0]
    high_inv = upper_inverse[:, 0]
    low_blocks = lower_blocks[:, 0, :, 0]
    low_pattern = lower_pattern[:, 0, :, 0]
    high_blocks = upper_blocks[:, 0, :, 0]
    high_pattern = upper_pattern[:, 0, :, 0]
    block_shape = right_rows.shape[1:]
    history = jnp.zeros((tiers * col_count,) + block_shape, jnp.bfloat16)
    forward_list = []
    for tier_index in range(tiers):
        residual_now = right_rows[tier_index]
        if tier_index > 0:
            partial_value = level_terms(
                history, low_blocks[tier_index - 1], low_pattern[tier_index - 1]
            )
            residual_now = residual_now - reduce_rows(partial_value)
        solved = apply_inverse(low_inv[tier_index], residual_now)
        forward_list.append(solved)
        if tier_index < tiers - 1:
            history = history.at[tier_index * col_count : (tier_index + 1) * col_count].set(
                share_solved(solved)
            )
    history = jnp.zeros((tiers * col_count,) + block_shape, jnp.bfloat16)
    backward_list = [None] * tiers
    for tier_index in range(tiers - 1, -1, -1):
        residual_now = forward_list[tier_index]
        if tier_index < tiers - 1:
            partial_value = level_terms(history, high_blocks[tier_index], high_pattern[tier_index])
            residual_now = residual_now - reduce_rows(partial_value)
        solved = apply_inverse(high_inv[tier_index], residual_now)
        backward_list[tier_index] = solved
        if tier_index > 0:
            history = history.at[tier_index * col_count : (tier_index + 1) * col_count].set(
                share_solved(solved)
            )
    return (jnp.stack(forward_list)[:, None], jnp.stack(backward_list)[:, None])


def solution(mesh):
    in_specs = (
        P(None, ("col", "row"), None, None),
        P(None, ("col", "row"), None, None),
        P(None, "col", None, "row", None, None, None),
        P(None, "col", None, "row", None),
        P(None, ("col", "row"), None, None),
        P(None, "col", None, "row", None, None, None),
        P(None, "col", None, "row", None),
    )
    out_specs = (P(None, ("col", "row"), None, None), P(None, ("col", "row"), None, None))
    return jax.shard_map(
        per_device, mesh=mesh, in_specs=in_specs, out_specs=out_specs, check_vma=False
    )
```

profile of v0, /device:TPU:1, one launch (start us, length us, event | category | flops | bytes accessed | tf_op | source)
XLA Modules:
  0.0 790.2 jit_solution(12615136783307037932)
XLA Ops:
  8.4 19.5 %all-gather = bf16[512,128]{1,0:T(8,128)(2,1)S(1)} all-gather(bf16[32,128]{1,0:T(8,128)(2,1)S(1)} %convert_element_type.42), channel_id=2, replica_groups=mesh['col'=16,'row'=8] {'col'}, dimensions={0}, use_global_device_ids=true | all-gather | bytes 139264 | tf_op jit(solution)/shard_map/all_gather | solution.py:21
  32.3 33.1 %reduce-scatter.15.cloned.1.call-done = f32[1,32,128]{2,1,0:T(8,128)} async-done(((f32[8,32,128]{2,1,0:T(8,128)}), f32[1,32,128]{2,1,0:T(8,128)}) %reduce-scatter.15.cloned.1.call-update) | async-done | bytes 16400 | tf_op jit(solution)/shard_map/reduce_scatter | solution.py:17
  66.5 18.8 %all-gather.1 = bf16[512,128]{1,0:T(8,128)(2,1)S(1)} all-gather(bf16[32,128]{1,0:T(8,128)(2,1)S(1)} %convert_element_type.43), channel_id=3, replica_groups=mesh['col'=16,'row'=8] {'col'}, dimensions={0}, use_global_device_ids=true | all-gather | bytes 139264 | tf_op jit(solution)/shard_map/all_gather | solution.py:21
  88.5 32.1 %reduce-scatter.17.cloned.1.call-done = f32[1,32,128]{2,1,0:T(8,128)} async-done(((f32[8,32,128]{2,1,0:T(8,128)}), f32[1,32,128]{2,1,0:T(8,128)}) %reduce-scatter.17.cloned.1.call-update) | async-done | bytes 16400 | tf_op jit(solution)/shard_map/reduce_scatter | solution.py:17
  121.8 18.8 %all-gather.2 = bf16[512,128]{1,0:T(8,128)(2,1)S(1)} all-gather(bf16[32,128]{1,0:T(8,128)(2,1)S(1)} %convert_element_type.44), channel_id=4, replica_groups=mesh['col'=16,'row'=8] {'col'}, dimensions={0}, use_global_device_ids=true | all-gather | bytes 139264 | tf_op jit(solution)/shard_map/all_gather | solution.py:21
  143.8 32.1 %reduce-scatter.19.cloned.1.call-done = f32[1,32,128]{2,1,0:T(8,128)} async-done(((f32[8,32,128]{2,1,0:T(8,128)}), f32[1,32,128]{2,1,0:T(8,128)}) %reduce-scatter.19.cloned.1.call-update) | async-done | bytes 16400 | tf_op jit(solution)/shard_map/reduce_scatter | solution.py:17
  176.8 18.8 %all-gather.3 = bf16[512,128]{1,0:T(8,128)(2,1)S(1)} all-gather(bf16[32,128]{1,0:T(8,128)(2,1)S(1)} %convert_element_type.45), channel_id=5, replica_groups=mesh['col'=16,'row'=8] {'col'}, dimensions={0}, use_global_device_ids=true | all-gather | bytes 139264 | tf_op jit(solution)/shard_map/all_gather | solution.py:21
  198.8 32.2 %reduce-scatter.21.cloned.1.call-done = f32[1,32,128]{2,1,0:T(8,128)} async-done(((f32[8,32,128]{2,1,0:T(8,128)}), f32[1,32,128]{2,1,0:T(8,128)}) %reduce-scatter.21.cloned.1.call-update) | async-done | bytes 16400 | tf_op jit(solution)/shard_map/reduce_scatter | solution.py:17
  253.9 32.1 %reduce-scatter.23.cloned.1.call-done = f32[1,32,128]{2,1,0:T(8,128)} async-done(((f32[8,32,128]{2,1,0:T(8,128)}), f32[1,32,128]{2,1,0:T(8,128)}) %reduce-scatter.23.cloned.1.call-update) | async-done | bytes 16400 | tf_op jit(solution)/shard_map/reduce_scatter | solution.py:17
  286.9 18.8 %all-gather.5 = bf16[512,128]{1,0:T(8,128)(2,1)S(1)} all-gather(bf16[32,128]{1,0:T(8,128)(2,1)S(1)} %convert_element_type.47), channel_id=7, replica_groups=mesh['col'=16,'row'=8] {'col'}, dimensions={0}, use_global_device_ids=true | all-gather | bytes 139264 | tf_op jit(solution)/shard_map/all_gather | solution.py:21
  309.0 32.2 %reduce-scatter.25.cloned.1.call-done = f32[1,32,128]{2,1,0:T(8,128)} async-done(((f32[8,32,128]{2,1,0:T(8,128)}), f32[1,32,128]{2,1,0:T(8,128)}) %reduce-scatter.25.cloned.1.call-update) | async-done | bytes 16400 | tf_op jit(solution)/shard_map/reduce_scatter | solution.py:17
  364.0 32.1 %reduce-scatter.27.cloned.1.call-done = f32[1,32,128]{2,1,0:T(8,128)} async-done(((f32[8,32,128]{2,1,0:T(8,128)}), f32[1,32,128]{2,1,0:T(8,128)}) %reduce-scatter.27.cloned.1.call-update) | async-done | bytes 16400 | tf_op jit(solution)/shard_map/reduce_scatter | solution.py:17
  397.3 18.8 %all-gather.7 = bf16[512,128]{1,0:T(8,128)(2,1)S(1)} all-gather(bf16[32,128]{1,0:T(8,128)(2,1)S(1)} %get-tuple-element.204), channel_id=9, replica_groups=mesh['col'=16,'row'=8] {'col'}, dimensions={0}, use_global_device_ids=true | all-gather | bytes 139264 | tf_op jit(solution)/shard_map/all_gather | solution.py:21
  419.4 32.2 %reduce-scatter.29.cloned.1.call-done = f32[1,32,128]{2,1,0:T(8,128)} async-done(((f32[8,32,128]{2,1,0:T(8,128)}), f32[1,32,128]{2,1,0:T(8,128)}) %reduce-scatter.29.cloned.1.call-update) | async-done | bytes 16400 | tf_op jit(solution)/shard_map/reduce_scatter | solution.py:17
  452.5 18.8 %all-gather.8 = bf16[512,128]{1,0:T(8,128)(2,1)S(1)} all-gather(bf16[32,128]{1,0:T(8,128)(2,1)S(1)} %get-tuple-element.206), channel_id=10, replica_groups=mesh['col'=16,'row'=8] {'col'}, dimensions={0}, use_global_device_ids=true | all-gather | bytes 139264 | tf_op jit(solution)/shard_map/all_gather | solution.py:21
  474.5 32.1 %reduce-scatter.31.cloned.1.call-done = f32[1,32,128]{2,1,0:T(8,128)} async-done(((f32[8,32,128]{2,1,0:T(8,128)}), f32[1,32,128]{2,1,0:T(8,128)}) %reduce-scatter.31.cloned.1.call-update) | async-done | bytes 16400 | tf_op jit(solution)/shard_map/reduce_scatter | solution.py:17
  529.6 32.2 %reduce-scatter.33.cloned.1.call-done = f32[1,32,128]{2,1,0:T(8,128)} async-done(((f32[8,32,128]{2,1,0:T(8,128)}), f32[1,32,128]{2,1,0:T(8,128)}) %reduce-scatter.33.cloned.1.call-update) | async-done | bytes 16400 | tf_op jit(solution)/shard_map/reduce_scatter | solution.py:17
  584.6 32.1 %reduce-scatter.35.cloned.1.call-done = f32[1,32,128]{2,1,0:T(8,128)} async-done(((f32[8,32,128]{2,1,0:T(8,128)}), f32[1,32,128]{2,1,0:T(8,128)}) %reduce-scatter.35.cloned.1.call-update) | async-done | bytes 16400 | tf_op jit(solution)/shard_map/reduce_scatter | solution.py:17
  617.6 18.8 %all-gather.11 = bf16[512,128]{1,0:T(8,128)(2,1)S(1)} all-gather(bf16[32,128]{1,0:T(8,128)(2,1)S(1)} %get-tuple-element.212), channel_id=13, replica_groups=mesh['col'=16,'row'=8] {'col'}, dimensions={0}, use_global_device_ids=true | all-gather | bytes 139264 | tf_op jit(solution)/shard_map/all_gather | solution.py:21
  639.7 32.1 %reduce-scatter.37.cloned.1.call-done = f32[1,32,128]{2,1,0:T(8,128)} async-done(((f32[8,32,128]{2,1,0:T(8,128)}), f32[1,32,128]{2,1,0:T(8,128)}) %reduce-scatter.37.cloned.1.call-update) | async-done | bytes 16400 | tf_op jit(solution)/shard_map/reduce_scatter | solution.py:17
  672.7 18.8 %all-gather.12 = bf16[512,128]{1,0:T(8,128)(2,1)S(1)} all-gather(bf16[32,128]{1,0:T(8,128)(2,1)S(1)} %get-tuple-element.214), channel_id=14, replica_groups=mesh['col'=16,'row'=8] {'col'}, dimensions={0}, use_global_device_ids=true | all-gather | bytes 139264 | tf_op jit(solution)/shard_map/all_gather | solution.py:21
  694.8 32.1 %reduce-scatter.39.cloned.1.call-done = f32[1,32,128]{2,1,0:T(8,128)} async-done(((f32[8,32,128]{2,1,0:T(8,128)}), f32[1,32,128]{2,1,0:T(8,128)}) %reduce-scatter.39.cloned.1.call-update) | async-done | bytes 16400 | tf_op jit(solution)/shard_map/reduce_scatter | solution.py:17
  727.9 18.8 %all-gather.13 = bf16[512,128]{1,0:T(8,128)(2,1)S(1)} all-gather(bf16[32,128]{1,0:T(8,128)(2,1)S(1)} %get-tuple-element.216), channel_id=15, replica_groups=mesh['col'=16,'row'=8] {'col'}, dimensions={0}, use_global_device_ids=true | all-gather | bytes 139264 | tf_op jit(solution)/shard_map/all_gather | solution.py:21
  749.6 32.4 %reduce-scatter.41.cloned.1.call-done = f32[1,32,128]{2,1,0:T(8,128)} async-done(((f32[8,32,128]{2,1,0:T(8,128)}), f32[1,32,128]{2,1,0:T(8,128)}) %reduce-scatter.41.cloned.1.call-update) | async-done | bytes 16400 | tf_op jit(solution)/shard_map/reduce_scatter | solution.py:17
  (157 shorter events, 135.9 us)
Async XLA Ops:
  7.2 168.7 %copy-start = (f32[8,1,128,128]{3,2,1,0:T(8,128)S(1)}, f32[8,1,128,128]{3,2,1,0:T(8,128)}, u32[]{:S(2)}) copy-start(f32[8,1,128,128]{3,2,1,0:T(8,128)} %param.36) | copy-start | bytes 1572868
  7.2 168.7 %copy-start.2 = (f32[8,1,32,128]{3,2,1,0:T(8,128)S(1)}, f32[8,1,32,128]{3,2,1,0:T(8,128)}, u32[]{:S(2)}) copy-start(f32[8,1,32,128]{3,2,1,0:T(8,128)} %param.35) | copy-start | bytes 393220
  7.2 58.2 %reduce-scatter.15.cloned.1.call-start = ((), (), s32[]{:S(2)}) async-start(), calls=%async_computation.14 | async-start | bytes 147456 | tf_op jit(solution)/shard_map/reduce_scatter | solution.py:17
  32.0 88.6 %reduce-scatter.17.cloned.1.call-start = ((), (), s32[]{:S(2)}) async-start(), calls=%async_computation.15 | async-start | bytes 147456 | tf_op jit(solution)/shard_map/reduce_scatter | solution.py:17
  85.9 311.2 %copy-start.1 = (f32[8,1,128,128]{3,2,1,0:T(8,128)S(1)}, f32[8,1,128,128]{3,2,1,0:T(8,128)}, u32[]{:S(2)}) copy-start(f32[8,1,128,128]{3,2,1,0:T(8,128)} %param.39) | copy-start | bytes 1572868
  88.3 87.5 %reduce-scatter.19.cloned.1.call-start = ((), (), s32[]{:S(2)}) async-start(), calls=%async_computation.16 | async-start | bytes 147456 | tf_op jit(solution)/shard_map/reduce_scatter | solution.py:17
  143.5 87.5 %reduce-scatter.21.cloned.1.call-start = ((), (), s32[]{:S(2)}) async-start(), calls=%async_computation.17 | async-start | bytes 147456 | tf_op jit(solution)/shard_map/reduce_scatter | solution.py:17
  198.6 87.4 %reduce-scatter.23.cloned.1.call-start = ((), (), s32[]{:S(2)}) async-start(), calls=%async_computation.18 | async-start | bytes 147456 | tf_op jit(solution)/shard_map/reduce_scatter | solution.py:17
  253.7 87.5 %reduce-scatter.25.cloned.1.call-start = ((), (), s32[]{:S(2)}) async-start(), calls=%async_computation.19 | async-start | bytes 147456 | tf_op jit(solution)/shard_map/reduce_scatter | solution.py:17
  308.8 87.4 %reduce-scatter.27.cloned.1.call-start = ((), (), s32[]{:S(2)}) async-start(), calls=%async_computation.20 | async-start | bytes 147456 | tf_op jit(solution)/shard_map/reduce_scatter | solution.py:17
  363.8 87.8 %reduce-scatter.29.cloned.1.call-start = ((), (), s32[]{:S(2)}) async-start(), calls=%async_computation.21 | async-start | bytes 147456 | tf_op jit(solution)/shard_map/reduce_scatter | solution.py:17
  397.0 294.5 %copy-start.3 = (f32[8,32,128]{2,1,0:T(8,128)}, f32[8,32,128]{2,1,0:T(8,128)S(1)}, u32[]{:S(2)}) copy-start(f32[8,32,128]{2,1,0:T(8,128)S(1)} %get-tuple-element.202) | copy-start | bytes 393220
  419.2 87.5 %reduce-scatter.31.cloned.1.call-start = ((), (), s32[]{:S(2)}) async-start(), calls=%async_computation.22 | async-start | bytes 147456 | tf_op jit(solution)/shard_map/reduce_scatter | solution.py:17
  474.3 87.4 %reduce-scatter.33.cloned.1.call-start = ((), (), s32[]{:S(2)}) async-start(), calls=%async_computation.23 | async-start | bytes 147456 | tf_op jit(solution)/shard_map/reduce_scatter | solution.py:17
  529.4 87.3 %reduce-scatter.35.cloned.1.call-start = ((), (), s32[]{:S(2)}) async-start(), calls=%async_computation.24 | async-start | bytes 147456 | tf_op jit(solution)/shard_map/reduce_scatter | solution.py:17
  584.4 87.4 %reduce-scatter.37.cloned.1.call-start = ((), (), s32[]{:S(2)}) async-start(), calls=%async_computation.25 | async-start | bytes 147456 | tf_op jit(solution)/shard_map/reduce_scatter | solution.py:17
  639.5 87.5 %reduce-scatter.39.cloned.1.call-start = ((), (), s32[]{:S(2)}) async-start(), calls=%async_computation.26 | async-start | bytes 147456 | tf_op jit(solution)/shard_map/reduce_scatter | solution.py:17
  694.5 87.4 %reduce-scatter.41.cloned.1.call-start = ((), (), s32[]{:S(2)}) async-start(), calls=%async_computation.27 | async-start | bytes 147456 | tf_op jit(solution)/shard_map/reduce_scatter | solution.py:17
  783.0 0.7 copy-start.4
Sparse Core Ops, SparseCore 0:
  32.1 33.1 reduce-scatter.14
  88.4 32.1 reduce-scatter.16
  143.7 32.1 reduce-scatter.18
  198.7 32.2 reduce-scatter.20
  253.8 32.1 reduce-scatter.22
  308.9 32.2 reduce-scatter.24
  363.9 32.1 reduce-scatter.26
  419.3 32.2 reduce-scatter.28
  474.4 32.1 reduce-scatter.30
  529.5 32.2 reduce-scatter.32
  584.5 32.1 reduce-scatter.34
  639.6 32.1 reduce-scatter.36
  694.7 32.2 reduce-scatter.38
  749.7 32.2 reduce-scatter.40
where the time goes:
time: 794 us; the launch traced here: 790 us
  waiting for transfers between devices  451 us (57%)
  blocking collectives  264 us (33%)
  matrix products  47.1 us (6%)
  between operations  14.5 us (2%)
  local copies, waits for them, and re-layouts  11.9 us (1%)
    reduce_scatter x14, waiting for transfers between devices, reduce_rows(): lax.psum_scatter(partial_value, 'row', scatter_dimension=0, tiled=True)[0]  451 us
    all_gather x14, blocking collectives, share_solved(): lax.all_gather(solved.astype(jnp.bfloat16)[None], 'col', axis=0, tiled=True)  264 us
    dot_general x14, matrix products, level_terms(): jnp.einsum('msxj,msoj->mxo', picked, blocks, preferred_element_type=jnp.f...  32.8 us
  transfers between devices with their start and end apart: 14, of which 14 were waited for; matrix products, arithmetic and copies ran while one was open for 0% of the time, Pallas kernels for 0%

commit v1 on v0

--- a/solution.py
+++ b/solution.py
@@ -14,11 +14,12 @@
 
 
 def reduce_rows(partial_value):
-    return lax.psum_scatter(partial_value, "row", scatter_dimension=0, tiled=True)[0]
+    return lax.all_to_all(partial_value, "row", 0, 0, tiled=True).sum(axis=0)
 
 
 def share_solved(solved):
-    return lax.all_gather(solved.astype(jnp.bfloat16)[None], "col", axis=0, tiled=True)
+    copies = jnp.broadcast_to(solved.astype(jnp.bfloat16), (lax.axis_size("col"),) + solved.shape)
+    return lax.all_to_all(copies, "col", 0, 0, tiled=True)
 
 
 def per_device(

time: 794 us -> 338 us (0.43)
  waiting for transfers between devices: 451 us -> 91.3 us
  blocking collectives: 264 us -> 139 us
  starting transfers between devices: 0.58 us -> 53.2 us
  matrix products: 47.1 us -> 28.1 us
  between operations: 14.5 us -> 1.25 us
  local copies, waits for them, and re-layouts: 11.9 us -> 21.6 us
    reduce_scatter x14 -> x0, waiting for transfers between devices: 451 us -> none  [reduce_rows(): lax.psum_scatter(partial_value, 'row', scatter_dimension=0, tiled=True)[0]]
    all_gather x14 -> x0, blocking collectives: 264 us -> none  [share_solved(): lax.all_gather(solved.astype(jnp.bfloat16)[None], 'col', axis=0, tiled=True)]
    all_to_all x0 -> x14, blocking collectives: none -> 139 us  [reduce_rows(): return lax.all_to_all(partial_value, 'row', 0, 0, tiled=True).sum(axis=0)]
    all_to_all x0 -> x14, waiting for transfers between devices: none -> 91.3 us  [share_solved(): return lax.all_to_all(copies, 'col', 0, 0, tiled=True)]
    all_to_all x0 -> x14, starting transfers between devices: none -> 53.2 us  [share_solved(): return lax.all_to_all(copies, 'col', 0, 0, tiled=True)]
    broadcast_in_dim x0 -> x14, local copies, waits for them, and re-layouts: none -> 9.65 us  [share_solved(): jnp.broadcast_to(solved.astype(jnp.bfloat16), (lax.axis_size('col'),) + s...]
    dot_general x14, matrix products: 32.8 us -> 23.3 us  [level_terms(): jnp.einsum('msxj,msoj->mxo', picked, blocks, preferred_element_type=jnp.f...]
    dot_general x16, matrix products: 14.3 us -> 4.82 us  [apply_inverse(): jnp.einsum('xi,oi->xo', vectors, inverse, precision=lax.Precision.HIGHEST)]
  transfers between devices with their start and end apart: 14 -> 14, of which waited for: 14 -> 14; matrix products, arithmetic and copies ran while one was open for 0% -> 1% of each run, Pallas kernels for 0% -> 0%
where the time goes in v1:
time: 338 us; the launch traced here: 335 us
  blocking collectives  139 us (41%)
  waiting for transfers between devices  91.3 us (27%)
  starting transfers between devices  53.2 us (16%)
  matrix products  28.1 us (8%)
  local copies, waits for them, and re-layouts  21.6 us (6%)
    all_to_all x14, blocking collectives, reduce_rows(): return lax.all_to_all(partial_value, 'row', 0, 0, tiled=True).sum(axis=0)  139 us
    all_to_all x14, waiting for transfers between devices, share_solved(): return lax.all_to_all(copies, 'col', 0, 0, tiled=True)  91.3 us
    all_to_all x14, starting transfers between devices, share_solved(): return lax.all_to_all(copies, 'col', 0, 0, tiled=True)  53.2 us
    dot_general x14, matrix products, level_terms(): jnp.einsum('msxj,msoj->mxo', picked, blocks, preferred_element_type=jnp.f...  23.3 us
    broadcast_in_dim x14, local copies, waits for them, and re-layouts, share_solved(): jnp.broadcast_to(solved.astype(jnp.bfloat16), (lax.axis_size('col'),) + s...  9.65 us
    gather x14, local copies, waits for them, and re-layouts, level_terms(): picked = history[pattern]  8.43 us
  transfers between devices with their start and end apart: 14, of which 14 were waited for; matrix products, arithmetic and copies ran while one was open for 1% of the time, Pallas kernels for 0%

profile of v1, /device:TPU:1, one launch (start us, length us, event | category | flops | bytes accessed | tf_op | source)
XLA Modules:
  0.0 335.3 jit_solution(14751060077539371523)
XLA Ops:
  2.5 7.6 %all-to-all-start = ((bf16[16,32,128]{2,1,0:T(8,128)(2,1)}), bf16[16,32,128]{2,1,0:T(8,128)(2,1)S(1)}, u32[]{:S(2)}, u32[]{:S(2)}) async-start(bf16[16,32,128]{2,1,0:T(8,128)(2,1)} %broadcast_in_dim.62), calls=%async_computation | async-start | bytes 262144 | tf_op jit(solution)/shard_map/all_to_all | solution.py:22
  19.3 12.3 %all_to_all.140 = f32[8,32,128]{2,1,0:T(8,128)S(1)} all-to-all(f32[8,32,128]{2,1,0:T(8,128)S(1)} %convolution_bitcast_fusion.13), channel_id=1, replica_groups=mesh['col'=16,'row'=8] {'row'}, dimensions={0} | all-to-all | bytes 262144 | tf_op jit(solution)/shard_map/all_to_all | solution.py:17
  37.1 6.6 %all-to-all-done.2 = bf16[16,32,128]{2,1,0:T(8,128)(2,1)S(1)} async-done(((bf16[16,32,128]{2,1,0:T(8,128)(2,1)}), bf16[16,32,128]{2,1,0:T(8,128)(2,1)S(1)}, u32[]{:S(2)}, u32[]{:S(2)}) %all-to-all-start.2) | async-done | bytes 131104 | tf_op jit(solution)/shard_map/all_to_all | solution.py:22
  46.0 9.7 %all_to_all.141 = f32[8,32,128]{2,1,0:T(8,128)S(1)} all-to-all(f32[8,32,128]{2,1,0:T(8,128)S(1)} %convolution_bitcast_fusion.12), channel_id=1, replica_groups=mesh['col'=16,'row'=8] {'row'}, dimensions={0} | all-to-all | bytes 262144 | tf_op jit(solution)/shard_map/all_to_all | solution.py:17
  60.3 6.6 %all-to-all-done.4 = bf16[16,32,128]{2,1,0:T(8,128)(2,1)S(1)} async-done(((bf16[16,32,128]{2,1,0:T(8,128)(2,1)}), bf16[16,32,128]{2,1,0:T(8,128)(2,1)S(1)}, u32[]{:S(2)}, u32[]{:S(2)}) %all-to-all-start.4) | async-done | bytes 131104 | tf_op jit(solution)/shard_map/all_to_all | solution.py:22
  69.3 9.7 %all_to_all.142 = f32[8,32,128]{2,1,0:T(8,128)S(1)} all-to-all(f32[8,32,128]{2,1,0:T(8,128)S(1)} %convolution_bitcast_fusion.11), channel_id=1, replica_groups=mesh['col'=16,'row'=8] {'row'}, dimensions={0} | all-to-all | bytes 262144 | tf_op jit(solution)/shard_map/all_to_all | solution.py:17
  83.6 6.6 %all-to-all-done.6 = bf16[16,32,128]{2,1,0:T(8,128)(2,1)S(1)} async-done(((bf16[16,32,128]{2,1,0:T(8,128)(2,1)}), bf16[16,32,128]{2,1,0:T(8,128)(2,1)S(1)}, u32[]{:S(2)}, u32[]{:S(2)}) %all-to-all-start.6) | async-done | bytes 131104 | tf_op jit(solution)/shard_map/all_to_all | solution.py:22
  92.5 9.7 %all_to_all.143 = f32[8,32,128]{2,1,0:T(8,128)S(1)} all-to-all(f32[8,32,128]{2,1,0:T(8,128)S(1)} %convolution_bitcast_fusion.10), channel_id=1, replica_groups=mesh['col'=16,'row'=8] {'row'}, dimensions={0} | all-to-all | bytes 262144 | tf_op jit(solution)/shard_map/all_to_all | solution.py:17
  106.8 6.6 %all-to-all-done.8 = bf16[16,32,128]{2,1,0:T(8,128)(2,1)S(1)} async-done(((bf16[16,32,128]{2,1,0:T(8,128)(2,1)}), bf16[16,32,128]{2,1,0:T(8,128)(2,1)S(1)}, u32[]{:S(2)}, u32[]{:S(2)}) %all-to-all-start.8) | async-done | bytes 131104 | tf_op jit(solution)/shard_map/all_to_all | solution.py:22
  115.6 9.7 %all_to_all.144 = f32[8,32,128]{2,1,0:T(8,128)S(1)} all-to-all(f32[8,32,128]{2,1,0:T(8,128)S(1)} %convolution_bitcast_fusion.9), channel_id=1, replica_groups=mesh['col'=16,'row'=8] {'row'}, dimensions={0} | all-to-all | bytes 262144 | tf_op jit(solution)/shard_map/all_to_all | solution.py:17
  130.0 6.6 %all-to-all-done.10 = bf16[16,32,128]{2,1,0:T(8,128)(2,1)S(1)} async-done(((bf16[16,32,128]{2,1,0:T(8,128)(2,1)}), bf16[16,32,128]{2,1,0:T(8,128)(2,1)S(1)}, u32[]{:S(2)}, u32[]{:S(2)}) %all-to-all-start.10) | async-done | bytes 131104 | tf_op jit(solution)/shard_map/all_to_all | solution.py:22
  138.8 9.7 %all_to_all.145 = f32[8,32,128]{2,1,0:T(8,128)S(1)} all-to-all(f32[8,32,128]{2,1,0:T(8,128)S(1)} %convolution_bitcast_fusion.8), channel_id=1, replica_groups=mesh['col'=16,'row'=8] {'row'}, dimensions={0} | all-to-all | bytes 262144 | tf_op jit(solution)/shard_map/all_to_all | solution.py:17
  153.2 6.6 %all-to-all-done.12 = bf16[16,32,128]{2,1,0:T(8,128)(2,1)S(1)} async-done(((bf16[16,32,128]{2,1,0:T(8,128)(2,1)}), bf16[16,32,128]{2,1,0:T(8,128)(2,1)S(1)}, u32[]{:S(2)}, u32[]{:S(2)}) %all-to-all-start.12) | async-done | bytes 131104 | tf_op jit(solution)/shard_map/all_to_all | solution.py:22
  162.0 9.7 %all_to_all.146 = f32[8,32,128]{2,1,0:T(8,128)S(1)} all-to-all(f32[8,32,128]{2,1,0:T(8,128)S(1)} %convolution_bitcast_fusion.7), channel_id=1, replica_groups=mesh['col'=16,'row'=8] {'row'}, dimensions={0} | all-to-all | bytes 262144 | tf_op jit(solution)/shard_map/all_to_all | solution.py:17
  176.6 6.6 %all-to-all-done.14 = bf16[16,32,128]{2,1,0:T(8,128)(2,1)S(1)} async-done(((bf16[16,32,128]{2,1,0:T(8,128)(2,1)}), bf16[16,32,128]{2,1,0:T(8,128)(2,1)S(1)}, u32[]{:S(2)}, u32[]{:S(2)}) %all-to-all-start.14) | async-done | bytes 131104 | tf_op jit(solution)/shard_map/all_to_all | solution.py:22
  185.6 9.7 %all_to_all.147 = f32[8,32,128]{2,1,0:T(8,128)S(1)} all-to-all(f32[8,32,128]{2,1,0:T(8,128)S(1)} %convolution_bitcast_fusion.6), channel_id=1, replica_groups=mesh['col'=16,'row'=8] {'row'}, dimensions={0} | all-to-all | bytes 262144 | tf_op jit(solution)/shard_map/all_to_all | solution.py:17
  199.9 6.6 %all-to-all-done.16 = bf16[16,32,128]{2,1,0:T(8,128)(2,1)S(1)} async-done(((bf16[16,32,128]{2,1,0:T(8,128)(2,1)}), bf16[16,32,128]{2,1,0:T(8,128)(2,1)S(1)}, u32[]{:S(2)}, u32[]{:S(2)}) %all-to-all-start.16) | async-done | bytes 131104 | tf_op jit(solution)/shard_map/all_to_all | solution.py:22
  208.7 9.7 %all_to_all.148 = f32[8,32,128]{2,1,0:T(8,128)S(1)} all-to-all(f32[8,32,128]{2,1,0:T(8,128)S(1)} %convolution_bitcast_fusion.5), channel_id=1, replica_groups=mesh['col'=16,'row'=8] {'row'}, dimensions={0} | all-to-all | bytes 262144 | tf_op jit(solution)/shard_map/all_to_all | solution.py:17
  223.1 6.6 %all-to-all-done.18 = bf16[16,32,128]{2,1,0:T(8,128)(2,1)S(1)} async-done(((bf16[16,32,128]{2,1,0:T(8,128)(2,1)}), bf16[16,32,128]{2,1,0:T(8,128)(2,1)S(1)}, u32[]{:S(2)}, u32[]{:S(2)}) %all-to-all-start.18) | async-done | bytes 131104 | tf_op jit(solution)/shard_map/all_to_all | solution.py:22
  231.9 9.7 %all_to_all.149 = f32[8,32,128]{2,1,0:T(8,128)S(1)} all-to-all(f32[8,32,128]{2,1,0:T(8,128)S(1)} %convolution_bitcast_fusion.4), channel_id=1, replica_groups=mesh['col'=16,'row'=8] {'row'}, dimensions={0} | all-to-all | bytes 262144 | tf_op jit(solution)/shard_map/all_to_all | solution.py:17
  255.1 9.7 %all_to_all.150 = f32[8,32,128]{2,1,0:T(8,128)S(1)} all-to-all(f32[8,32,128]{2,1,0:T(8,128)S(1)} %convolution_bitcast_fusion.3), channel_id=1, replica_groups=mesh['col'=16,'row'=8] {'row'}, dimensions={0} | all-to-all | bytes 262144 | tf_op jit(solution)/shard_map/all_to_all | solution.py:17
  278.3 9.7 %all_to_all.151 = f32[8,32,128]{2,1,0:T(8,128)S(1)} all-to-all(f32[8,32,128]{2,1,0:T(8,128)S(1)} %convolution_bitcast_fusion.2), channel_id=1, replica_groups=mesh['col'=16,'row'=8] {'row'}, dimensions={0} | all-to-all | bytes 262144 | tf_op jit(solution)/shard_map/all_to_all | solution.py:17
  301.5 9.7 %all_to_all.152 = f32[8,32,128]{2,1,0:T(8,128)S(1)} all-to-all(f32[8,32,128]{2,1,0:T(8,128)S(1)} %convolution_bitcast_fusion.1), channel_id=1, replica_groups=mesh['col'=16,'row'=8] {'row'}, dimensions={0} | all-to-all | bytes 262144 | tf_op jit(solution)/shard_map/all_to_all | solution.py:17
  324.7 9.7 %all_to_all.153 = f32[8,32,128]{2,1,0:T(8,128)S(1)} all-to-all(f32[8,32,128]{2,1,0:T(8,128)S(1)} %convolution_bitcast_fusion), channel_id=1, replica_groups=mesh['col'=16,'row'=8] {'row'}, dimensions={0} | all-to-all | bytes 262144 | tf_op jit(solution)/shard_map/all_to_all | solution.py:17
  (171 shorter events, 128.9 us)
Async XLA Ops:
  0.6 55.1 %copy-start = (f32[8,1,128,128]{3,2,1,0:T(8,128)S(1)}, f32[8,1,128,128]{3,2,1,0:T(8,128)}, u32[]{:S(2)}) copy-start(f32[8,1,128,128]{3,2,1,0:T(8,128)} %param.36) | copy-start | bytes 1572868
  0.6 55.1 %copy-start.2 = (f32[8,1,32,128]{3,2,1,0:T(8,128)S(1)}, f32[8,1,32,128]{3,2,1,0:T(8,128)}, u32[]{:S(2)}) copy-start(f32[8,1,32,128]{3,2,1,0:T(8,128)} %param.35) | copy-start | bytes 393220
  2.5 14.5 %all-to-all-start = ((bf16[16,32,128]{2,1,0:T(8,128)(2,1)}), bf16[16,32,128]{2,1,0:T(8,128)(2,1)S(1)}, u32[]{:S(2)}, u32[]{:S(2)}) async-start(bf16[16,32,128]{2,1,0:T(8,128)(2,1)} %broadcast_in_dim.62), calls=%async_computation | async-start | bytes 262144 | tf_op jit(solution)/shard_map/all_to_all | solution.py:22
  33.4 10.3 %all-to-all-start.2 = ((bf16[16,32,128]{2,1,0:T(8,128)(2,1)}), bf16[16,32,128]{2,1,0:T(8,128)(2,1)S(1)}, u32[]{:S(2)}, u32[]{:S(2)}) async-start(bf16[16,32,128]{2,1,0:T(8,128)(2,1)} %broadcast_in_dim.63), calls=%async_computation.2 | async-start | bytes 262144 | tf_op jit(solution)/shard_map/all_to_all | solution.py:22
  56.6 10.3 %all-to-all-start.4 = ((bf16[16,32,128]{2,1,0:T(8,128)(2,1)}), bf16[16,32,128]{2,1,0:T(8,128)(2,1)S(1)}, u32[]{:S(2)}, u32[]{:S(2)}) async-start(bf16[16,32,128]{2,1,0:T(8,128)(2,1)} %broadcast_in_dim.64), calls=%async_computation.4 | async-start | bytes 262144 | tf_op jit(solution)/shard_map/all_to_all | solution.py:22
  67.5 104.4 %copy-start.1 = (f32[8,1,128,128]{3,2,1,0:T(8,128)S(1)}, f32[8,1,128,128]{3,2,1,0:T(8,128)}, u32[]{:S(2)}) copy-start(f32[8,1,128,128]{3,2,1,0:T(8,128)} %param.39) | copy-start | bytes 1572868
  79.9 10.3 %all-to-all-start.6 = ((bf16[16,32,128]{2,1,0:T(8,128)(2,1)}), bf16[16,32,128]{2,1,0:T(8,128)(2,1)S(1)}, u32[]{:S(2)}, u32[]{:S(2)}) async-start(bf16[16,32,128]{2,1,0:T(8,128)(2,1)} %broadcast_in_dim.65), calls=%async_computation.6 | async-start | bytes 262144 | tf_op jit(solution)/shard_map/all_to_all | solution.py:22
  103.1 10.3 %all-to-all-start.8 = ((bf16[16,32,128]{2,1,0:T(8,128)(2,1)}), bf16[16,32,128]{2,1,0:T(8,128)(2,1)S(1)}, u32[]{:S(2)}, u32[]{:S(2)}) async-start(bf16[16,32,128]{2,1,0:T(8,128)(2,1)} %broadcast_in_dim.66), calls=%async_computation.8 | async-start | bytes 262144 | tf_op jit(solution)/shard_map/all_to_all | solution.py:22
  126.3 10.3 %all-to-all-start.10 = ((bf16[16,32,128]{2,1,0:T(8,128)(2,1)}), bf16[16,32,128]{2,1,0:T(8,128)(2,1)S(1)}, u32[]{:S(2)}, u32[]{:S(2)}) async-start(bf16[16,32,128]{2,1,0:T(8,128)(2,1)} %broadcast_in_dim.67), calls=%async_computation.10 | async-start | bytes 262144 | tf_op jit(solution)/shard_map/all_to_all | solution.py:22
  149.5 10.3 %all-to-all-start.12 = ((bf16[16,32,128]{2,1,0:T(8,128)(2,1)}), bf16[16,32,128]{2,1,0:T(8,128)(2,1)S(1)}, u32[]{:S(2)}, u32[]{:S(2)}) async-start(bf16[16,32,128]{2,1,0:T(8,128)(2,1)} %broadcast_in_dim.68), calls=%async_computation.12 | async-start | bytes 262144 | tf_op jit(solution)/shard_map/all_to_all | solution.py:22
  171.9 104.7 %copy-start.3 = (f32[8,32,128]{2,1,0:T(8,128)}, f32[8,32,128]{2,1,0:T(8,128)S(1)}, u32[]{:S(2)}) copy-start(f32[8,32,128]{2,1,0:T(8,128)S(1)} %get-tuple-element.204) | copy-start | bytes 393220
  172.9 10.3 %all-to-all-start.14 = ((bf16[16,32,128]{2,1,0:T(8,128)(2,1)}), bf16[16,32,128]{2,1,0:T(8,128)(2,1)S(1)}, u32[]{:S(2)}, u32[]{:S(2)}) async-start(bf16[16,32,128]{2,1,0:T(8,128)(2,1)} %broadcast_in_dim.70), calls=%async_computation.14 | async-start | bytes 262144 | tf_op jit(solution)/shard_map/all_to_all | solution.py:22
  196.2 10.3 %all-to-all-start.16 = ((bf16[16,32,128]{2,1,0:T(8,128)(2,1)}), bf16[16,32,128]{2,1,0:T(8,128)(2,1)S(1)}, u32[]{:S(2)}, u32[]{:S(2)}) async-start(bf16[16,32,128]{2,1,0:T(8,128)(2,1)} %broadcast_in_dim.71), calls=%async_computation.16 | async-start | bytes 262144 | tf_op jit(solution)/shard_map/all_to_all | solution.py:22
  219.4 10.3 %all-to-all-start.18 = ((bf16[16,32,128]{2,1,0:T(8,128)(2,1)}), bf16[16,32,128]{2,1,0:T(8,128)(2,1)S(1)}, u32[]{:S(2)}, u32[]{:S(2)}) async-start(bf16[16,32,128]{2,1,0:T(8,128)(2,1)} %broadcast_in_dim.72), calls=%async_computation.18 | async-start | bytes 262144 | tf_op jit(solution)/shard_map/all_to_all | solution.py:22
  242.5 10.3 %all-to-all-start.20 = ((bf16[16,32,128]{2,1,0:T(8,128)(2,1)}), bf16[16,32,128]{2,1,0:T(8,128)(2,1)S(1)}, u32[]{:S(2)}, u32[]{:S(2)}) async-start(bf16[16,32,128]{2,1,0:T(8,128)(2,1)} %broadcast_in_dim.73), calls=%async_computation.20 | async-start | bytes 262144 | tf_op jit(solution)/shard_map/all_to_all | solution.py:22
  265.7 10.3 %all-to-all-start.22 = ((bf16[16,32,128]{2,1,0:T(8,128)(2,1)}), bf16[16,32,128]{2,1,0:T(8,128)(2,1)S(1)}, u32[]{:S(2)}, u32[]{:S(2)}) async-start(bf16[16,32,128]{2,1,0:T(8,128)(2,1)} %broadcast_in_dim.74), calls=%async_computation.22 | async-start | bytes 262144 | tf_op jit(solution)/shard_map/all_to_all | solution.py:22
  288.9 10.3 %all-to-all-start.24 = ((bf16[16,32,128]{2,1,0:T(8,128)(2,1)}), bf16[16,32,128]{2,1,0:T(8,128)(2,1)S(1)}, u32[]{:S(2)}, u32[]{:S(2)}) async-start(bf16[16,32,128]{2,1,0:T(8,128)(2,1)} %broadcast_in_dim.75), calls=%async_computation.24 | async-start | bytes 262144 | tf_op jit(solution)/shard_map/all_to_all | solution.py:22
  312.1 10.3 %all-to-all-start.26 = ((bf16[16,32,128]{2,1,0:T(8,128)(2,1)}), bf16[16,32,128]{2,1,0:T(8,128)(2,1)S(1)}, u32[]{:S(2)}, u32[]{:S(2)}) async-start(bf16[16,32,128]{2,1,0:T(8,128)(2,1)} %broadcast_in_dim.76), calls=%async_computation.26 | async-start | bytes 262144 | tf_op jit(solution)/shard_map/all_to_all | solution.py:22
  334.7 0.7 copy-start.4

commit v2 on v1

--- a/solution.py
+++ b/solution.py
@@ -1,20 +1,52 @@
+import functools
+
 import jax
 import jax.numpy as jnp
 from jax import lax
+from jax.experimental import pallas as pl
+from jax.experimental.pallas import tpu as pltpu
 from jax.sharding import PartitionSpec as P
+
+BLOCKS_LAST = (((1,), (1,)), ((), ()))
 
 
 def apply_inverse(inverse, vectors):
     return jnp.einsum("xi,oi->xo", vectors, inverse, precision=lax.Precision.HIGHEST)
 
 
-def level_terms(history, blocks, pattern):
-    picked = history[pattern]
-    return jnp.einsum("msxj,msoj->mxo", picked, blocks, preferred_element_type=jnp.float32)
+def product_kernel(level, pattern_ref, history_ref, blocks_ref, sums_ref):
+    rows, slots = blocks_ref.shape[1:3]
+    for m in range(rows):
+        total = None
+        for s in range(slots):
+            picked = history_ref[pattern_ref[(level * rows + m) * slots + s]]
+            term = lax.dot_general(
+                picked, blocks_ref[level, m, s], BLOCKS_LAST, preferred_element_type=jnp.float32
+            )
+            total = term if total is None else total + term
+        sums_ref[m] = total.astype(sums_ref.dtype)
+
+
+def level_terms(history, blocks, pattern, level):
+    rows, slots, block = blocks.shape[1:4]
+    vmem = pl.BlockSpec(memory_space=pltpu.VMEM)
+    return pl.pallas_call(
+        functools.partial(product_kernel, level),
+        out_shape=jax.ShapeDtypeStruct((rows,) + history.shape[1:], jnp.bfloat16),
+        in_specs=[pl.BlockSpec(memory_space=pltpu.SMEM), vmem, vmem],
+        out_specs=vmem,
+        compiler_params=pltpu.CompilerParams(vmem_limit_bytes=24 * 2**20),
+        cost_estimate=pl.CostEstimate(
+            flops=2 * rows * slots * history.shape[1] * block * block,
+            bytes_accessed=2 * rows * slots * block * block + 2 * history.size,
+            transcendentals=0,
+        ),
+    )(pattern.reshape(-1), history, blocks)
 
 
 def reduce_rows(partial_value):
-    return lax.all_to_all(partial_value, "row", 0, 0, tiled=True).sum(axis=0)
+    parts = lax.all_to_all(partial_value, "row", 0, 0, tiled=True)
+    return parts.astype(jnp.float32).sum(axis=0)
 
 
 def share_solved(solved):
@@ -46,9 +78,7 @@
     for tier_index in range(tiers):
         residual_now = right_rows[tier_index]
         if tier_index > 0:
-            partial_value = level_terms(
-                history, low_blocks[tier_index - 1], low_pattern[tier_index - 1]
-            )
+            partial_value = level_terms(history, low_blocks, low_pattern, tier_index - 1)
             residual_now = residual_now - reduce_rows(partial_value)
         solved = apply_inverse(low_inv[tier_index], residual_now)
         forward_list.append(solved)
@@ -61,7 +91,7 @@
     for tier_index in range(tiers - 1, -1, -1):
         residual_now = forward_list[tier_index]
         if tier_index < tiers - 1:
-            partial_value = level_terms(history, high_blocks[tier_index], high_pattern[tier_index])
+            partial_value = level_terms(history, high_blocks, high_pattern, tier_index)
             residual_now = residual_now - reduce_rows(partial_value)
         solved = apply_inverse(high_inv[tier_index], residual_now)
         backward_list[tier_index] = solved

time: 338 us -> 309 us (0.914)
  blocking collectives: 139 us -> 252 us
  waiting for transfers between devices: 91.3 us -> 12.5 us
  starting transfers between devices: 53.2 us -> 11.1 us
  matrix products: 28.1 us -> 3.96 us
  Pallas kernels: 0 us -> 16.7 us
  local copies, waits for them, and re-layouts: 21.6 us -> 10.3 us
    all_to_all x14 -> x26, blocking collectives: 139 us -> 252 us  [the longest x14 134 us: reduce_rows(): parts = lax.all_to_all(partial_value, 'row', 0, 0, tiled=True)]
    all_to_all x14 -> x2, waiting for transfers between devices: 91.3 us -> 12.5 us  [share_solved(): return lax.all_to_all(copies, 'col', 0, 0, tiled=True)]
    all_to_all x14 -> x2, starting transfers between devices: 53.2 us -> 11.1 us  [share_solved(): return lax.all_to_all(copies, 'col', 0, 0, tiled=True)]
    dot_general x14 -> x0, matrix products: 23.3 us -> none  [level_terms(): jnp.einsum('msxj,msoj->mxo', picked, blocks, preferred_element_type=jnp.f...]
    pallas_call x0 -> x14, Pallas kernels: none -> 16.7 us  [level_terms(): pl.pallas_call(functools.partial(product_kernel, level), out_shape=jax.Sh...]
    gather x14 -> x0, local copies, waits for them, and re-layouts: 8.43 us -> none  [level_terms(): picked = history[pattern]]
    broadcast_in_dim x14, local copies, waits for them, and re-layouts: 9.65 us -> 1.76 us  [share_solved(): jnp.broadcast_to(solved.astype(jnp.bfloat16), (lax.axis_size('col'),) + s...]
    unnamed x16 -> x24, local copies, waits for them, and re-layouts: 0.74 us -> 7.86 us
  transfers between devices with their start and end apart: 14 -> 2, of which waited for: 14 -> 2; matrix products, arithmetic and copies ran while one was open for 1% -> 0% of each run, Pallas kernels for 0% -> 0%
where the time goes in v2:
time: 309 us; the launch traced here: 308 us
  blocking collectives  252 us (82%)
  Pallas kernels  16.7 us (5%)
  waiting for transfers between devices  12.5 us (4%)
  starting transfers between devices  11.1 us (4%)
  local copies, waits for them, and re-layouts  10.3 us (3%)
  matrix products  3.96 us (1%)
    all_to_all x14, blocking collectives, reduce_rows(): parts = lax.all_to_all(partial_value, 'row', 0, 0, tiled=True)  134 us
    all_to_all x12, blocking collectives, share_solved(): return lax.all_to_all(copies, 'col', 0, 0, tiled=True)  118 us
    pallas_call x14, Pallas kernels, level_terms(): pl.pallas_call(functools.partial(product_kernel, level), out_shape=jax.Sh...  16.7 us
    all_to_all x2, waiting for transfers between devices, share_solved(): return lax.all_to_all(copies, 'col', 0, 0, tiled=True)  12.5 us
    all_to_all x2, starting transfers between devices, share_solved(): return lax.all_to_all(copies, 'col', 0, 0, tiled=True)  11.1 us
    unnamed x24, local copies, waits for them, and re-layouts  7.86 us
  transfers between devices with their start and end apart: 2, of which 2 were waited for; matrix products, arithmetic and copies ran while one was open for 0% of the time, Pallas kernels for 0%

profile of v2, /device:TPU:1, one launch (start us, length us, event | category | flops | bytes accessed | tf_op | source)
XLA Modules:
  0.0 308.1 jit_solution(5267735317542082540)
XLA Ops:
  21.4 11.9 %all_to_all.140 = bf16[8,32,128]{2,1,0:T(8,128)(2,1)S(1)} all-to-all(bf16[8,32,128]{2,1,0:T(8,128)(2,1)S(1)} %shard_map.86), channel_id=1, replica_groups=mesh['col'=16,'row'=8] {'row'}, dimensions={0} | all-to-all | bytes 131072 | tf_op jit(solution)/shard_map/all_to_all | solution.py:48
  33.6 9.9 %all_to_all.141 = bf16[16,32,128]{2,1,0:T(8,128)(2,1)S(1)} all-to-all(bf16[16,32,128]{2,1,0:T(8,128)(2,1)S(1)} %broadcast_in_dim.49), channel_id=1, replica_groups=mesh['col'=16,'row'=8] {'col'}, dimensions={0} | all-to-all | bytes 262144 | tf_op jit(solution)/shard_map/all_to_all | solution.py:54
  44.6 9.4 %all_to_all.142 = bf16[8,32,128]{2,1,0:T(8,128)(2,1)S(1)} all-to-all(bf16[8,32,128]{2,1,0:T(8,128)(2,1)S(1)} %shard_map.87), channel_id=1, replica_groups=mesh['col'=16,'row'=8] {'row'}, dimensions={0} | all-to-all | bytes 131072 | tf_op jit(solution)/shard_map/all_to_all | solution.py:48
  54.3 9.9 %all_to_all.143 = bf16[16,32,128]{2,1,0:T(8,128)(2,1)S(1)} all-to-all(bf16[16,32,128]{2,1,0:T(8,128)(2,1)S(1)} %broadcast_in_dim.50), channel_id=1, replica_groups=mesh['col'=16,'row'=8] {'col'}, dimensions={0} | all-to-all | bytes 262144 | tf_op jit(solution)/shard_map/all_to_all | solution.py:54
  65.4 9.4 %all_to_all.144 = bf16[8,32,128]{2,1,0:T(8,128)(2,1)S(1)} all-to-all(bf16[8,32,128]{2,1,0:T(8,128)(2,1)S(1)} %shard_map.88), channel_id=1, replica_groups=mesh['col'=16,'row'=8] {'row'}, dimensions={0} | all-to-all | bytes 131072 | tf_op jit(solution)/shard_map/all_to_all | solution.py:48
  75.0 9.9 %all_to_all.145 = bf16[16,32,128]{2,1,0:T(8,128)(2,1)S(1)} all-to-all(bf16[16,32,128]{2,1,0:T(8,128)(2,1)S(1)} %broadcast_in_dim.51), channel_id=1, replica_groups=mesh['col'=16,'row'=8] {'col'}, dimensions={0} | all-to-all | bytes 262144 | tf_op jit(solution)/shard_map/all_to_all | solution.py:54
  86.1 9.4 %all_to_all.146 = bf16[8,32,128]{2,1,0:T(8,128)(2,1)S(1)} all-to-all(bf16[8,32,128]{2,1,0:T(8,128)(2,1)S(1)} %shard_map.89), channel_id=1, replica_groups=mesh['col'=16,'row'=8] {'row'}, dimensions={0} | all-to-all | bytes 131072 | tf_op jit(solution)/shard_map/all_to_all | solution.py:48
  95.8 9.9 %all_to_all.147 = bf16[16,32,128]{2,1,0:T(8,128)(2,1)S(1)} all-to-all(bf16[16,32,128]{2,1,0:T(8,128)(2,1)S(1)} %broadcast_in_dim.52), channel_id=1, replica_groups=mesh['col'=16,'row'=8] {'col'}, dimensions={0} | all-to-all | bytes 262144 | tf_op jit(solution)/shard_map/all_to_all | solution.py:54
  106.8 9.4 %all_to_all.148 = bf16[8,32,128]{2,1,0:T(8,128)(2,1)S(1)} all-to-all(bf16[8,32,128]{2,1,0:T(8,128)(2,1)S(1)} %shard_map.90), channel_id=1, replica_groups=mesh['col'=16,'row'=8] {'row'}, dimensions={0} | all-to-all | bytes 131072 | tf_op jit(solution)/shard_map/all_to_all | solution.py:48
  116.5 9.9 %all_to_all.149 = bf16[16,32,128]{2,1,0:T(8,128)(2,1)S(1)} all-to-all(bf16[16,32,128]{2,1,0:T(8,128)(2,1)S(1)} %broadcast_in_dim.53), channel_id=1, replica_groups=mesh['col'=16,'row'=8] {'col'}, dimensions={0} | all-to-all | bytes 262144 | tf_op jit(solution)/shard_map/all_to_all | solution.py:54
  127.6 9.4 %all_to_all.150 = bf16[8,32,128]{2,1,0:T(8,128)(2,1)S(1)} all-to-all(bf16[8,32,128]{2,1,0:T(8,128)(2,1)S(1)} %shard_map.91), channel_id=1, replica_groups=mesh['col'=16,'row'=8] {'row'}, dimensions={0} | all-to-all | bytes 131072 | tf_op jit(solution)/shard_map/all_to_all | solution.py:48
  137.3 9.9 %all_to_all.151 = bf16[16,32,128]{2,1,0:T(8,128)(2,1)S(1)} all-to-all(bf16[16,32,128]{2,1,0:T(8,128)(2,1)S(1)} %broadcast_in_dim.54), channel_id=1, replica_groups=mesh['col'=16,'row'=8] {'col'}, dimensions={0} | all-to-all | bytes 262144 | tf_op jit(solution)/shard_map/all_to_all | solution.py:54
  148.3 9.4 %all_to_all.152 = bf16[8,32,128]{2,1,0:T(8,128)(2,1)S(1)} all-to-all(bf16[8,32,128]{2,1,0:T(8,128)(2,1)S(1)} %shard_map.92), channel_id=1, replica_groups=mesh['col'=16,'row'=8] {'row'}, dimensions={0} | all-to-all | bytes 131072 | tf_op jit(solution)/shard_map/all_to_all | solution.py:48
  183.0 9.9 %all_to_all.154 = bf16[16,32,128]{2,1,0:T(8,128)(2,1)S(1)} all-to-all(bf16[16,32,128]{2,1,0:T(8,128)(2,1)S(1)} %broadcast_in_dim.57), channel_id=1, replica_groups=mesh['col'=16,'row'=8] {'col'}, dimensions={0} | all-to-all | bytes 262144 | tf_op jit(solution)/shard_map/all_to_all | solution.py:54
  194.1 9.4 %all_to_all.155 = bf16[8,32,128]{2,1,0:T(8,128)(2,1)S(1)} all-to-all(bf16[8,32,128]{2,1,0:T(8,128)(2,1)S(1)} %shard_map.94), channel_id=1, replica_groups=mesh['col'=16,'row'=8] {'row'}, dimensions={0} | all-to-all | bytes 131072 | tf_op jit(solution)/shard_map/all_to_all | solution.py:48
  203.8 9.9 %all_to_all.156 = bf16[16,32,128]{2,1,0:T(8,128)(2,1)S(1)} all-to-all(bf16[16,32,128]{2,1,0:T(8,128)(2,1)S(1)} %broadcast_in_dim.58), channel_id=1, replica_groups=mesh['col'=16,'row'=8] {'col'}, dimensions={0} | all-to-all | bytes 262144 | tf_op jit(solution)/shard_map/all_to_all | solution.py:54
  214.8 9.4 %all_to_all.157 = bf16[8,32,128]{2,1,0:T(8,128)(2,1)S(1)} all-to-all(bf16[8,32,128]{2,1,0:T(8,128)(2,1)S(1)} %shard_map.95), channel_id=1, replica_groups=mesh['col'=16,'row'=8] {'row'}, dimensions={0} | all-to-all | bytes 131072 | tf_op jit(solution)/shard_map/all_to_all | solution.py:48
  224.5 9.9 %all_to_all.158 = bf16[16,32,128]{2,1,0:T(8,128)(2,1)S(1)} all-to-all(bf16[16,32,128]{2,1,0:T(8,128)(2,1)S(1)} %broadcast_in_dim.59), channel_id=1, replica_groups=mesh['col'=16,'row'=8] {'col'}, dimensions={0} | all-to-all | bytes 262144 | tf_op jit(solution)/shard_map/all_to_all | solution.py:54
  245.2 9.9 %all_to_all.160 = bf16[16,32,128]{2,1,0:T(8,128)(2,1)S(1)} all-to-all(bf16[16,32,128]{2,1,0:T(8,128)(2,1)S(1)} %broadcast_in_dim.60), channel_id=1, replica_groups=mesh['col'=16,'row'=8] {'col'}, dimensions={0} | all-to-all | bytes 262144 | tf_op jit(solution)/shard_map/all_to_all | solution.py:54
  256.3 9.4 %all_to_all.161 = bf16[8,32,128]{2,1,0:T(8,128)(2,1)S(1)} all-to-all(bf16[8,32,128]{2,1,0:T(8,128)(2,1)S(1)} %shard_map.97), channel_id=1, replica_groups=mesh['col'=16,'row'=8] {'row'}, dimensions={0} | all-to-all | bytes 131072 | tf_op jit(solution)/shard_map/all_to_all | solution.py:48
  265.9 9.9 %all_to_all.162 = bf16[16,32,128]{2,1,0:T(8,128)(2,1)S(1)} all-to-all(bf16[16,32,128]{2,1,0:T(8,128)(2,1)S(1)} %broadcast_in_dim.61), channel_id=1, replica_groups=mesh['col'=16,'row'=8] {'col'}, dimensions={0} | all-to-all | bytes 262144 | tf_op jit(solution)/shard_map/all_to_all | solution.py:54
  277.0 9.4 %all_to_all.163 = bf16[8,32,128]{2,1,0:T(8,128)(2,1)S(1)} all-to-all(bf16[8,32,128]{2,1,0:T(8,128)(2,1)S(1)} %shard_map.98), channel_id=1, replica_groups=mesh['col'=16,'row'=8] {'row'}, dimensions={0} | all-to-all | bytes 131072 | tf_op jit(solution)/shard_map/all_to_all | solution.py:48
  286.7 9.9 %all_to_all.164 = bf16[16,32,128]{2,1,0:T(8,128)(2,1)S(1)} all-to-all(bf16[16,32,128]{2,1,0:T(8,128)(2,1)S(1)} %broadcast_in_dim.62), channel_id=1, replica_groups=mesh['col'=16,'row'=8] {'col'}, dimensions={0} | all-to-all | bytes 262144 | tf_op jit(solution)/shard_map/all_to_all | solution.py:54
  297.7 9.4 %all_to_all.165 = bf16[8,32,128]{2,1,0:T(8,128)(2,1)S(1)} all-to-all(bf16[8,32,128]{2,1,0:T(8,128)(2,1)S(1)} %shard_map.99), channel_id=1, replica_groups=mesh['col'=16,'row'=8] {'row'}, dimensions={0} | all-to-all | bytes 131072 | tf_op jit(solution)/shard_map/all_to_all | solution.py:48
  (112 shorter events, 73.5 us)
Async XLA Ops:
  0.6 32.7 %copy-start.2 = (f32[8,1,128,128]{3,2,1,0:T(8,128)S(1)}, f32[8,1,128,128]{3,2,1,0:T(8,128)}, u32[]{:S(2)}) copy-start(f32[8,1,128,128]{3,2,1,0:T(8,128)} %param.36) | copy-start | bytes 1572868
  0.6 32.7 %copy-start.4 = (f32[8,1,32,128]{3,2,1,0:T(8,128)S(1)}, f32[8,1,32,128]{3,2,1,0:T(8,128)}, u32[]{:S(2)}) copy-start(f32[8,1,32,128]{3,2,1,0:T(8,128)} %param.35) | copy-start | bytes 393220
  2.5 14.5 %all-to-all-start = ((bf16[16,32,128]{2,1,0:T(8,128)(2,1)}), bf16[16,32,128]{2,1,0:T(8,128)(2,1)S(1)}, u32[]{:S(2)}, u32[]{:S(2)}) async-start(bf16[16,32,128]{2,1,0:T(8,128)(2,1)} %broadcast_in_dim.48), calls=%async_computation | async-start | bytes 262144 | tf_op jit(solution)/shard_map/all_to_all | solution.py:54
  17.1 3.1 %copy-start = (bf16[7,1,8,1,4,128,128]{6,5,4,3,2,1,0:T(8,128)(2,1)S(1)}, bf16[7,1,8,1,4,128,128]{6,5,4,3,2,1,0:T(8,128)(2,1)}, u32[]{:S(2)}) copy-start(bf16[7,1,8,1,4,128,128]{6,5,4,3,2,1,0:T(8,128)(2,1)} %param.37) | copy-start | bytes 22020100
  126.4 31.6 %copy-start.3 = (f32[8,1,128,128]{3,2,1,0:T(8,128)S(1)}, f32[8,1,128,128]{3,2,1,0:T(8,128)}, u32[]{:S(2)}) copy-start(f32[8,1,128,128]{3,2,1,0:T(8,128)} %param.39) | copy-start | bytes 1572868
  126.4 36.0 %copy-start.5 = (s32[7,1,8,1,4]{2,4,3,1,0:T(4,128)S(1)}, s32[7,1,8,1,4]{2,4,3,1,0:T(4,128)}, u32[]{:S(2)}) copy-start(s32[7,1,8,1,4]{2,4,3,1,0:T(4,128)} %param.41) | copy-start | bytes 2692
  157.9 36.1 %copy-start.6 = (f32[8,32,128]{2,1,0:T(8,128)}, f32[8,32,128]{2,1,0:T(8,128)S(1)}, u32[]{:S(2)}) copy-start(f32[8,32,128]{2,1,0:T(8,128)S(1)} %get-tuple-element.188) | copy-start | bytes 393220
  158.9 10.3 %all-to-all-start.14 = ((bf16[16,32,128]{2,1,0:T(8,128)(2,1)}), bf16[16,32,128]{2,1,0:T(8,128)(2,1)S(1)}, u32[]{:S(2)}, u32[]{:S(2)}) async-start(bf16[16,32,128]{2,1,0:T(8,128)(2,1)} %broadcast_in_dim.56), calls=%async_computation.14 | async-start | bytes 262144 | tf_op jit(solution)/shard_map/all_to_all | solution.py:54
  169.3 3.1 %copy-start.1 = (bf16[7,1,8,1,4,128,128]{6,5,4,3,2,1,0:T(8,128)(2,1)S(1)}, bf16[7,1,8,1,4,128,128]{6,5,4,3,2,1,0:T(8,128)(2,1)}, u32[]{:S(2)}) copy-start(bf16[7,1,8,1,4,128,128]{6,5,4,3,2,1,0:T(8,128)(2,1)} %param.40) | copy-start | bytes 22020100
  307.4 0.7 copy-start.7

commit v3 on v0

v3 whole, which is shorter than its diff:
```python
import functools

import jax
import jax.numpy as jnp
from jax import lax
from jax.experimental import pallas as pl
from jax.experimental.pallas import tpu as pltpu
from jax.sharding import PartitionSpec as P

BLOCKS_LAST = (((1,), (1,)), ((), ()))
AXES = ("col", "row")
PARTIAL_TYPE = jnp.bfloat16
VLIM = 12
SLIM = 28


def apply_inverse(inverse, vectors):
    return jnp.einsum("xi,oi->xo", vectors, inverse, precision=lax.Precision.HIGHEST)


def product_kernel(level, index_ref, history_ref, even_ref, odd_ref, *sum_refs):
    rows, slots = odd_ref.shape[:2]
    patterns = (index_ref.shape[0] - 2) // 2

    @pl.when(index_ref[1] == 1)
    def _():
        for step, sums_ref in enumerate(sum_refs):
            chip = index_ref[0] ^ step
            for core in range(2):
                m = chip * 2 + core
                picked, taken = [], []
                for side, blocks_ref in enumerate((even_ref, odd_ref)):
                    for s in range(slots):
                        where = index_ref[2 + side * patterns + (level * rows + m) * slots + s]
                        picked.append(history_ref[where, side])
                        taken.append(blocks_ref[m, s])
                total = lax.dot_general(
                    jnp.concatenate(taken, 1),
                    jnp.concatenate(picked, 1),
                    BLOCKS_LAST,
                    preferred_element_type=jnp.float32,
                )
                sums_ref[core] = total.T.astype(sums_ref.dtype)

    @pl.when(index_ref[1] == 0)
    def _():
        for ref in sum_refs:
            ref[...] = jnp.zeros_like(ref)


def level_terms(index, history, blocks, level):
    rows, slots, block = blocks[1].shape[:3]
    steps = rows // 2
    vmem = pl.BlockSpec(memory_space=pltpu.VMEM)
    shape = (2,) + history.shape[2:]
    out_shape = [jax.ShapeDtypeStruct(shape, jnp.float32)]
    out_shape += [jax.ShapeDtypeStruct(shape, PARTIAL_TYPE)] * (steps - 1)
    return pl.pallas_call(
        functools.partial(product_kernel, level),
        out_shape=out_shape,
        in_specs=[pl.BlockSpec(memory_space=pltpu.SMEM)] + [vmem] * 3,
        out_specs=[vmem] * steps,
        compiler_params=pltpu.CompilerParams(vmem_limit_bytes=VLIM * 2**20),
        cost_estimate=pl.CostEstimate(
            flops=4 * rows * slots * history.shape[2] * block * block,
            bytes_accessed=4 * rows * slots * block * block + 2 * history.size,
            transcendentals=0,
        ),
    )(index, history, *blocks)


def stage_kernel(places, _, *refs):
    sources, held, arrived = refs[: len(places)], refs[len(places) : -1], refs[-1]
    copies = []
    for source, at, kept in zip(sources, places, held):
        if len(kept.shape) == 4:
            pieces = [(source.at[at, m], kept.at[m]) for m in range(kept.shape[0])]
        else:
            pieces = [(source.at[at], kept)]
        for piece in pieces:
            copies.append(pltpu.make_async_copy(*piece, arrived.at[len(copies)]))
    for copy in copies:
        copy.start()
    for copy in copies:
        copy.wait()


def stage(after, following):
    arrays, places = zip(*following)
    vmem = pl.BlockSpec(memory_space=pltpu.VMEM)
    hbm = pl.BlockSpec(memory_space=pltpu.HBM)
    out_shape = [jax.ShapeDtypeStruct(array.shape[1:], array.dtype) for array in arrays]
    pieces = sum(array.shape[1] if array.ndim == 5 else 1 for array in arrays)
    return pl.pallas_call(
        functools.partial(stage_kernel, places),
        out_shape=out_shape,
        in_specs=[vmem] + [hbm] * len(arrays),
        out_specs=[vmem] * len(out_shape),
        scratch_shapes=[pltpu.SemaphoreType.DMA((pieces,))],
        compiler_params=pltpu.CompilerParams(vmem_limit_bytes=SLIM * 2**20),
        cost_estimate=pl.CostEstimate(flops=0, bytes_accessed=3 * 2**20, transcendentals=0),
    )(after, *[pltpu.with_memory_space_constraint(array, pltpu.HBM) for array in arrays])


def stack_kernel(*refs):
    values, (even_ref, odd_ref) = refs[:-2], refs[-2:]
    turns, tiers = even_ref.shape[:2]
    for i in range(turns):
        for j in range(tiers):
            even_ref[i, j] = values[2 * (i * tiers + j)][...]
            odd_ref[i, j] = values[2 * (i * tiers + j) + 1][...]


def stack_levels(*turns):
    values = [value for levels in turns for pair in levels for value in pair]
    shape = jax.ShapeDtypeStruct((len(turns), len(turns[0])) + values[0].shape, values[0].dtype)
    vmem = pl.BlockSpec(memory_space=pltpu.VMEM)
    return pl.pallas_call(
        stack_kernel,
        out_shape=[shape, shape],
        in_specs=[vmem] * len(values),
        out_specs=[vmem, vmem],
    )(*values)


def swap_cores(value):
    count = lax.axis_size("row")
    return lax.ppermute(value, "row", [(i, i ^ 1) for i in range(count)])


def reduce_rows(parts):
    count = lax.axis_size("row")
    total = parts[0]
    for step in (2, 3, 1):
        pairs = [(i, i ^ (2 * step if i % 2 else 2)) for i in range(count)]
        total = total + lax.ppermute(parts[step], "row", pairs).astype(jnp.float32)
    return total


def gather_groups(col_count, row_count):
    side = 1
    while side * side < col_count:
        side *= 2
    at = lambda x, y, r: (x * side + y) * row_count + r
    groups = [
        [at(x, y, r) for x in range(side) for y in range(side)] for r in range(1, row_count, 2)
    ]
    for x in range(0, side, 2):
        for y in range(0, side, 2):
            groups.append(
                [at(x + i, y + j, r) for i in range(2) for j in range(2) for r in range(0, row_count, 2)]
            )
    return groups


def share_solved(even, odd):
    col_count, row_count = lax.axis_size("col"), lax.axis_size("row")
    pair = jnp.stack([even, odd]).astype(jnp.bfloat16)
    copies = jnp.broadcast_to(pair, (col_count,) + pair.shape)
    return lax.all_to_all(
        copies, AXES, 0, 0, tiled=True, axis_index_groups=gather_groups(col_count, row_count)
    )


def per_device(
    right_side,
    lower_inverse,
    lower_blocks,
    lower_pattern,
    upper_inverse,
    upper_blocks,
    upper_pattern,
):
    col_count = lax.axis_size("col")
    tiers = right_side.shape[0]
    place = lax.axis_index("row")
    is_odd = place % 2 == 1
    right_odd = right_side[:, 0]
    low_inv_odd = lower_inverse[:, 0]
    high_inv_odd = upper_inverse[:, 0]
    low_odd = lower_blocks[:, 0, :, 0]
    high_odd = upper_blocks[:, 0, :, 0]
    low_pattern = lower_pattern.reshape(-1)
    high_pattern = upper_pattern.reshape(-1)

    first_odd = apply_inverse(low_inv_odd[0], right_odd[0])
    first_even = swap_cores(first_odd)
    pattern_even = swap_cores(jnp.concatenate([low_pattern, high_pattern]))
    here = jnp.stack([place // 2, place % 2]).astype(jnp.int32)
    low_index = jnp.concatenate([here, pattern_even[: low_pattern.size], low_pattern])
    high_index = jnp.concatenate([here, pattern_even[low_pattern.size :], high_pattern])
    history = jnp.zeros((tiers * col_count, 2) + right_odd.shape[1:], jnp.bfloat16)
    first_even, start, right, low_inv, low, high_inv, high, history = lax.optimization_barrier(
        (first_even, low_odd[0], right_odd, low_inv_odd, low_odd, high_inv_odd, high_odd, history)
    )
    blocks = (swap_cores(start), start)
    right_even = swap_cores(right)
    low_inv_even = swap_cores(low_inv)
    low_even = swap_cores(low)
    high_inv_even = swap_cores(high_inv)
    high_even = swap_cores(high)

    forward = [(first_even, first_odd)]
    history = history.at[:col_count].set(share_solved(first_even, first_odd))
    for tier in range(1, tiers):
        following = [(low_inv_even, tier), (low_inv_odd, tier), (right_even, tier), (right_odd, tier)]
        if tier < tiers - 1:
            following += [(low_even, tier), (low_odd, tier)]
        else:
            following += [(high_even, tier - 1), (high_odd, tier - 1)]
            following += [(high_inv_even, tier), (high_inv_odd, tier)]
        parts = level_terms(low_index, history, blocks, tier - 1)
        kept = stage(parts[0], following)
        blocks, top_inv = kept[4:6], kept[6:]
        sums = reduce_rows(parts)
        even = apply_inverse(kept[0], kept[2] - sums[0])
        odd = apply_inverse(kept[1], kept[3] - sums[1])
        even, odd = lax.optimization_barrier((even, odd))
        forward.append((even, odd))
        if tier < tiers - 1:
            history = history.at[tier * col_count : (tier + 1) * col_count].set(
                share_solved(even, odd)
            )
    backward = [None] * tiers
    for tier in range(tiers - 1, -1, -1):
        even, odd = forward[tier]
        if tier < tiers - 1:
            following = [(high_inv_even, tier), (high_inv_odd, tier)]
            if tier > 0:
                following += [(high_even, tier - 1), (high_odd, tier - 1)]
            parts = level_terms(high_index, history, blocks, tier)
            kept = stage(parts[0], following)
            top_inv, blocks = kept[:2], kept[2:]
            sums = reduce_rows(parts)
            even, odd = even - sums[0], odd - sums[1]
        even = apply_inverse(top_inv[0], even)
        odd = apply_inverse(top_inv[1], odd)
        even, odd = lax.optimization_barrier((even, odd))
        backward[tier] = (even, odd)
        if tier > 0:
            history = history.at[tier * col_count : (tier + 1) * col_count].set(
                share_solved(even, odd)
            )
    evens, odds = stack_levels(forward, backward)
    evens = swap_cores(evens)
    outs = [jnp.where(is_odd, odds[i], evens[i]) for i in range(2)]
    return outs[0][:, None], outs[1][:, None]


def solution(mesh):
    in_specs = (
        P(None, ("col", "row"), None, None),
        P(None, ("col", "row"), None, None),
        P(None, "col", None, "row", None, None, None),
        P(None, "col", None, "row", None),
        P(None, ("col", "row"), None, None),
        P(None, "col", None, "row", None, None, None),
        P(None, "col", None, "row", None),
    )
    out_specs = (P(None, ("col", "row"), None, None), P(None, ("col", "row"), None, None))
    return jax.shard_map(
        per_device, mesh=mesh, in_specs=in_specs, out_specs=out_specs, check_vma=False
    )
```

time: 794 us -> 299 us (0.38)
  waiting for transfers between devices: 451 us -> 28.4 us
  blocking collectives: 264 us -> 135 us
  starting transfers between devices: 0.58 us -> 62.6 us
  Pallas kernels: 0 us -> 45.8 us
  matrix products: 47.1 us -> 8.01 us
  between operations: 14.5 us -> 2.29 us
    reduce_scatter x14 -> x0, waiting for transfers between devices: 451 us -> none  [reduce_rows(): lax.psum_scatter(partial_value, 'row', scatter_dimension=0, tiled=True)[0]]
    all_gather x14 -> x0, blocking collectives: 264 us -> none  [share_solved(): lax.all_gather(solved.astype(jnp.bfloat16)[None], 'col', axis=0, tiled=True)]
    all_to_all x0 -> x12, blocking collectives: none -> 135 us  [share_solved(): lax.all_to_all(copies, AXES, 0, 0, tiled=True, axis_index_groups=gather_g...]
    ppermute x0 -> x51, starting transfers between devices: none -> 52 us  [the longest x42 47.7 us: reduce_rows(): total = total + lax.ppermute(parts[step], 'row', pairs).astype(jnp.float32)]
    pallas_call x0 -> x29, Pallas kernels: none -> 45.8 us  [the longest x14 25 us: stage(): pl.pallas_call(functools.partial(stage_kernel, places), out_shape=out_sha...]
    dot_general x14 -> x0, matrix products: 32.8 us -> none  [level_terms(): jnp.einsum('msxj,msoj->mxo', picked, blocks, preferred_element_type=jnp.f...]
    ppermute x0 -> x51, waiting for transfers between devices: none -> 16.7 us  [the longest x42 13.3 us: reduce_rows(): total = total + lax.ppermute(parts[step], 'row', pairs).astype(jnp.float32)]
    all_to_all x0 -> x2, waiting for transfers between devices: none -> 11.8 us  [share_solved(): lax.all_to_all(copies, AXES, 0, 0, tiled=True, axis_index_groups=gather_g...]
  transfers between devices with their start and end apart: 14 -> 53, of which waited for: 14 -> 24; matrix products, arithmetic and copies ran while one was open for 0% -> 2% of each run, Pallas kernels for 0% -> 11%
where the time goes in v3:
time: 299 us; the launch traced here: 297 us
  blocking collectives  135 us (45%)
  starting transfers between devices  62.6 us (21%)
  Pallas kernels  45.8 us (15%)
  waiting for transfers between devices  28.4 us (9%)
  local copies, waits for them, and re-layouts  12.8 us (4%)
  matrix products  8.01 us (3%)
    all_to_all x12, blocking collectives, share_solved(): lax.all_to_all(copies, AXES, 0, 0, tiled=True, axis_index_groups=gather_g...  135 us
    ppermute x42, starting transfers between devices, reduce_rows(): total = total + lax.ppermute(parts[step], 'row', pairs).astype(jnp.float32)  47.7 us
    pallas_call x14, Pallas kernels, stage(): pl.pallas_call(functools.partial(stage_kernel, places), out_shape=out_sha...  25 us
    pallas_call x14, Pallas kernels, level_terms(): pl.pallas_call(functools.partial(product_kernel, level), out_shape=out_sh...  19 us
    ppermute x42, waiting for transfers between devices, reduce_rows(): total = total + lax.ppermute(parts[step], 'row', pairs).astype(jnp.float32)  13.3 us
    all_to_all x2, waiting for transfers between devices, share_solved(): lax.all_to_all(copies, AXES, 0, 0, tiled=True, axis_index_groups=gather_g...  11.8 us
    all_to_all x2, starting transfers between devices, share_solved(): lax.all_to_all(copies, AXES, 0, 0, tiled=True, axis_index_groups=gather_g...  10.6 us
    unnamed x96, local copies, waits for them, and re-layouts  8.16 us
  transfers between devices with their start and end apart: 53, of which 24 were waited for; matrix products, arithmetic and copies ran while one was open for 2% of the time, Pallas kernels for 11%

profile of v3, /device:TPU:1, one launch (start us, length us, event | category | flops | bytes accessed | tf_op | source)
XLA Modules:
  0.0 297.3 jit_solution(6474933134594682356)
XLA Ops:
  6.6 6.8 %all-to-all-start = ((bf16[16,2,32,128]{3,2,1,0:T(8,128)(2,1)}), bf16[16,2,32,128]{3,2,1,0:T(8,128)(2,1)S(1)}, u32[]{:S(2)}, u32[]{:S(2)}) async-start(bf16[16,2,32,128]{3,2,1,0:T(8,128)(2,1)} %broadcast_in_dim.48), calls=%async_computation | async-start | bytes 524288 | tf_op jit(solution)/shard_map/all_to_all | solution.py:160
  16.3 4.5 %all-to-all-done = bf16[16,2,32,128]{3,2,1,0:T(8,128)(2,1)S(1)} async-done(((bf16[16,2,32,128]{3,2,1,0:T(8,128)(2,1)}), bf16[16,2,32,128]{3,2,1,0:T(8,128)(2,1)S(1)}, u32[]{:S(2)}, u32[]{:S(2)}) %all-to-all-start) | async-done | bytes 262176 | tf_op jit(solution)/shard_map/all_to_all | solution.py:160
  23.5 4.0 %collective-permute-start.6 = (bf16[2,32,128]{2,1,0:T(8,128)(2,1)S(1)}, bf16[2,32,128]{2,1,0:T(8,128)(2,1)S(1)}, u32[]{:S(2)}, u32[]{:S(2)}) collective-permute-start(bf16[2,32,128]{2,1,0:T(8,128)(2,1)S(1)} %get-tuple-element.344), channel_id=1, source_target_pairs={{0,2},{1,5},{2,0},{3,7},{4,6},{5,1},{6,4},{7,3},{8,10},{9,13},{10,... | collective-permute-start | bytes 49160 | tf_op jit(solution)/shard_map/ppermute | solution.py:136
  32.0 2.1 shard_map.87
  34.7 12.1 %all_to_all.70 = bf16[16,2,32,128]{3,2,1,0:T(8,128)(2,1)S(1)} all-to-all(bf16[16,2,32,128]{3,2,1,0:T(8,128)(2,1)S(1)} %broadcast_in_dim.49), channel_id=1, replica_groups={{1,9,17,25,33,41,49,57,65,73,81,89,97,105,113,121},{3,11,19,27,35,43,51..., dimensions={0} | all-to-all | bytes 524288 | tf_op jit(solution)/shard_map/all_to_all | solution.py:160
  49.5 2.6 collective-permute-start.9
  54.5 11.3 %all_to_all.71 = bf16[16,2,32,128]{3,2,1,0:T(8,128)(2,1)S(1)} all-to-all(bf16[16,2,32,128]{3,2,1,0:T(8,128)(2,1)S(1)} %broadcast_in_dim.50), channel_id=1, replica_groups={{1,9,17,25,33,41,49,57,65,73,81,89,97,105,113,121},{3,11,19,27,35,43,51..., dimensions={0} | all-to-all | bytes 524288 | tf_op jit(solution)/shard_map/all_to_all | solution.py:160
  67.2 2.7 collective-permute-start.12
  74.2 10.9 %all_to_all.72 = bf16[16,2,32,128]{3,2,1,0:T(8,128)(2,1)S(1)} all-to-all(bf16[16,2,32,128]{3,2,1,0:T(8,128)(2,1)S(1)} %broadcast_in_dim.51), channel_id=1, replica_groups={{1,9,17,25,33,41,49,57,65,73,81,89,97,105,113,121},{3,11,19,27,35,43,51..., dimensions={0} | all-to-all | bytes 524288 | tf_op jit(solution)/shard_map/all_to_all | solution.py:160
  86.5 2.3 collective-permute-start.15
  93.2 10.9 %all_to_all.73 = bf16[16,2,32,128]{3,2,1,0:T(8,128)(2,1)S(1)} all-to-all(bf16[16,2,32,128]{3,2,1,0:T(8,128)(2,1)S(1)} %broadcast_in_dim.52), channel_id=1, replica_groups={{1,9,17,25,33,41,49,57,65,73,81,89,97,105,113,121},{3,11,19,27,35,43,51..., dimensions={0} | all-to-all | bytes 524288 | tf_op jit(solution)/shard_map/all_to_all | solution.py:160
  112.6 11.0 %all_to_all.74 = bf16[16,2,32,128]{3,2,1,0:T(8,128)(2,1)S(1)} all-to-all(bf16[16,2,32,128]{3,2,1,0:T(8,128)(2,1)S(1)} %broadcast_in_dim.53), channel_id=1, replica_groups={{1,9,17,25,33,41,49,57,65,73,81,89,97,105,113,121},{3,11,19,27,35,43,51..., dimensions={0} | all-to-all | bytes 524288 | tf_op jit(solution)/shard_map/all_to_all | solution.py:160
  131.9 11.7 %all_to_all.75 = bf16[16,2,32,128]{3,2,1,0:T(8,128)(2,1)S(1)} all-to-all(bf16[16,2,32,128]{3,2,1,0:T(8,128)(2,1)S(1)} %broadcast_in_dim.54), channel_id=1, replica_groups={{1,9,17,25,33,41,49,57,65,73,81,89,97,105,113,121},{3,11,19,27,35,43,51..., dimensions={0} | all-to-all | bytes 524288 | tf_op jit(solution)/shard_map/all_to_all | solution.py:160
  149.2 2.3 copy-done.2
  156.1 3.8 %all-to-all-start.7 = ((bf16[16,2,32,128]{3,2,1,0:T(8,128)(2,1)}), bf16[16,2,32,128]{3,2,1,0:T(8,128)(2,1)S(1)}, u32[]{:S(2)}, u32[]{:S(2)}) async-start(bf16[16,2,32,128]{3,2,1,0:T(8,128)(2,1)} %broadcast_in_dim.55), calls=%async_computation.7 | async-start | bytes 524288 | tf_op jit(solution)/shard_map/all_to_all | solution.py:160
  160.0 7.3 %all-to-all-done.7 = bf16[16,2,32,128]{3,2,1,0:T(8,128)(2,1)S(1)} async-done(((bf16[16,2,32,128]{3,2,1,0:T(8,128)(2,1)}), bf16[16,2,32,128]{3,2,1,0:T(8,128)(2,1)S(1)}, u32[]{:S(2)}, u32[]{:S(2)}) %all-to-all-start.7) | async-done | bytes 262176 | tf_op jit(solution)/shard_map/all_to_all | solution.py:160
  169.8 2.7 collective-permute-start.29
  177.0 11.1 %all_to_all.76 = bf16[16,2,32,128]{3,2,1,0:T(8,128)(2,1)S(1)} all-to-all(bf16[16,2,32,128]{3,2,1,0:T(8,128)(2,1)S(1)} %broadcast_in_dim.56), channel_id=1, replica_groups={{1,9,17,25,33,41,49,57,65,73,81,89,97,105,113,121},{3,11,19,27,35,43,51..., dimensions={0} | all-to-all | bytes 524288 | tf_op jit(solution)/shard_map/all_to_all | solution.py:160
  189.4 2.2 collective-permute-start.32
  196.0 11.1 %all_to_all.77 = bf16[16,2,32,128]{3,2,1,0:T(8,128)(2,1)S(1)} all-to-all(bf16[16,2,32,128]{3,2,1,0:T(8,128)(2,1)S(1)} %broadcast_in_dim.57), channel_id=1, replica_groups={{1,9,17,25,33,41,49,57,65,73,81,89,97,105,113,121},{3,11,19,27,35,43,51..., dimensions={0} | all-to-all | bytes 524288 | tf_op jit(solution)/shard_map/all_to_all | solution.py:160
  215.1 11.3 %all_to_all.78 = bf16[16,2,32,128]{3,2,1,0:T(8,128)(2,1)S(1)} all-to-all(bf16[16,2,32,128]{3,2,1,0:T(8,128)(2,1)S(1)} %broadcast_in_dim.58), channel_id=1, replica_groups={{1,9,17,25,33,41,49,57,65,73,81,89,97,105,113,121},{3,11,19,27,35,43,51..., dimensions={0} | all-to-all | bytes 524288 | tf_op jit(solution)/shard_map/all_to_all | solution.py:160
  234.1 11.2 %all_to_all.79 = bf16[16,2,32,128]{3,2,1,0:T(8,128)(2,1)S(1)} all-to-all(bf16[16,2,32,128]{3,2,1,0:T(8,128)(2,1)S(1)} %broadcast_in_dim.59), channel_id=1, replica_groups={{1,9,17,25,33,41,49,57,65,73,81,89,97,105,113,121},{3,11,19,27,35,43,51..., dimensions={0} | all-to-all | bytes 524288 | tf_op jit(solution)/shard_map/all_to_all | solution.py:160
  253.0 11.3 %all_to_all.80 = bf16[16,2,32,128]{3,2,1,0:T(8,128)(2,1)S(1)} all-to-all(bf16[16,2,32,128]{3,2,1,0:T(8,128)(2,1)S(1)} %broadcast_in_dim.60), channel_id=1, replica_groups={{1,9,17,25,33,41,49,57,65,73,81,89,97,105,113,121},{3,11,19,27,35,43,51..., dimensions={0} | all-to-all | bytes 524288 | tf_op jit(solution)/shard_map/all_to_all | solution.py:160
  271.9 11.2 %all_to_all.81 = bf16[16,2,32,128]{3,2,1,0:T(8,128)(2,1)S(1)} all-to-all(bf16[16,2,32,128]{3,2,1,0:T(8,128)(2,1)S(1)} %broadcast_in_dim.61), channel_id=1, replica_groups={{1,9,17,25,33,41,49,57,65,73,81,89,97,105,113,121},{3,11,19,27,35,43,51..., dimensions={0} | all-to-all | bytes 524288 | tf_op jit(solution)/shard_map/all_to_all | solution.py:160
  (343 shorter events, 116.6 us)
Async XLA Ops:
  4.6 26.8 %collective-permute-start.5 = (bf16[7,8,4,128,128]{4,3,2,1,0:T(8,128)(2,1)}, bf16[7,8,4,128,128]{4,3,2,1,0:T(8,128)(2,1)}, u32[]{:S(2)}, u32[]{:S(2)}) collective-permute-start(bf16[7,8,4,128,128]{4,3,2,1,0:T(8,128)(2,1)} %bitcast.271), channel_id=1, source_target_pairs={{0,1},{1,0},{2,3},{3,2},{4,5},{5,4},{6,7},{7,6},{8,9},{9,8},{10,11... | collective-permute-start | bytes 22020104 | tf_op jit(solution)/shard_map/ppermute | solution.py:128
  5.1 16.3 %collective-permute-start.2 = (bf16[8,4,128,128]{3,2,1,0:T(8,128)(2,1)S(1)}, bf16[8,4,128,128]{3,2,1,0:T(8,128)(2,1)}, u32[]{:S(2)}, u32[]{:S(2)}) collective-permute-start(bf16[8,4,128,128]{3,2,1,0:T(8,128)(2,1)S(1)} %slice_bitcast_fusion.odd_ref), channel_id=1, source_target_pairs={{0,1},{1,0},{2,3},{3,2},{4,5},{5,4},{6,7},{7,6},{8,9},{9,8},{10,11... | collective-permute-start | bytes 3145736 | tf_op jit(solution)/shard_map/ppermute | solution.py:128
  5.8 10.4 %collective-permute-start.1 = (s32[448]{0:T(512)S(1)}, s32[448]{0:T(512)S(1)}, u32[]{:S(2)}, u32[]{:S(2)}) collective-permute-start(s32[448]{0:T(512)S(1)} %pad_add_fusion), channel_id=1, source_target_pairs={{0,1},{1,0},{2,3},{3,2},{4,5},{5,4},{6,7},{7,6},{8,9},{9,8},{10,11... | collective-permute-start | bytes 5384 | tf_op jit(solution)/shard_map/ppermute | solution.py:128
  6.6 14.2 %all-to-all-start = ((bf16[16,2,32,128]{3,2,1,0:T(8,128)(2,1)}), bf16[16,2,32,128]{3,2,1,0:T(8,128)(2,1)S(1)}, u32[]{:S(2)}, u32[]{:S(2)}) async-start(bf16[16,2,32,128]{3,2,1,0:T(8,128)(2,1)} %broadcast_in_dim.48), calls=%async_computation | async-start | bytes 524288 | tf_op jit(solution)/shard_map/all_to_all | solution.py:160
  13.4 17.9 %collective-permute-start.3 = (f32[8,128,128]{2,1,0:T(8,128)}, f32[8,128,128]{2,1,0:T(8,128)}, u32[]{:S(2)}, u32[]{:S(2)}) collective-permute-start(f32[8,128,128]{2,1,0:T(8,128)} %bitcast.5.refs_1_), channel_id=1, source_target_pairs={{0,1},{1,0},{2,3},{3,2},{4,5},{5,4},{6,7},{7,6},{8,9},{9,8},{10,11... | collective-permute-start | bytes 1572872 | tf_op jit(solution)/shard_map/ppermute | solution.py:128
  23.5 5.1 %collective-permute-start.6 = (bf16[2,32,128]{2,1,0:T(8,128)(2,1)S(1)}, bf16[2,32,128]{2,1,0:T(8,128)(2,1)S(1)}, u32[]{:S(2)}, u32[]{:S(2)}) collective-permute-start(bf16[2,32,128]{2,1,0:T(8,128)(2,1)S(1)} %get-tuple-element.344), channel_id=1, source_target_pairs={{0,2},{1,5},{2,0},{3,7},{4,6},{5,1},{6,4},{7,3},{8,10},{9,13},{10,... | collective-permute-start | bytes 49160 | tf_op jit(solution)/shard_map/ppermute | solution.py:136
  48.1 5.8 %collective-permute-start.10 = (bf16[2,32,128]{2,1,0:T(8,128)(2,1)S(1)}, bf16[2,32,128]{2,1,0:T(8,128)(2,1)S(1)}, u32[]{:S(2)}, u32[]{:S(2)}) collective-permute-start(bf16[2,32,128]{2,1,0:T(8,128)(2,1)S(1)} %get-tuple-element.357), channel_id=1, source_target_pairs={{0,2},{1,7},{2,0},{3,5},{4,6},{5,3},{6,4},{7,1},{8,10},{9,15},{10,... | collective-permute-start | bytes 49160 | tf_op jit(solution)/shard_map/ppermute | solution.py:136
  49.2 4.7 %collective-permute-start.11 = (bf16[2,32,128]{2,1,0:T(8,128)(2,1)S(1)}, bf16[2,32,128]{2,1,0:T(8,128)(2,1)S(1)}, u32[]{:S(2)}, u32[]{:S(2)}) collective-permute-start(bf16[2,32,128]{2,1,0:T(8,128)(2,1)S(1)} %get-tuple-element.358), channel_id=1, source_target_pairs={{0,2},{1,3},{2,0},{3,1},{4,6},{5,7},{6,4},{7,5},{8,10},{9,11},{10,... | collective-permute-start | bytes 49160 | tf_op jit(solution)/shard_map/ppermute | solution.py:136
  52.1 96.3 %collective-permute-start.24 = (bf16[7,8,4,128,128]{4,3,2,1,0:T(8,128)(2,1)S(1)}, bf16[7,8,4,128,128]{4,3,2,1,0:T(8,128)(2,1)S(1)}, u32[]{:S(2)}, u32[]{:S(2)}) collective-permute-start(bf16[7,8,4,128,128]{4,3,2,1,0:T(8,128)(2,1)S(1)} %bitcast.269), channel_id=1, source_target_pairs={{0,1},{1,0},{2,3},{3,2},{4,5},{5,4},{6,7},{7,6},{8,9},{9,8},{10,11... | collective-permute-start | bytes 22020104 | tf_op jit(solution)/shard_map/ppermute | solution.py:128
  67.2 5.4 %collective-permute-start.12 = (bf16[2,32,128]{2,1,0:T(8,128)(2,1)S(1)}, bf16[2,32,128]{2,1,0:T(8,128)(2,1)S(1)}, u32[]{:S(2)}, u32[]{:S(2)}) collective-permute-start(bf16[2,32,128]{2,1,0:T(8,128)(2,1)S(1)} %get-tuple-element.368), channel_id=1, source_target_pairs={{0,2},{1,5},{2,0},{3,7},{4,6},{5,1},{6,4},{7,3},{8,10},{9,13},{10,... | collective-permute-start | bytes 49160 | tf_op jit(solution)/shard_map/ppermute | solution.py:136
  86.5 5.0 %collective-permute-start.15 = (bf16[2,32,128]{2,1,0:T(8,128)(2,1)S(1)}, bf16[2,32,128]{2,1,0:T(8,128)(2,1)S(1)}, u32[]{:S(2)}, u32[]{:S(2)}) collective-permute-start(bf16[2,32,128]{2,1,0:T(8,128)(2,1)S(1)} %get-tuple-element.380), channel_id=1, source_target_pairs={{0,2},{1,5},{2,0},{3,7},{4,6},{5,1},{6,4},{7,3},{8,10},{9,13},{10,... | collective-permute-start | bytes 49160 | tf_op jit(solution)/shard_map/ppermute | solution.py:136
  105.5 4.9 %collective-permute-start.18 = (bf16[2,32,128]{2,1,0:T(8,128)(2,1)S(1)}, bf16[2,32,128]{2,1,0:T(8,128)(2,1)S(1)}, u32[]{:S(2)}, u32[]{:S(2)}) collective-permute-start(bf16[2,32,128]{2,1,0:T(8,128)(2,1)S(1)} %get-tuple-element.392), channel_id=1, source_target_pairs={{0,2},{1,5},{2,0},{3,7},{4,6},{5,1},{6,4},{7,3},{8,10},{9,13},{10,... | collective-permute-start | bytes 49160 | tf_op jit(solution)/shard_map/ppermute | solution.py:136
  125.0 4.8 %collective-permute-start.21 = (bf16[2,32,128]{2,1,0:T(8,128)(2,1)S(1)}, bf16[2,32,128]{2,1,0:T(8,128)(2,1)S(1)}, u32[]{:S(2)}, u32[]{:S(2)}) collective-permute-start(bf16[2,32,128]{2,1,0:T(8,128)(2,1)S(1)} %get-tuple-element.404), channel_id=1, source_target_pairs={{0,2},{1,5},{2,0},{3,7},{4,6},{5,1},{6,4},{7,3},{8,10},{9,13},{10,... | collective-permute-start | bytes 49160 | tf_op jit(solution)/shard_map/ppermute | solution.py:136
  127.9 20.4 %collective-permute-start.25 = (f32[8,128,128]{2,1,0:T(8,128)S(1)}, f32[8,128,128]{2,1,0:T(8,128)S(1)}, u32[]{:S(2)}, u32[]{:S(2)}) collective-permute-start(f32[8,128,128]{2,1,0:T(8,128)S(1)} %bitcast.286), channel_id=1, source_target_pairs={{0,1},{1,0},{2,3},{3,2},{4,5},{5,4},{6,7},{7,6},{8,9},{9,8},{10,11... | collective-permute-start | bytes 1572872 | tf_op jit(solution)/shard_map/ppermute | solution.py:128
  144.9 9.4 %collective-permute-start.26 = (bf16[2,32,128]{2,1,0:T(8,128)(2,1)S(1)}, bf16[2,32,128]{2,1,0:T(8,128)(2,1)S(1)}, u32[]{:S(2)}, u32[]{:S(2)}) collective-permute-start(bf16[2,32,128]{2,1,0:T(8,128)(2,1)S(1)} %get-tuple-element.418), channel_id=1, source_target_pairs={{0,2},{1,5},{2,0},{3,7},{4,6},{5,1},{6,4},{7,3},{8,10},{9,13},{10,... | collective-permute-start | bytes 49160 | tf_op jit(solution)/shard_map/ppermute | solution.py:136
  146.9 7.4 %collective-permute-start.27 = (bf16[2,32,128]{2,1,0:T(8,128)(2,1)S(1)}, bf16[2,32,128]{2,1,0:T(8,128)(2,1)S(1)}, u32[]{:S(2)}, u32[]{:S(2)}) collective-permute-start(bf16[2,32,128]{2,1,0:T(8,128)(2,1)S(1)} %get-tuple-element.419), channel_id=1, source_target_pairs={{0,2},{1,7},{2,0},{3,5},{4,6},{5,3},{6,4},{7,1},{8,10},{9,15},{10,... | collective-permute-start | bytes 49160 | tf_op jit(solution)/shard_map/ppermute | solution.py:136
  148.3 6.0 %collective-permute-start.28 = (bf16[2,32,128]{2,1,0:T(8,128)(2,1)S(1)}, bf16[2,32,128]{2,1,0:T(8,128)(2,1)S(1)}, u32[]{:S(2)}, u32[]{:S(2)}) collective-permute-start(bf16[2,32,128]{2,1,0:T(8,128)(2,1)S(1)} %get-tuple-element.420), channel_id=1, source_target_pairs={{0,2},{1,3},{2,0},{3,1},{4,6},{5,7},{6,4},{7,5},{8,10},{9,11},{10,... | collective-permute-start | bytes 49160 | tf_op jit(solution)/shard_map/ppermute | solution.py:136
  156.1 11.2 %all-to-all-start.7 = ((bf16[16,2,32,128]{3,2,1,0:T(8,128)(2,1)}), bf16[16,2,32,128]{3,2,1,0:T(8,128)(2,1)S(1)}, u32[]{:S(2)}, u32[]{:S(2)}) async-start(bf16[16,2,32,128]{3,2,1,0:T(8,128)(2,1)} %broadcast_in_dim.55), calls=%async_computation.7 | async-start | bytes 524288 | tf_op jit(solution)/shard_map/all_to_all | solution.py:160
  169.8 5.7 %collective-permute-start.29 = (bf16[2,32,128]{2,1,0:T(8,128)(2,1)S(1)}, bf16[2,32,128]{2,1,0:T(8,128)(2,1)S(1)}, u32[]{:S(2)}, u32[]{:S(2)}) collective-permute-start(bf16[2,32,128]{2,1,0:T(8,128)(2,1)S(1)} %get-tuple-element.433), channel_id=1, source_target_pairs={{0,2},{1,5},{2,0},{3,7},{4,6},{5,1},{6,4},{7,3},{8,10},{9,13},{10,... | collective-permute-start | bytes 49160 | tf_op jit(solution)/shard_map/ppermute | solution.py:136
  189.4 5.0 %collective-permute-start.32 = (bf16[2,32,128]{2,1,0:T(8,128)(2,1)S(1)}, bf16[2,32,128]{2,1,0:T(8,128)(2,1)S(1)}, u32[]{:S(2)}, u32[]{:S(2)}) collective-permute-start(bf16[2,32,128]{2,1,0:T(8,128)(2,1)S(1)} %get-tuple-element.443), channel_id=1, source_target_pairs={{0,2},{1,5},{2,0},{3,7},{4,6},{5,1},{6,4},{7,3},{8,10},{9,13},{10,... | collective-permute-start | bytes 49160 | tf_op jit(solution)/shard_map/ppermute | solution.py:136
  208.5 4.8 %collective-permute-start.35 = (bf16[2,32,128]{2,1,0:T(8,128)(2,1)S(1)}, bf16[2,32,128]{2,1,0:T(8,128)(2,1)S(1)}, u32[]{:S(2)}, u32[]{:S(2)}) collective-permute-start(bf16[2,32,128]{2,1,0:T(8,128)(2,1)S(1)} %get-tuple-element.453), channel_id=1, source_target_pairs={{0,2},{1,5},{2,0},{3,7},{4,6},{5,1},{6,4},{7,3},{8,10},{9,13},{10,... | collective-permute-start | bytes 49160 | tf_op jit(solution)/shard_map/ppermute | solution.py:136
  227.7 4.8 %collective-permute-start.38 = (bf16[2,32,128]{2,1,0:T(8,128)(2,1)S(1)}, bf16[2,32,128]{2,1,0:T(8,128)(2,1)S(1)}, u32[]{:S(2)}, u32[]{:S(2)}) collective-permute-start(bf16[2,32,128]{2,1,0:T(8,128)(2,1)S(1)} %get-tuple-element.463), channel_id=1, source_target_pairs={{0,2},{1,5},{2,0},{3,7},{4,6},{5,1},{6,4},{7,3},{8,10},{9,13},{10,... | collective-permute-start | bytes 49160 | tf_op jit(solution)/shard_map/ppermute | solution.py:136
  246.6 5.0 %collective-permute-start.41 = (bf16[2,32,128]{2,1,0:T(8,128)(2,1)S(1)}, bf16[2,32,128]{2,1,0:T(8,128)(2,1)S(1)}, u32[]{:S(2)}, u32[]{:S(2)}) collective-permute-start(bf16[2,32,128]{2,1,0:T(8,128)(2,1)S(1)} %get-tuple-element.473), channel_id=1, source_target_pairs={{0,2},{1,5},{2,0},{3,7},{4,6},{5,1},{6,4},{7,3},{8,10},{9,13},{10,... | collective-permute-start | bytes 49160 | tf_op jit(solution)/shard_map/ppermute | solution.py:136
  265.7 4.9 %collective-permute-start.44 = (bf16[2,32,128]{2,1,0:T(8,128)(2,1)S(1)}, bf16[2,32,128]{2,1,0:T(8,128)(2,1)S(1)}, u32[]{:S(2)}, u32[]{:S(2)}) collective-permute-start(bf16[2,32,128]{2,1,0:T(8,128)(2,1)S(1)} %get-tuple-element.483), channel_id=1, source_target_pairs={{0,2},{1,5},{2,0},{3,7},{4,6},{5,1},{6,4},{7,3},{8,10},{9,13},{10,... | collective-permute-start | bytes 49160 | tf_op jit(solution)/shard_map/ppermute | solution.py:136
  (76 other events, 1820.1 us)

commit v4 on v3

--- a/solution.py
+++ b/solution.py
@@ -11,7 +11,8 @@
 AXES = ("col", "row")
 PARTIAL_TYPE = jnp.bfloat16
 VLIM = 12
-SLIM = 28
+SLIM = 12
+TURN = 2
 
 
 def apply_inverse(inverse, vectors):
@@ -99,7 +100,7 @@
         scratch_shapes=[pltpu.SemaphoreType.DMA((pieces,))],
         compiler_params=pltpu.CompilerParams(vmem_limit_bytes=SLIM * 2**20),
         cost_estimate=pl.CostEstimate(flops=0, bytes_accessed=3 * 2**20, transcendentals=0),
-    )(after, *[pltpu.with_memory_space_constraint(array, pltpu.HBM) for array in arrays])
+    )(after, *[in_hbm(array) for array in arrays])
 
 
 def stack_kernel(*refs):
@@ -121,6 +122,10 @@
         in_specs=[vmem] * len(values),
         out_specs=[vmem, vmem],
     )(*values)
+
+
+def in_hbm(value):
+    return pltpu.with_memory_space_constraint(value, pltpu.HBM)
 
 
 def swap_cores(value):
@@ -189,6 +194,7 @@
     here = jnp.stack([place // 2, place % 2]).astype(jnp.int32)
     low_index = jnp.concatenate([here, pattern_even[: low_pattern.size], low_pattern])
     high_index = jnp.concatenate([here, pattern_even[low_pattern.size :], high_pattern])
+    low_index, high_index = lax.optimization_barrier((low_index, high_index))
     history = jnp.zeros((tiers * col_count, 2) + right_odd.shape[1:], jnp.bfloat16)
     first_even, start, right, low_inv, low, high_inv, high, history = lax.optimization_barrier(
         (first_even, low_odd[0], right_odd, low_inv_odd, low_odd, high_inv_odd, high_odd, history)
@@ -196,9 +202,7 @@
     blocks = (swap_cores(start), start)
     right_even = swap_cores(right)
     low_inv_even = swap_cores(low_inv)
-    low_even = swap_cores(low)
-    high_inv_even = swap_cores(high_inv)
-    high_even = swap_cores(high)
+    low_even = in_hbm(swap_cores(in_hbm(low)))
 
     forward = [(first_even, first_odd)]
     history = history.at[:col_count].set(share_solved(first_even, first_odd))
@@ -216,6 +220,14 @@
         even = apply_inverse(kept[0], kept[2] - sums[0])
         odd = apply_inverse(kept[1], kept[3] - sums[1])
         even, odd = lax.optimization_barrier((even, odd))
+        if tier == TURN:
+            even, odd, high, high_inv = lax.optimization_barrier((even, odd, high, high_inv))
+            high_inv_even = swap_cores(high_inv)
+            high_even = in_hbm(swap_cores(in_hbm(high)))
+        if tier == TURN + 3:
+            even, odd, high_even, high_inv_even = lax.optimization_barrier(
+                (even, odd, high_even, high_inv_even)
+            )
         forward.append((even, odd))
         if tier < tiers - 1:
             history = history.at[tier * col_count : (tier + 1) * col_count].set(

time: 299 us -> 293 us (0.980)
  blocking collectives: 135 us -> 146 us
  local copies, waits for them, and re-layouts: 12.8 us -> 5.85 us
  waiting for transfers between devices: 28.4 us -> 23.3 us
  starting transfers between devices: 62.6 us -> 59 us
    all_to_all x12 -> x13, blocking collectives: 135 us -> 146 us  [share_solved(): lax.all_to_all(copies, AXES, 0, 0, tiled=True, axis_index_groups=gather_g...]
    all_to_all x2 -> x1, waiting for transfers between devices: 11.8 us -> 3.23 us  [share_solved(): lax.all_to_all(copies, AXES, 0, 0, tiled=True, axis_index_groups=gather_g...]
    unnamed x96 -> x84, local copies, waits for them, and re-layouts: 8.16 us -> 1.93 us
    all_to_all x2 -> x1, starting transfers between devices: 10.6 us -> 6.84 us  [share_solved(): lax.all_to_all(copies, AXES, 0, 0, tiled=True, axis_index_groups=gather_g...]
  transfers between devices with their start and end apart: 53 -> 52, of which waited for: 24 -> 21; matrix products, arithmetic and copies ran while one was open for 2% -> 2% of each run, Pallas kernels for 11% -> 10%
where the time goes in v4:
time: 293 us; the launch traced here: 291 us
  blocking collectives  146 us (50%)
  starting transfers between devices  59 us (20%)
  Pallas kernels  44.9 us (15%)
  waiting for transfers between devices  23.3 us (8%)
  matrix products  8.04 us (3%)
  local copies, waits for them, and re-layouts  5.85 us (2%)
    all_to_all x13, blocking collectives, share_solved(): lax.all_to_all(copies, AXES, 0, 0, tiled=True, axis_index_groups=gather_g...  146 us
    ppermute x42, starting transfers between devices, reduce_rows(): total = total + lax.ppermute(parts[step], 'row', pairs).astype(jnp.float32)  47.5 us
    pallas_call x14, Pallas kernels, stage(): pl.pallas_call(functools.partial(stage_kernel, places), out_shape=out_sha...  24.8 us
    pallas_call x14, Pallas kernels, level_terms(): pl.pallas_call(functools.partial(product_kernel, level), out_shape=out_sh...  18.3 us
    ppermute x42, waiting for transfers between devices, reduce_rows(): total = total + lax.ppermute(parts[step], 'row', pairs).astype(jnp.float32)  15.8 us
    dot_general x31, matrix products, apply_inverse(): jnp.einsum('xi,oi->xo', vectors, inverse, precision=lax.Precision.HIGHEST)  8.04 us
    all_to_all x1, starting transfers between devices, share_solved(): lax.all_to_all(copies, AXES, 0, 0, tiled=True, axis_index_groups=gather_g...  6.84 us
  transfers between devices with their start and end apart: 52, of which 21 were waited for; matrix products, arithmetic and copies ran while one was open for 2% of the time, Pallas kernels for 10%

profile of v4, /device:TPU:1, one launch (start us, length us, event | category | flops | bytes accessed | tf_op | source)
XLA Modules:
  0.0 291.4 jit_solution(13555647641555148507)
XLA Ops:
  6.7 6.8 %all-to-all-start = ((bf16[16,2,32,128]{3,2,1,0:T(8,128)(2,1)}), bf16[16,2,32,128]{3,2,1,0:T(8,128)(2,1)S(1)}, u32[]{:S(2)}, u32[]{:S(2)}) async-start(bf16[16,2,32,128]{3,2,1,0:T(8,128)(2,1)} %broadcast_in_dim.48), calls=%async_computation | async-start | bytes 524288 | tf_op jit(solution)/shard_map/all_to_all | solution.py:165
  14.7 2.8 collective-permute-done.1
  17.7 3.2 %all-to-all-done = bf16[16,2,32,128]{3,2,1,0:T(8,128)(2,1)S(1)} async-done(((bf16[16,2,32,128]{3,2,1,0:T(8,128)(2,1)}), bf16[16,2,32,128]{3,2,1,0:T(8,128)(2,1)S(1)}, u32[]{:S(2)}, u32[]{:S(2)}) %all-to-all-start) | async-done | bytes 262176 | tf_op jit(solution)/shard_map/all_to_all | solution.py:165
  22.8 4.0 %collective-permute-start.6 = (bf16[2,32,128]{2,1,0:T(8,128)(2,1)S(1)}, bf16[2,32,128]{2,1,0:T(8,128)(2,1)S(1)}, u32[]{:S(2)}, u32[]{:S(2)}) collective-permute-start(bf16[2,32,128]{2,1,0:T(8,128)(2,1)S(1)} %get-tuple-element.355), channel_id=1, source_target_pairs={{0,2},{1,5},{2,0},{3,7},{4,6},{5,1},{6,4},{7,3},{8,10},{9,13},{10,... | collective-permute-start | bytes 49160 | tf_op jit(solution)/shard_map/ppermute | solution.py:141
  33.9 12.2 %all_to_all.70 = bf16[16,2,32,128]{3,2,1,0:T(8,128)(2,1)S(1)} all-to-all(bf16[16,2,32,128]{3,2,1,0:T(8,128)(2,1)S(1)} %broadcast_in_dim.49), channel_id=1, replica_groups={{1,9,17,25,33,41,49,57,65,73,81,89,97,105,113,121},{3,11,19,27,35,43,51..., dimensions={0} | all-to-all | bytes 524288 | tf_op jit(solution)/shard_map/all_to_all | solution.py:165
  48.5 2.4 collective-permute-start.10
  54.2 12.0 %all_to_all.71 = bf16[16,2,32,128]{3,2,1,0:T(8,128)(2,1)S(1)} all-to-all(bf16[16,2,32,128]{3,2,1,0:T(8,128)(2,1)S(1)} %broadcast_in_dim.50), channel_id=1, replica_groups={{1,9,17,25,33,41,49,57,65,73,81,89,97,105,113,121},{3,11,19,27,35,43,51..., dimensions={0} | all-to-all | bytes 524288 | tf_op jit(solution)/shard_map/all_to_all | solution.py:165
  73.8 11.0 %all_to_all.72 = bf16[16,2,32,128]{3,2,1,0:T(8,128)(2,1)S(1)} all-to-all(bf16[16,2,32,128]{3,2,1,0:T(8,128)(2,1)S(1)} %broadcast_in_dim.51), channel_id=1, replica_groups={{1,9,17,25,33,41,49,57,65,73,81,89,97,105,113,121},{3,11,19,27,35,43,51..., dimensions={0} | all-to-all | bytes 524288 | tf_op jit(solution)/shard_map/all_to_all | solution.py:165
  86.2 2.5 collective-permute-start.15
  93.0 11.0 %all_to_all.73 = bf16[16,2,32,128]{3,2,1,0:T(8,128)(2,1)S(1)} all-to-all(bf16[16,2,32,128]{3,2,1,0:T(8,128)(2,1)S(1)} %broadcast_in_dim.52), channel_id=1, replica_groups={{1,9,17,25,33,41,49,57,65,73,81,89,97,105,113,121},{3,11,19,27,35,43,51..., dimensions={0} | all-to-all | bytes 524288 | tf_op jit(solution)/shard_map/all_to_all | solution.py:165
  105.4 2.5 collective-permute-start.18
  112.3 11.3 %all_to_all.74 = bf16[16,2,32,128]{3,2,1,0:T(8,128)(2,1)S(1)} all-to-all(bf16[16,2,32,128]{3,2,1,0:T(8,128)(2,1)S(1)} %broadcast_in_dim.53), channel_id=1, replica_groups={{1,9,17,25,33,41,49,57,65,73,81,89,97,105,113,121},{3,11,19,27,35,43,51..., dimensions={0} | all-to-all | bytes 524288 | tf_op jit(solution)/shard_map/all_to_all | solution.py:165
  125.0 2.6 collective-permute-start.23
  132.0 11.2 %all_to_all.75 = bf16[16,2,32,128]{3,2,1,0:T(8,128)(2,1)S(1)} all-to-all(bf16[16,2,32,128]{3,2,1,0:T(8,128)(2,1)S(1)} %broadcast_in_dim.54), channel_id=1, replica_groups={{1,9,17,25,33,41,49,57,65,73,81,89,97,105,113,121},{3,11,19,27,35,43,51..., dimensions={0} | all-to-all | bytes 524288 | tf_op jit(solution)/shard_map/all_to_all | solution.py:165
  144.6 2.5 collective-permute-start.26
  151.9 11.0 %all_to_all.76 = bf16[16,2,32,128]{3,2,1,0:T(8,128)(2,1)S(1)} all-to-all(bf16[16,2,32,128]{3,2,1,0:T(8,128)(2,1)S(1)} %broadcast_in_dim.55), channel_id=1, replica_groups={{1,9,17,25,33,41,49,57,65,73,81,89,97,105,113,121},{3,11,19,27,35,43,51..., dimensions={0} | all-to-all | bytes 524288 | tf_op jit(solution)/shard_map/all_to_all | solution.py:165
  164.3 2.5 collective-permute-start.29
  171.2 11.0 %all_to_all.77 = bf16[16,2,32,128]{3,2,1,0:T(8,128)(2,1)S(1)} all-to-all(bf16[16,2,32,128]{3,2,1,0:T(8,128)(2,1)S(1)} %broadcast_in_dim.56), channel_id=1, replica_groups={{1,9,17,25,33,41,49,57,65,73,81,89,97,105,113,121},{3,11,19,27,35,43,51..., dimensions={0} | all-to-all | bytes 524288 | tf_op jit(solution)/shard_map/all_to_all | solution.py:165
  183.5 2.4 collective-permute-start.32
  190.3 11.0 %all_to_all.78 = bf16[16,2,32,128]{3,2,1,0:T(8,128)(2,1)S(1)} all-to-all(bf16[16,2,32,128]{3,2,1,0:T(8,128)(2,1)S(1)} %broadcast_in_dim.57), channel_id=1, replica_groups={{1,9,17,25,33,41,49,57,65,73,81,89,97,105,113,121},{3,11,19,27,35,43,51..., dimensions={0} | all-to-all | bytes 524288 | tf_op jit(solution)/shard_map/all_to_all | solution.py:165
  209.4 10.9 %all_to_all.79 = bf16[16,2,32,128]{3,2,1,0:T(8,128)(2,1)S(1)} all-to-all(bf16[16,2,32,128]{3,2,1,0:T(8,128)(2,1)S(1)} %broadcast_in_dim.58), channel_id=1, replica_groups={{1,9,17,25,33,41,49,57,65,73,81,89,97,105,113,121},{3,11,19,27,35,43,51..., dimensions={0} | all-to-all | bytes 524288 | tf_op jit(solution)/shard_map/all_to_all | solution.py:165
  228.2 11.1 %all_to_all.80 = bf16[16,2,32,128]{3,2,1,0:T(8,128)(2,1)S(1)} all-to-all(bf16[16,2,32,128]{3,2,1,0:T(8,128)(2,1)S(1)} %broadcast_in_dim.59), channel_id=1, replica_groups={{1,9,17,25,33,41,49,57,65,73,81,89,97,105,113,121},{3,11,19,27,35,43,51..., dimensions={0} | all-to-all | bytes 524288 | tf_op jit(solution)/shard_map/all_to_all | solution.py:165
  247.1 11.0 %all_to_all.81 = bf16[16,2,32,128]{3,2,1,0:T(8,128)(2,1)S(1)} all-to-all(bf16[16,2,32,128]{3,2,1,0:T(8,128)(2,1)S(1)} %broadcast_in_dim.60), channel_id=1, replica_groups={{1,9,17,25,33,41,49,57,65,73,81,89,97,105,113,121},{3,11,19,27,35,43,51..., dimensions={0} | all-to-all | bytes 524288 | tf_op jit(solution)/shard_map/all_to_all | solution.py:165
  265.9 11.1 %all_to_all.82 = bf16[16,2,32,128]{3,2,1,0:T(8,128)(2,1)S(1)} all-to-all(bf16[16,2,32,128]{3,2,1,0:T(8,128)(2,1)S(1)} %broadcast_in_dim.61), channel_id=1, replica_groups={{1,9,17,25,33,41,49,57,65,73,81,89,97,105,113,121},{3,11,19,27,35,43,51..., dimensions={0} | all-to-all | bytes 524288 | tf_op jit(solution)/shard_map/all_to_all | solution.py:165
  (330 shorter events, 109.0 us)
Async XLA Ops:
  4.6 26.0 %collective-permute-start.5 = (bf16[7,8,4,128,128]{4,3,2,1,0:T(8,128)(2,1)}, bf16[7,8,4,128,128]{4,3,2,1,0:T(8,128)(2,1)}, u32[]{:S(2)}, u32[]{:S(2)}) collective-permute-start(bf16[7,8,4,128,128]{4,3,2,1,0:T(8,128)(2,1)} %bitcast.271), channel_id=1, source_target_pairs={{0,1},{1,0},{2,3},{3,2},{4,5},{5,4},{6,7},{7,6},{8,9},{9,8},{10,11... | collective-permute-start | bytes 22020104 | tf_op jit(solution)/shard_map/ppermute | solution.py:133
  5.2 16.3 %collective-permute-start.2 = (bf16[8,4,128,128]{3,2,1,0:T(8,128)(2,1)S(1)}, bf16[8,4,128,128]{3,2,1,0:T(8,128)(2,1)S(1)}, u32[]{:S(2)}, u32[]{:S(2)}) collective-permute-start(bf16[8,4,128,128]{3,2,1,0:T(8,128)(2,1)S(1)} %slice_bitcast_fusion.odd_ref), channel_id=1, source_target_pairs={{0,1},{1,0},{2,3},{3,2},{4,5},{5,4},{6,7},{7,6},{8,9},{9,8},{10,11... | collective-permute-start | bytes 3145736 | tf_op jit(solution)/shard_map/ppermute | solution.py:133
  5.8 11.7 %collective-permute-start.1 = (s32[448]{0:T(512)S(1)}, s32[448]{0:T(512)S(1)}, u32[]{:S(2)}, u32[]{:S(2)}) collective-permute-start(s32[448]{0:T(512)S(1)} %pad_add_fusion), channel_id=1, source_target_pairs={{0,1},{1,0},{2,3},{3,2},{4,5},{5,4},{6,7},{7,6},{8,9},{9,8},{10,11... | collective-permute-start | bytes 5384 | tf_op jit(solution)/shard_map/ppermute | solution.py:133
  6.7 14.2 %all-to-all-start = ((bf16[16,2,32,128]{3,2,1,0:T(8,128)(2,1)}), bf16[16,2,32,128]{3,2,1,0:T(8,128)(2,1)S(1)}, u32[]{:S(2)}, u32[]{:S(2)}) async-start(bf16[16,2,32,128]{3,2,1,0:T(8,128)(2,1)} %broadcast_in_dim.48), calls=%async_computation | async-start | bytes 524288 | tf_op jit(solution)/shard_map/all_to_all | solution.py:165
  13.5 17.1 %collective-permute-start.3 = (f32[8,128,128]{2,1,0:T(8,128)S(1)}, f32[8,128,128]{2,1,0:T(8,128)S(1)}, u32[]{:S(2)}, u32[]{:S(2)}) collective-permute-start(f32[8,128,128]{2,1,0:T(8,128)S(1)} %bitcast.294), channel_id=1, source_target_pairs={{0,1},{1,0},{2,3},{3,2},{4,5},{5,4},{6,7},{7,6},{8,9},{9,8},{10,11... | collective-permute-start | bytes 1572872 | tf_op jit(solution)/shard_map/ppermute | solution.py:133
  22.8 5.1 %collective-permute-start.6 = (bf16[2,32,128]{2,1,0:T(8,128)(2,1)S(1)}, bf16[2,32,128]{2,1,0:T(8,128)(2,1)S(1)}, u32[]{:S(2)}, u32[]{:S(2)}) collective-permute-start(bf16[2,32,128]{2,1,0:T(8,128)(2,1)S(1)} %get-tuple-element.355), channel_id=1, source_target_pairs={{0,2},{1,5},{2,0},{3,7},{4,6},{5,1},{6,4},{7,3},{8,10},{9,13},{10,... | collective-permute-start | bytes 49160 | tf_op jit(solution)/shard_map/ppermute | solution.py:141
  26.8 3.8 %collective-permute-start.7 = (bf16[2,32,128]{2,1,0:T(8,128)(2,1)S(1)}, bf16[2,32,128]{2,1,0:T(8,128)(2,1)S(1)}, u32[]{:S(2)}, u32[]{:S(2)}) collective-permute-start(bf16[2,32,128]{2,1,0:T(8,128)(2,1)S(1)} %get-tuple-element.356), channel_id=1, source_target_pairs={{0,2},{1,7},{2,0},{3,5},{4,6},{5,3},{6,4},{7,1},{8,10},{9,15},{10,... | collective-permute-start | bytes 49160 | tf_op jit(solution)/shard_map/ppermute | solution.py:141
  47.4 5.5 %collective-permute-start.9 = (bf16[2,32,128]{2,1,0:T(8,128)(2,1)S(1)}, bf16[2,32,128]{2,1,0:T(8,128)(2,1)S(1)}, u32[]{:S(2)}, u32[]{:S(2)}) collective-permute-start(bf16[2,32,128]{2,1,0:T(8,128)(2,1)S(1)} %get-tuple-element.367), channel_id=1, source_target_pairs={{0,2},{1,5},{2,0},{3,7},{4,6},{5,1},{6,4},{7,3},{8,10},{9,13},{10,... | collective-permute-start | bytes 49160 | tf_op jit(solution)/shard_map/ppermute | solution.py:141
  48.5 4.4 %collective-permute-start.10 = (bf16[2,32,128]{2,1,0:T(8,128)(2,1)S(1)}, bf16[2,32,128]{2,1,0:T(8,128)(2,1)S(1)}, u32[]{:S(2)}, u32[]{:S(2)}) collective-permute-start(bf16[2,32,128]{2,1,0:T(8,128)(2,1)S(1)} %get-tuple-element.368), channel_id=1, source_target_pairs={{0,2},{1,7},{2,0},{3,5},{4,6},{5,3},{6,4},{7,1},{8,10},{9,15},{10,... | collective-permute-start | bytes 49160 | tf_op jit(solution)/shard_map/ppermute | solution.py:141
  54.0 58.2 %collective-permute-start.21 = (bf16[7,8,4,128,128]{4,3,2,1,0:T(8,128)(2,1)S(1)}, bf16[7,8,4,128,128]{4,3,2,1,0:T(8,128)(2,1)S(1)}, u32[]{:S(2)}, u32[]{:S(2)}) collective-permute-start(bf16[7,8,4,128,128]{4,3,2,1,0:T(8,128)(2,1)S(1)} %bitcast.269), channel_id=1, source_target_pairs={{0,1},{1,0},{2,3},{3,2},{4,5},{5,4},{6,7},{7,6},{8,9},{9,8},{10,11... | collective-permute-start | bytes 22020104 | tf_op jit(solution)/shard_map/ppermute | solution.py:133
  67.6 4.9 %collective-permute-start.12 = (bf16[2,32,128]{2,1,0:T(8,128)(2,1)S(1)}, bf16[2,32,128]{2,1,0:T(8,128)(2,1)S(1)}, u32[]{:S(2)}, u32[]{:S(2)}) collective-permute-start(bf16[2,32,128]{2,1,0:T(8,128)(2,1)S(1)} %get-tuple-element.383), channel_id=1, source_target_pairs={{0,2},{1,5},{2,0},{3,7},{4,6},{5,1},{6,4},{7,3},{8,10},{9,13},{10,... | collective-permute-start | bytes 49160 | tf_op jit(solution)/shard_map/ppermute | solution.py:141
  69.2 3.8 %collective-permute-start.13 = (bf16[2,32,128]{2,1,0:T(8,128)(2,1)S(1)}, bf16[2,32,128]{2,1,0:T(8,128)(2,1)S(1)}, u32[]{:S(2)}, u32[]{:S(2)}) collective-permute-start(bf16[2,32,128]{2,1,0:T(8,128)(2,1)S(1)} %get-tuple-element.384), channel_id=1, source_target_pairs={{0,2},{1,7},{2,0},{3,5},{4,6},{5,3},{6,4},{7,1},{8,10},{9,15},{10,... | collective-permute-start | bytes 49160 | tf_op jit(solution)/shard_map/ppermute | solution.py:141
  86.2 5.2 %collective-permute-start.15 = (bf16[2,32,128]{2,1,0:T(8,128)(2,1)S(1)}, bf16[2,32,128]{2,1,0:T(8,128)(2,1)S(1)}, u32[]{:S(2)}, u32[]{:S(2)}) collective-permute-start(bf16[2,32,128]{2,1,0:T(8,128)(2,1)S(1)} %get-tuple-element.395), channel_id=1, source_target_pairs={{0,2},{1,5},{2,0},{3,7},{4,6},{5,1},{6,4},{7,3},{8,10},{9,13},{10,... | collective-permute-start | bytes 49160 | tf_op jit(solution)/shard_map/ppermute | solution.py:141
  88.7 3.8 %collective-permute-start.16 = (bf16[2,32,128]{2,1,0:T(8,128)(2,1)S(1)}, bf16[2,32,128]{2,1,0:T(8,128)(2,1)S(1)}, u32[]{:S(2)}, u32[]{:S(2)}) collective-permute-start(bf16[2,32,128]{2,1,0:T(8,128)(2,1)S(1)} %get-tuple-element.396), channel_id=1, source_target_pairs={{0,2},{1,7},{2,0},{3,5},{4,6},{5,3},{6,4},{7,1},{8,10},{9,15},{10,... | collective-permute-start | bytes 49160 | tf_op jit(solution)/shard_map/ppermute | solution.py:141
  105.4 5.3 %collective-permute-start.18 = (bf16[2,32,128]{2,1,0:T(8,128)(2,1)S(1)}, bf16[2,32,128]{2,1,0:T(8,128)(2,1)S(1)}, u32[]{:S(2)}, u32[]{:S(2)}) collective-permute-start(bf16[2,32,128]{2,1,0:T(8,128)(2,1)S(1)} %get-tuple-element.407), channel_id=1, source_target_pairs={{0,2},{1,5},{2,0},{3,7},{4,6},{5,1},{6,4},{7,3},{8,10},{9,13},{10,... | collective-permute-start | bytes 49160 | tf_op jit(solution)/shard_map/ppermute | solution.py:141
  125.0 5.5 %collective-permute-start.23 = (bf16[2,32,128]{2,1,0:T(8,128)(2,1)S(1)}, bf16[2,32,128]{2,1,0:T(8,128)(2,1)S(1)}, u32[]{:S(2)}, u32[]{:S(2)}) collective-permute-start(bf16[2,32,128]{2,1,0:T(8,128)(2,1)S(1)} %get-tuple-element.423), channel_id=1, source_target_pairs={{0,2},{1,5},{2,0},{3,7},{4,6},{5,1},{6,4},{7,3},{8,10},{9,13},{10,... | collective-permute-start | bytes 49160 | tf_op jit(solution)/shard_map/ppermute | solution.py:141
  144.6 5.2 %collective-permute-start.26 = (bf16[2,32,128]{2,1,0:T(8,128)(2,1)S(1)}, bf16[2,32,128]{2,1,0:T(8,128)(2,1)S(1)}, u32[]{:S(2)}, u32[]{:S(2)}) collective-permute-start(bf16[2,32,128]{2,1,0:T(8,128)(2,1)S(1)} %get-tuple-element.437), channel_id=1, source_target_pairs={{0,2},{1,5},{2,0},{3,7},{4,6},{5,1},{6,4},{7,3},{8,10},{9,13},{10,... | collective-permute-start | bytes 49160 | tf_op jit(solution)/shard_map/ppermute | solution.py:141
  164.3 5.2 %collective-permute-start.29 = (bf16[2,32,128]{2,1,0:T(8,128)(2,1)S(1)}, bf16[2,32,128]{2,1,0:T(8,128)(2,1)S(1)}, u32[]{:S(2)}, u32[]{:S(2)}) collective-permute-start(bf16[2,32,128]{2,1,0:T(8,128)(2,1)S(1)} %get-tuple-element.453), channel_id=1, source_target_pairs={{0,2},{1,5},{2,0},{3,7},{4,6},{5,1},{6,4},{7,3},{8,10},{9,13},{10,... | collective-permute-start | bytes 49160 | tf_op jit(solution)/shard_map/ppermute | solution.py:141
  183.5 5.1 %collective-permute-start.32 = (bf16[2,32,128]{2,1,0:T(8,128)(2,1)S(1)}, bf16[2,32,128]{2,1,0:T(8,128)(2,1)S(1)}, u32[]{:S(2)}, u32[]{:S(2)}) collective-permute-start(bf16[2,32,128]{2,1,0:T(8,128)(2,1)S(1)} %get-tuple-element.463), channel_id=1, source_target_pairs={{0,2},{1,5},{2,0},{3,7},{4,6},{5,1},{6,4},{7,3},{8,10},{9,13},{10,... | collective-permute-start | bytes 49160 | tf_op jit(solution)/shard_map/ppermute | solution.py:141
  202.6 4.9 %collective-permute-start.35 = (bf16[2,32,128]{2,1,0:T(8,128)(2,1)S(1)}, bf16[2,32,128]{2,1,0:T(8,128)(2,1)S(1)}, u32[]{:S(2)}, u32[]{:S(2)}) collective-permute-start(bf16[2,32,128]{2,1,0:T(8,128)(2,1)S(1)} %get-tuple-element.473), channel_id=1, source_target_pairs={{0,2},{1,5},{2,0},{3,7},{4,6},{5,1},{6,4},{7,3},{8,10},{9,13},{10,... | collective-permute-start | bytes 49160 | tf_op jit(solution)/shard_map/ppermute | solution.py:141
  221.7 4.8 %collective-permute-start.38 = (bf16[2,32,128]{2,1,0:T(8,128)(2,1)S(1)}, bf16[2,32,128]{2,1,0:T(8,128)(2,1)S(1)}, u32[]{:S(2)}, u32[]{:S(2)}) collective-permute-start(bf16[2,32,128]{2,1,0:T(8,128)(2,1)S(1)} %get-tuple-element.483), channel_id=1, source_target_pairs={{0,2},{1,5},{2,0},{3,7},{4,6},{5,1},{6,4},{7,3},{8,10},{9,13},{10,... | collective-permute-start | bytes 49160 | tf_op jit(solution)/shard_map/ppermute | solution.py:141
  240.6 4.7 %collective-permute-start.41 = (bf16[2,32,128]{2,1,0:T(8,128)(2,1)S(1)}, bf16[2,32,128]{2,1,0:T(8,128)(2,1)S(1)}, u32[]{:S(2)}, u32[]{:S(2)}) collective-permute-start(bf16[2,32,128]{2,1,0:T(8,128)(2,1)S(1)} %get-tuple-element.493), channel_id=1, source_target_pairs={{0,2},{1,5},{2,0},{3,7},{4,6},{5,1},{6,4},{7,3},{8,10},{9,13},{10,... | collective-permute-start | bytes 49160 | tf_op jit(solution)/shard_map/ppermute | solution.py:141
  259.4 5.0 %collective-permute-start.44 = (bf16[2,32,128]{2,1,0:T(8,128)(2,1)S(1)}, bf16[2,32,128]{2,1,0:T(8,128)(2,1)S(1)}, u32[]{:S(2)}, u32[]{:S(2)}) collective-permute-start(bf16[2,32,128]{2,1,0:T(8,128)(2,1)S(1)} %get-tuple-element.503), channel_id=1, source_target_pairs={{0,2},{1,5},{2,0},{3,7},{4,6},{5,1},{6,4},{7,3},{8,10},{9,13},{10,... | collective-permute-start | bytes 49160 | tf_op jit(solution)/shard_map/ppermute | solution.py:141
  278.4 4.2 %collective-permute-start.47 = (bf16[2,32,128]{2,1,0:T(8,128)(2,1)S(1)}, bf16[2,32,128]{2,1,0:T(8,128)(2,1)S(1)}, u32[]{:S(2)}, u32[]{:S(2)}) collective-permute-start(bf16[2,32,128]{2,1,0:T(8,128)(2,1)S(1)} %get-tuple-element.513), channel_id=1, source_target_pairs={{0,2},{1,5},{2,0},{3,7},{4,6},{5,1},{6,4},{7,3},{8,10},{9,13},{10,... | collective-permute-start | bytes 49160 | tf_op jit(solution)/shard_map/ppermute | solution.py:141
  (69 other events, 2554.0 us)

commit v5 on v4

--- a/solution.py
+++ b/solution.py
@@ -89,39 +89,64 @@
 def stage(after, following):
     arrays, places = zip(*following)
     vmem = pl.BlockSpec(memory_space=pltpu.VMEM)
-    hbm = pl.BlockSpec(memory_space=pltpu.HBM)
+    anywhere = pl.BlockSpec(memory_space=pl.ANY)
     out_shape = [jax.ShapeDtypeStruct(array.shape[1:], array.dtype) for array in arrays]
     pieces = sum(array.shape[1] if array.ndim == 5 else 1 for array in arrays)
     return pl.pallas_call(
         functools.partial(stage_kernel, places),
         out_shape=out_shape,
-        in_specs=[vmem] + [hbm] * len(arrays),
+        in_specs=[vmem] + [anywhere] * len(arrays),
         out_specs=[vmem] * len(out_shape),
         scratch_shapes=[pltpu.SemaphoreType.DMA((pieces,))],
         compiler_params=pltpu.CompilerParams(vmem_limit_bytes=SLIM * 2**20),
         cost_estimate=pl.CostEstimate(flops=0, bytes_accessed=3 * 2**20, transcendentals=0),
-    )(after, *[in_hbm(array) for array in arrays])
-
-
-def stack_kernel(*refs):
+    )(after, *[in_hbm(array) if array.size > 2**18 else array for array in arrays])
+
+
+def stack_kernel(_, *refs):
     values, (even_ref, odd_ref) = refs[:-2], refs[-2:]
-    turns, tiers = even_ref.shape[:2]
-    for i in range(turns):
-        for j in range(tiers):
-            even_ref[i, j] = values[2 * (i * tiers + j)][...]
-            odd_ref[i, j] = values[2 * (i * tiers + j) + 1][...]
-
-
-def stack_levels(*turns):
-    values = [value for levels in turns for pair in levels for value in pair]
-    shape = jax.ShapeDtypeStruct((len(turns), len(turns[0])) + values[0].shape, values[0].dtype)
+    for i in range(even_ref.shape[0]):
+        even_ref[i] = values[2 * i][...]
+        odd_ref[i] = values[2 * i + 1][...]
+
+
+def stack_levels(after, levels):
+    values = [value for pair in levels for value in pair]
+    shape = jax.ShapeDtypeStruct((len(levels),) + values[0].shape, values[0].dtype)
     vmem = pl.BlockSpec(memory_space=pltpu.VMEM)
     return pl.pallas_call(
         stack_kernel,
         out_shape=[shape, shape],
-        in_specs=[vmem] * len(values),
+        in_specs=[vmem] * (1 + len(values)),
         out_specs=[vmem, vmem],
-    )(*values)
+        compiler_params=pltpu.CompilerParams(vmem_limit_bytes=4 * 2**20),
+        cost_estimate=pl.CostEstimate(flops=0, bytes_accessed=2**20, transcendentals=0),
+    )(after, *values)
+
+
+def finish_kernel(first, odd_core_ref, even_ref, odd_ref, *refs):
+    out_ref = refs[-1]
+    tail = out_ref.shape[0] if len(refs) == 1 else out_ref.shape[0] - 1
+
+    def write(kept_ref, last_ref):
+        out_ref[out_ref.shape[0] - tail :] = kept_ref[first : first + tail]
+        if last_ref is not None:
+            out_ref[0] = last_ref[...]
+
+    last_even, last_odd = refs[:2] if len(refs) == 3 else (None, None)
+    pl.when(odd_core_ref[0] == 1)(lambda: write(odd_ref, last_odd))
+    pl.when(odd_core_ref[0] == 0)(lambda: write(even_ref, last_even))
+
+
+def finish(odd_core, evens, odds, first, tiers, last=()):
+    vmem = pl.BlockSpec(memory_space=pltpu.VMEM)
+    return pl.pallas_call(
+        functools.partial(finish_kernel, first),
+        out_shape=jax.ShapeDtypeStruct((tiers,) + odds.shape[1:], odds.dtype),
+        in_specs=[pl.BlockSpec(memory_space=pltpu.SMEM)] + [vmem] * (2 + len(last)),
+        out_specs=vmem,
+        compiler_params=pltpu.CompilerParams(vmem_limit_bytes=4 * 2**20),
+    )(odd_core, evens, odds, *last)
 
 
 def in_hbm(value):
@@ -240,9 +265,15 @@
             following = [(high_inv_even, tier), (high_inv_odd, tier)]
             if tier > 0:
                 following += [(high_even, tier - 1), (high_odd, tier - 1)]
+            else:
+                following += [(even[None], 0), (odd[None], 0)]
             parts = level_terms(high_index, history, blocks, tier)
             kept = stage(parts[0], following)
             top_inv, blocks = kept[:2], kept[2:]
+            if tier == 0:
+                even, odd = kept[2:]
+                evens, odds = stack_levels(kept[0], forward + backward[1:])
+                evens = swap_cores(evens)
             sums = reduce_rows(parts)
             even, odd = even - sums[0], odd - sums[1]
         even = apply_inverse(top_inv[0], even)
@@ -253,10 +284,12 @@
             history = history.at[tier * col_count : (tier + 1) * col_count].set(
                 share_solved(even, odd)
             )
-    evens, odds = stack_levels(forward, backward)
-    evens = swap_cores(evens)
-    outs = [jnp.where(is_odd, odds[i], evens[i]) for i in range(2)]
-    return outs[0][:, None], outs[1][:, None]
+    last_even, last_odd = backward[0]
+    forward_out = finish(here[1:], evens, odds, 0, tiers)
+    backward_out = finish(
+        here[1:], evens, odds, tiers, tiers, (swap_cores(last_even), last_odd)
+    )
+    return forward_out[:, None], backward_out[:, None]
 
 
 def solution(mesh):

time: 293 us -> 287 us (0.980)
    ppermute x9 -> x10, waiting for transfers between devices: 4.28 us -> 0.53 us  [swap_cores(): return lax.ppermute(value, 'row', [(i, i ^ 1) for i in range(count)])]
  transfers between devices with their start and end apart: 52 -> 53, of which waited for: 21 -> 21; matrix products, arithmetic and copies ran while one was open for 2% -> 2% of each run, Pallas kernels for 10% -> 10%
where the time goes in v5:
time: 287 us; the launch traced here: 286 us
  blocking collectives  146 us (51%)
  starting transfers between devices  59.7 us (21%)
  Pallas kernels  45.2 us (16%)
  waiting for transfers between devices  20.4 us (7%)
  matrix products  7.26 us (3%)
  local copies, waits for them, and re-layouts  4.21 us (1%)
    all_to_all x13, blocking collectives, share_solved(): lax.all_to_all(copies, AXES, 0, 0, tiled=True, axis_index_groups=gather_g...  146 us
    ppermute x42, starting transfers between devices, reduce_rows(): total = total + lax.ppermute(parts[step], 'row', pairs).astype(jnp.float32)  48.5 us
    pallas_call x14, Pallas kernels, stage(): pl.pallas_call(functools.partial(stage_kernel, places), out_shape=out_sha...  25.6 us
    pallas_call x14, Pallas kernels, level_terms(): pl.pallas_call(functools.partial(product_kernel, level), out_shape=out_sh...  18.2 us
    ppermute x42, waiting for transfers between devices, reduce_rows(): total = total + lax.ppermute(parts[step], 'row', pairs).astype(jnp.float32)  13.8 us
    dot_general x31, matrix products, apply_inverse(): jnp.einsum('xi,oi->xo', vectors, inverse, precision=lax.Precision.HIGHEST)  7.26 us
    all_to_all x1, starting transfers between devices, share_solved(): lax.all_to_all(copies, AXES, 0, 0, tiled=True, axis_index_groups=gather_g...  6.84 us
    all_to_all x1, waiting for transfers between devices, share_solved(): lax.all_to_all(copies, AXES, 0, 0, tiled=True, axis_index_groups=gather_g...  6.1 us
  transfers between devices with their start and end apart: 53, of which 21 were waited for; matrix products, arithmetic and copies ran while one was open for 2% of the time, Pallas kernels for 10%

profile of v5, /device:TPU:1, one launch (start us, length us, event | category | flops | bytes accessed | tf_op | source)
XLA Modules:
  0.0 285.7 jit_solution(9085640256648027574)
XLA Ops:
  6.6 6.8 %all-to-all-start = ((bf16[16,2,32,128]{3,2,1,0:T(8,128)(2,1)}), bf16[16,2,32,128]{3,2,1,0:T(8,128)(2,1)S(1)}, u32[]{:S(2)}, u32[]{:S(2)}) async-start(bf16[16,2,32,128]{3,2,1,0:T(8,128)(2,1)} %broadcast_in_dim.54), calls=%async_computation | async-start | bytes 524288 | tf_op jit(solution)/shard_map/all_to_all | solution.py:190
  14.7 6.1 %all-to-all-done = bf16[16,2,32,128]{3,2,1,0:T(8,128)(2,1)S(1)} async-done(((bf16[16,2,32,128]{3,2,1,0:T(8,128)(2,1)}), bf16[16,2,32,128]{3,2,1,0:T(8,128)(2,1)S(1)}, u32[]{:S(2)}, u32[]{:S(2)}) %all-to-all-start) | async-done | bytes 262176 | tf_op jit(solution)/shard_map/all_to_all | solution.py:190
  22.7 4.0 %collective-permute-start.6 = (bf16[2,32,128]{2,1,0:T(8,128)(2,1)S(1)}, bf16[2,32,128]{2,1,0:T(8,128)(2,1)S(1)}, u32[]{:S(2)}, u32[]{:S(2)}) collective-permute-start(bf16[2,32,128]{2,1,0:T(8,128)(2,1)S(1)} %get-tuple-element.358), channel_id=1, source_target_pairs={{0,2},{1,5},{2,0},{3,7},{4,6},{5,1},{6,4},{7,3},{8,10},{9,13},{10,... | collective-permute-start | bytes 49160 | tf_op jit(solution)/shard_map/ppermute | solution.py:166
  33.2 12.1 %all_to_all.70 = bf16[16,2,32,128]{3,2,1,0:T(8,128)(2,1)S(1)} all-to-all(bf16[16,2,32,128]{3,2,1,0:T(8,128)(2,1)S(1)} %broadcast_in_dim.55), channel_id=1, replica_groups={{1,9,17,25,33,41,49,57,65,73,81,89,97,105,113,121},{3,11,19,27,35,43,51..., dimensions={0} | all-to-all | bytes 524288 | tf_op jit(solution)/shard_map/all_to_all | solution.py:190
  47.7 2.4 collective-permute-start.10
  53.4 12.0 %all_to_all.71 = bf16[16,2,32,128]{3,2,1,0:T(8,128)(2,1)S(1)} all-to-all(bf16[16,2,32,128]{3,2,1,0:T(8,128)(2,1)S(1)} %broadcast_in_dim.56), channel_id=1, replica_groups={{1,9,17,25,33,41,49,57,65,73,81,89,97,105,113,121},{3,11,19,27,35,43,51..., dimensions={0} | all-to-all | bytes 524288 | tf_op jit(solution)/shard_map/all_to_all | solution.py:190
  73.1 10.8 %all_to_all.72 = bf16[16,2,32,128]{3,2,1,0:T(8,128)(2,1)S(1)} all-to-all(bf16[16,2,32,128]{3,2,1,0:T(8,128)(2,1)S(1)} %broadcast_in_dim.57), channel_id=1, replica_groups={{1,9,17,25,33,41,49,57,65,73,81,89,97,105,113,121},{3,11,19,27,35,43,51..., dimensions={0} | all-to-all | bytes 524288 | tf_op jit(solution)/shard_map/all_to_all | solution.py:190
  85.2 2.6 collective-permute-start.15
  92.2 11.0 %all_to_all.73 = bf16[16,2,32,128]{3,2,1,0:T(8,128)(2,1)S(1)} all-to-all(bf16[16,2,32,128]{3,2,1,0:T(8,128)(2,1)S(1)} %broadcast_in_dim.58), channel_id=1, replica_groups={{1,9,17,25,33,41,49,57,65,73,81,89,97,105,113,121},{3,11,19,27,35,43,51..., dimensions={0} | all-to-all | bytes 524288 | tf_op jit(solution)/shard_map/all_to_all | solution.py:190
  104.5 2.4 collective-permute-start.18
  111.3 11.6 %all_to_all.74 = bf16[16,2,32,128]{3,2,1,0:T(8,128)(2,1)S(1)} all-to-all(bf16[16,2,32,128]{3,2,1,0:T(8,128)(2,1)S(1)} %broadcast_in_dim.59), channel_id=1, replica_groups={{1,9,17,25,33,41,49,57,65,73,81,89,97,105,113,121},{3,11,19,27,35,43,51..., dimensions={0} | all-to-all | bytes 524288 | tf_op jit(solution)/shard_map/all_to_all | solution.py:190
  124.2 2.4 collective-permute-start.23
  131.1 11.1 %all_to_all.75 = bf16[16,2,32,128]{3,2,1,0:T(8,128)(2,1)S(1)} all-to-all(bf16[16,2,32,128]{3,2,1,0:T(8,128)(2,1)S(1)} %broadcast_in_dim.60), channel_id=1, replica_groups={{1,9,17,25,33,41,49,57,65,73,81,89,97,105,113,121},{3,11,19,27,35,43,51..., dimensions={0} | all-to-all | bytes 524288 | tf_op jit(solution)/shard_map/all_to_all | solution.py:190
  143.5 2.7 collective-permute-start.26
  151.0 11.0 %all_to_all.76 = bf16[16,2,32,128]{3,2,1,0:T(8,128)(2,1)S(1)} all-to-all(bf16[16,2,32,128]{3,2,1,0:T(8,128)(2,1)S(1)} %broadcast_in_dim.61), channel_id=1, replica_groups={{1,9,17,25,33,41,49,57,65,73,81,89,97,105,113,121},{3,11,19,27,35,43,51..., dimensions={0} | all-to-all | bytes 524288 | tf_op jit(solution)/shard_map/all_to_all | solution.py:190
  163.3 2.5 collective-permute-start.29
  170.1 11.0 %all_to_all.77 = bf16[16,2,32,128]{3,2,1,0:T(8,128)(2,1)S(1)} all-to-all(bf16[16,2,32,128]{3,2,1,0:T(8,128)(2,1)S(1)} %broadcast_in_dim.62), channel_id=1, replica_groups={{1,9,17,25,33,41,49,57,65,73,81,89,97,105,113,121},{3,11,19,27,35,43,51..., dimensions={0} | all-to-all | bytes 524288 | tf_op jit(solution)/shard_map/all_to_all | solution.py:190
  182.4 2.2 collective-permute-start.32
  189.0 11.1 %all_to_all.78 = bf16[16,2,32,128]{3,2,1,0:T(8,128)(2,1)S(1)} all-to-all(bf16[16,2,32,128]{3,2,1,0:T(8,128)(2,1)S(1)} %broadcast_in_dim.63), channel_id=1, replica_groups={{1,9,17,25,33,41,49,57,65,73,81,89,97,105,113,121},{3,11,19,27,35,43,51..., dimensions={0} | all-to-all | bytes 524288 | tf_op jit(solution)/shard_map/all_to_all | solution.py:190
  201.4 2.2 collective-permute-start.35
  207.9 11.2 %all_to_all.79 = bf16[16,2,32,128]{3,2,1,0:T(8,128)(2,1)S(1)} all-to-all(bf16[16,2,32,128]{3,2,1,0:T(8,128)(2,1)S(1)} %broadcast_in_dim.64), channel_id=1, replica_groups={{1,9,17,25,33,41,49,57,65,73,81,89,97,105,113,121},{3,11,19,27,35,43,51..., dimensions={0} | all-to-all | bytes 524288 | tf_op jit(solution)/shard_map/all_to_all | solution.py:190
  227.2 11.0 %all_to_all.80 = bf16[16,2,32,128]{3,2,1,0:T(8,128)(2,1)S(1)} all-to-all(bf16[16,2,32,128]{3,2,1,0:T(8,128)(2,1)S(1)} %broadcast_in_dim.65), channel_id=1, replica_groups={{1,9,17,25,33,41,49,57,65,73,81,89,97,105,113,121},{3,11,19,27,35,43,51..., dimensions={0} | all-to-all | bytes 524288 | tf_op jit(solution)/shard_map/all_to_all | solution.py:190
  245.8 11.3 %all_to_all.81 = bf16[16,2,32,128]{3,2,1,0:T(8,128)(2,1)S(1)} all-to-all(bf16[16,2,32,128]{3,2,1,0:T(8,128)(2,1)S(1)} %broadcast_in_dim.66), channel_id=1, replica_groups={{1,9,17,25,33,41,49,57,65,73,81,89,97,105,113,121},{3,11,19,27,35,43,51..., dimensions={0} | all-to-all | bytes 524288 | tf_op jit(solution)/shard_map/all_to_all | solution.py:190
  264.8 11.1 %all_to_all.82 = bf16[16,2,32,128]{3,2,1,0:T(8,128)(2,1)S(1)} all-to-all(bf16[16,2,32,128]{3,2,1,0:T(8,128)(2,1)S(1)} %broadcast_in_dim.67), channel_id=1, replica_groups={{1,9,17,25,33,41,49,57,65,73,81,89,97,105,113,121},{3,11,19,27,35,43,51..., dimensions={0} | all-to-all | bytes 524288 | tf_op jit(solution)/shard_map/all_to_all | solution.py:190
  (266 shorter events, 101.2 us)
Async XLA Ops:
  4.6 26.0 %collective-permute-start.5 = (bf16[7,8,4,128,128]{4,3,2,1,0:T(8,128)(2,1)}, bf16[7,8,4,128,128]{4,3,2,1,0:T(8,128)(2,1)}, u32[]{:S(2)}, u32[]{:S(2)}) collective-permute-start(bf16[7,8,4,128,128]{4,3,2,1,0:T(8,128)(2,1)} %bitcast.300), channel_id=1, source_target_pairs={{0,1},{1,0},{2,3},{3,2},{4,5},{5,4},{6,7},{7,6},{8,9},{9,8},{10,11... | collective-permute-start | bytes 22020104 | tf_op jit(solution)/shard_map/ppermute | solution.py:158
  4.7 16.7 %collective-permute-start.2 = (bf16[8,4,128,128]{3,2,1,0:T(8,128)(2,1)S(1)}, bf16[8,4,128,128]{3,2,1,0:T(8,128)(2,1)S(1)}, u32[]{:S(2)}, u32[]{:S(2)}) collective-permute-start(bf16[8,4,128,128]{3,2,1,0:T(8,128)(2,1)S(1)} %slice_bitcast_fusion.odd_ref), channel_id=1, source_target_pairs={{0,1},{1,0},{2,3},{3,2},{4,5},{5,4},{6,7},{7,6},{8,9},{9,8},{10,11... | collective-permute-start | bytes 3145736 | tf_op jit(solution)/shard_map/ppermute | solution.py:158
  5.7 8.9 %collective-permute-start = (s32[448]{0:T(512)S(1)}, s32[448]{0:T(512)S(1)}, u32[]{:S(2)}, u32[]{:S(2)}) collective-permute-start(s32[448]{0:T(512)S(1)} %pad_add_fusion), channel_id=1, source_target_pairs={{0,1},{1,0},{2,3},{3,2},{4,5},{5,4},{6,7},{7,6},{8,9},{9,8},{10,11... | collective-permute-start | bytes 5384 | tf_op jit(solution)/shard_map/ppermute | solution.py:158
  6.6 14.2 %all-to-all-start = ((bf16[16,2,32,128]{3,2,1,0:T(8,128)(2,1)}), bf16[16,2,32,128]{3,2,1,0:T(8,128)(2,1)S(1)}, u32[]{:S(2)}, u32[]{:S(2)}) async-start(bf16[16,2,32,128]{3,2,1,0:T(8,128)(2,1)} %broadcast_in_dim.54), calls=%async_computation | async-start | bytes 524288 | tf_op jit(solution)/shard_map/all_to_all | solution.py:190
  13.5 17.1 %collective-permute-start.3 = (f32[8,128,128]{2,1,0:T(8,128)S(1)}, f32[8,128,128]{2,1,0:T(8,128)S(1)}, u32[]{:S(2)}, u32[]{:S(2)}) collective-permute-start(f32[8,128,128]{2,1,0:T(8,128)S(1)} %bitcast.271), channel_id=1, source_target_pairs={{0,1},{1,0},{2,3},{3,2},{4,5},{5,4},{6,7},{7,6},{8,9},{9,8},{10,11... | collective-permute-start | bytes 1572872 | tf_op jit(solution)/shard_map/ppermute | solution.py:158
  22.7 5.2 %collective-permute-start.6 = (bf16[2,32,128]{2,1,0:T(8,128)(2,1)S(1)}, bf16[2,32,128]{2,1,0:T(8,128)(2,1)S(1)}, u32[]{:S(2)}, u32[]{:S(2)}) collective-permute-start(bf16[2,32,128]{2,1,0:T(8,128)(2,1)S(1)} %get-tuple-element.358), channel_id=1, source_target_pairs={{0,2},{1,5},{2,0},{3,7},{4,6},{5,1},{6,4},{7,3},{8,10},{9,13},{10,... | collective-permute-start | bytes 49160 | tf_op jit(solution)/shard_map/ppermute | solution.py:166
  26.8 3.8 %collective-permute-start.7 = (bf16[2,32,128]{2,1,0:T(8,128)(2,1)S(1)}, bf16[2,32,128]{2,1,0:T(8,128)(2,1)S(1)}, u32[]{:S(2)}, u32[]{:S(2)}) collective-permute-start(bf16[2,32,128]{2,1,0:T(8,128)(2,1)S(1)} %get-tuple-element.359), channel_id=1, source_target_pairs={{0,2},{1,7},{2,0},{3,5},{4,6},{5,3},{6,4},{7,1},{8,10},{9,15},{10,... | collective-permute-start | bytes 49160 | tf_op jit(solution)/shard_map/ppermute | solution.py:166
  46.6 5.7 %collective-permute-start.9 = (bf16[2,32,128]{2,1,0:T(8,128)(2,1)S(1)}, bf16[2,32,128]{2,1,0:T(8,128)(2,1)S(1)}, u32[]{:S(2)}, u32[]{:S(2)}) collective-permute-start(bf16[2,32,128]{2,1,0:T(8,128)(2,1)S(1)} %get-tuple-element.370), channel_id=1, source_target_pairs={{0,2},{1,5},{2,0},{3,7},{4,6},{5,1},{6,4},{7,3},{8,10},{9,13},{10,... | collective-permute-start | bytes 49160 | tf_op jit(solution)/shard_map/ppermute | solution.py:166
  47.7 4.6 %collective-permute-start.10 = (bf16[2,32,128]{2,1,0:T(8,128)(2,1)S(1)}, bf16[2,32,128]{2,1,0:T(8,128)(2,1)S(1)}, u32[]{:S(2)}, u32[]{:S(2)}) collective-permute-start(bf16[2,32,128]{2,1,0:T(8,128)(2,1)S(1)} %get-tuple-element.371), channel_id=1, source_target_pairs={{0,2},{1,7},{2,0},{3,5},{4,6},{5,3},{6,4},{7,1},{8,10},{9,15},{10,... | collective-permute-start | bytes 49160 | tf_op jit(solution)/shard_map/ppermute | solution.py:166
  53.3 57.9 %collective-permute-start.21 = (bf16[7,8,4,128,128]{4,3,2,1,0:T(8,128)(2,1)S(1)}, bf16[7,8,4,128,128]{4,3,2,1,0:T(8,128)(2,1)S(1)}, u32[]{:S(2)}, u32[]{:S(2)}) collective-permute-start(bf16[7,8,4,128,128]{4,3,2,1,0:T(8,128)(2,1)S(1)} %bitcast.298), channel_id=1, source_target_pairs={{0,1},{1,0},{2,3},{3,2},{4,5},{5,4},{6,7},{7,6},{8,9},{9,8},{10,11... | collective-permute-start | bytes 22020104 | tf_op jit(solution)/shard_map/ppermute | solution.py:158
  66.8 5.1 %collective-permute-start.12 = (bf16[2,32,128]{2,1,0:T(8,128)(2,1)S(1)}, bf16[2,32,128]{2,1,0:T(8,128)(2,1)S(1)}, u32[]{:S(2)}, u32[]{:S(2)}) collective-permute-start(bf16[2,32,128]{2,1,0:T(8,128)(2,1)S(1)} %get-tuple-element.386), channel_id=1, source_target_pairs={{0,2},{1,5},{2,0},{3,7},{4,6},{5,1},{6,4},{7,3},{8,10},{9,13},{10,... | collective-permute-start | bytes 49160 | tf_op jit(solution)/shard_map/ppermute | solution.py:166
  68.4 3.8 %collective-permute-start.13 = (bf16[2,32,128]{2,1,0:T(8,128)(2,1)S(1)}, bf16[2,32,128]{2,1,0:T(8,128)(2,1)S(1)}, u32[]{:S(2)}, u32[]{:S(2)}) collective-permute-start(bf16[2,32,128]{2,1,0:T(8,128)(2,1)S(1)} %get-tuple-element.387), channel_id=1, source_target_pairs={{0,2},{1,7},{2,0},{3,5},{4,6},{5,3},{6,4},{7,1},{8,10},{9,15},{10,... | collective-permute-start | bytes 49160 | tf_op jit(solution)/shard_map/ppermute | solution.py:166
  85.2 5.4 %collective-permute-start.15 = (bf16[2,32,128]{2,1,0:T(8,128)(2,1)S(1)}, bf16[2,32,128]{2,1,0:T(8,128)(2,1)S(1)}, u32[]{:S(2)}, u32[]{:S(2)}) collective-permute-start(bf16[2,32,128]{2,1,0:T(8,128)(2,1)S(1)} %get-tuple-element.398), channel_id=1, source_target_pairs={{0,2},{1,5},{2,0},{3,7},{4,6},{5,1},{6,4},{7,3},{8,10},{9,13},{10,... | collective-permute-start | bytes 49160 | tf_op jit(solution)/shard_map/ppermute | solution.py:166
  87.8 3.8 %collective-permute-start.16 = (bf16[2,32,128]{2,1,0:T(8,128)(2,1)S(1)}, bf16[2,32,128]{2,1,0:T(8,128)(2,1)S(1)}, u32[]{:S(2)}, u32[]{:S(2)}) collective-permute-start(bf16[2,32,128]{2,1,0:T(8,128)(2,1)S(1)} %get-tuple-element.399), channel_id=1, source_target_pairs={{0,2},{1,7},{2,0},{3,5},{4,6},{5,3},{6,4},{7,1},{8,10},{9,15},{10,... | collective-permute-start | bytes 49160 | tf_op jit(solution)/shard_map/ppermute | solution.py:166
  104.5 5.3 %collective-permute-start.18 = (bf16[2,32,128]{2,1,0:T(8,128)(2,1)S(1)}, bf16[2,32,128]{2,1,0:T(8,128)(2,1)S(1)}, u32[]{:S(2)}, u32[]{:S(2)}) collective-permute-start(bf16[2,32,128]{2,1,0:T(8,128)(2,1)S(1)} %get-tuple-element.410), channel_id=1, source_target_pairs={{0,2},{1,5},{2,0},{3,7},{4,6},{5,1},{6,4},{7,3},{8,10},{9,13},{10,... | collective-permute-start | bytes 49160 | tf_op jit(solution)/shard_map/ppermute | solution.py:166
  124.2 5.6 %collective-permute-start.23 = (bf16[2,32,128]{2,1,0:T(8,128)(2,1)S(1)}, bf16[2,32,128]{2,1,0:T(8,128)(2,1)S(1)}, u32[]{:S(2)}, u32[]{:S(2)}) collective-permute-start(bf16[2,32,128]{2,1,0:T(8,128)(2,1)S(1)} %get-tuple-element.426), channel_id=1, source_target_pairs={{0,2},{1,5},{2,0},{3,7},{4,6},{5,1},{6,4},{7,3},{8,10},{9,13},{10,... | collective-permute-start | bytes 49160 | tf_op jit(solution)/shard_map/ppermute | solution.py:166
  143.5 5.6 %collective-permute-start.26 = (bf16[2,32,128]{2,1,0:T(8,128)(2,1)S(1)}, bf16[2,32,128]{2,1,0:T(8,128)(2,1)S(1)}, u32[]{:S(2)}, u32[]{:S(2)}) collective-permute-start(bf16[2,32,128]{2,1,0:T(8,128)(2,1)S(1)} %get-tuple-element.440), channel_id=1, source_target_pairs={{0,2},{1,5},{2,0},{3,7},{4,6},{5,1},{6,4},{7,3},{8,10},{9,13},{10,... | collective-permute-start | bytes 49160 | tf_op jit(solution)/shard_map/ppermute | solution.py:166
  163.3 5.3 %collective-permute-start.29 = (bf16[2,32,128]{2,1,0:T(8,128)(2,1)S(1)}, bf16[2,32,128]{2,1,0:T(8,128)(2,1)S(1)}, u32[]{:S(2)}, u32[]{:S(2)}) collective-permute-start(bf16[2,32,128]{2,1,0:T(8,128)(2,1)S(1)} %get-tuple-element.455), channel_id=1, source_target_pairs={{0,2},{1,5},{2,0},{3,7},{4,6},{5,1},{6,4},{7,3},{8,10},{9,13},{10,... | collective-permute-start | bytes 49160 | tf_op jit(solution)/shard_map/ppermute | solution.py:166
  182.4 5.0 %collective-permute-start.32 = (bf16[2,32,128]{2,1,0:T(8,128)(2,1)S(1)}, bf16[2,32,128]{2,1,0:T(8,128)(2,1)S(1)}, u32[]{:S(2)}, u32[]{:S(2)}) collective-permute-start(bf16[2,32,128]{2,1,0:T(8,128)(2,1)S(1)} %get-tuple-element.465), channel_id=1, source_target_pairs={{0,2},{1,5},{2,0},{3,7},{4,6},{5,1},{6,4},{7,3},{8,10},{9,13},{10,... | collective-permute-start | bytes 49160 | tf_op jit(solution)/shard_map/ppermute | solution.py:166
  201.4 5.0 %collective-permute-start.35 = (bf16[2,32,128]{2,1,0:T(8,128)(2,1)S(1)}, bf16[2,32,128]{2,1,0:T(8,128)(2,1)S(1)}, u32[]{:S(2)}, u32[]{:S(2)}) collective-permute-start(bf16[2,32,128]{2,1,0:T(8,128)(2,1)S(1)} %get-tuple-element.475), channel_id=1, source_target_pairs={{0,2},{1,5},{2,0},{3,7},{4,6},{5,1},{6,4},{7,3},{8,10},{9,13},{10,... | collective-permute-start | bytes 49160 | tf_op jit(solution)/shard_map/ppermute | solution.py:166
  220.4 5.3 %collective-permute-start.38 = (bf16[2,32,128]{2,1,0:T(8,128)(2,1)S(1)}, bf16[2,32,128]{2,1,0:T(8,128)(2,1)S(1)}, u32[]{:S(2)}, u32[]{:S(2)}) collective-permute-start(bf16[2,32,128]{2,1,0:T(8,128)(2,1)S(1)} %get-tuple-element.485), channel_id=1, source_target_pairs={{0,2},{1,5},{2,0},{3,7},{4,6},{5,1},{6,4},{7,3},{8,10},{9,13},{10,... | collective-permute-start | bytes 49160 | tf_op jit(solution)/shard_map/ppermute | solution.py:166
  239.5 5.1 %collective-permute-start.41 = (bf16[2,32,128]{2,1,0:T(8,128)(2,1)S(1)}, bf16[2,32,128]{2,1,0:T(8,128)(2,1)S(1)}, u32[]{:S(2)}, u32[]{:S(2)}) collective-permute-start(bf16[2,32,128]{2,1,0:T(8,128)(2,1)S(1)} %get-tuple-element.495), channel_id=1, source_target_pairs={{0,2},{1,5},{2,0},{3,7},{4,6},{5,1},{6,4},{7,3},{8,10},{9,13},{10,... | collective-permute-start | bytes 49160 | tf_op jit(solution)/shard_map/ppermute | solution.py:166
  258.4 5.2 %collective-permute-start.44 = (bf16[2,32,128]{2,1,0:T(8,128)(2,1)S(1)}, bf16[2,32,128]{2,1,0:T(8,128)(2,1)S(1)}, u32[]{:S(2)}, u32[]{:S(2)}) collective-permute-start(bf16[2,32,128]{2,1,0:T(8,128)(2,1)S(1)} %get-tuple-element.505), channel_id=1, source_target_pairs={{0,2},{1,5},{2,0},{3,7},{4,6},{5,1},{6,4},{7,3},{8,10},{9,13},{10,... | collective-permute-start | bytes 49160 | tf_op jit(solution)/shard_map/ppermute | solution.py:166
  277.3 4.2 %collective-permute-start.48 = (bf16[2,32,128]{2,1,0:T(8,128)(2,1)S(1)}, bf16[2,32,128]{2,1,0:T(8,128)(2,1)S(1)}, u32[]{:S(2)}, u32[]{:S(2)}) collective-permute-start(bf16[2,32,128]{2,1,0:T(8,128)(2,1)S(1)} %get-tuple-element.519), channel_id=1, source_target_pairs={{0,2},{1,5},{2,0},{3,7},{4,6},{5,1},{6,4},{7,3},{8,10},{9,13},{10,... | collective-permute-start | bytes 49160 | tf_op jit(solution)/shard_map/ppermute | solution.py:166
  (37 other events, 153.0 us)

commit v6 on v5

--- a/solution.py
+++ b/solution.py
@@ -16,7 +16,7 @@
 
 
 def apply_inverse(inverse, vectors):
-    return jnp.einsum("xi,oi->xo", vectors, inverse, precision=lax.Precision.HIGHEST)
+    return jnp.einsum("xi,oi->xo", vectors, inverse, precision=lax.Precision.HIGH)
 
 
 def product_kernel(level, index_ref, history_ref, even_ref, odd_ref, *sum_refs):
@@ -75,15 +75,19 @@
     copies = []
     for source, at, kept in zip(sources, places, held):
         if len(kept.shape) == 4:
-            pieces = [(source.at[at, m], kept.at[m]) for m in range(kept.shape[0])]
+            pieces = [
+                (source.at[at, pl.ds(m, 4)], kept.at[pl.ds(m, 4)]) for m in range(0, kept.shape[0], 4)
+            ]
         else:
             pieces = [(source.at[at], kept)]
         for piece in pieces:
             copies.append(pltpu.make_async_copy(*piece, arrived.at[len(copies)]))
-    for copy in copies:
-        copy.start()
-    for copy in copies:
-        copy.wait()
+    @pl.when(lax.axis_index("row") % 2 == 1)
+    def _():
+        for copy in copies:
+            copy.start()
+        for copy in copies:
+            copy.wait()
 
 
 def stage(after, following):
@@ -91,7 +95,7 @@
     vmem = pl.BlockSpec(memory_space=pltpu.VMEM)
     anywhere = pl.BlockSpec(memory_space=pl.ANY)
     out_shape = [jax.ShapeDtypeStruct(array.shape[1:], array.dtype) for array in arrays]
-    pieces = sum(array.shape[1] if array.ndim == 5 else 1 for array in arrays)
+    pieces = sum(array.shape[1] // 4 if array.ndim == 5 else 1 for array in arrays)
     return pl.pallas_call(
         functools.partial(stage_kernel, places),
         out_shape=out_shape,
@@ -161,7 +165,7 @@
 def reduce_rows(parts):
     count = lax.axis_size("row")
     total = parts[0]
-    for step in (2, 3, 1):
+    for step in (3, 2, 1):
         pairs = [(i, i ^ (2 * step if i % 2 else 2)) for i in range(count)]
         total = total + lax.ppermute(parts[step], "row", pairs).astype(jnp.float32)
     return total

time: 287 us -> 283 us (0.986)
  blocking collectives: 146 us -> 149 us
    all_to_all x13, blocking collectives: 146 us -> 149 us  [share_solved(): lax.all_to_all(copies, AXES, 0, 0, tiled=True, axis_index_groups=gather_g...]
  transfers between devices with their start and end apart: 53 -> 53, of which waited for: 21 -> 18; matrix products, arithmetic and copies ran while one was open for 2% -> 2% of each run, Pallas kernels for 10% -> 10%
where the time goes in v6:
time: 283 us; the launch traced here: 282 us
  blocking collectives  149 us (53%)
  starting transfers between devices  58.9 us (21%)
  Pallas kernels  42.7 us (15%)
  waiting for transfers between devices  18.3 us (6%)
  matrix products  5.82 us (2%)
  local copies, waits for them, and re-layouts  4.4 us (2%)
    all_to_all x13, blocking collectives, share_solved(): lax.all_to_all(copies, AXES, 0, 0, tiled=True, axis_index_groups=gather_g...  149 us
    ppermute x42, starting transfers between devices, reduce_rows(): total = total + lax.ppermute(parts[step], 'row', pairs).astype(jnp.float32)  48.3 us
    pallas_call x14, Pallas kernels, stage(): pl.pallas_call(functools.partial(stage_kernel, places), out_shape=out_sha...  23 us
    pallas_call x14, Pallas kernels, level_terms(): pl.pallas_call(functools.partial(product_kernel, level), out_shape=out_sh...  18.2 us
    ppermute x42, waiting for transfers between devices, reduce_rows(): total = total + lax.ppermute(parts[step], 'row', pairs).astype(jnp.float32)  11.6 us
    all_to_all x1, starting transfers between devices, share_solved(): lax.all_to_all(copies, AXES, 0, 0, tiled=True, axis_index_groups=gather_g...  6.84 us
    all_to_all x1, waiting for transfers between devices, share_solved(): lax.all_to_all(copies, AXES, 0, 0, tiled=True, axis_index_groups=gather_g...  6.1 us
    dot_general x31, matrix products, apply_inverse(): jnp.einsum('xi,oi->xo', vectors, inverse, precision=lax.Precision.HIGH)  5.82 us
  transfers between devices with their start and end apart: 53, of which 18 were waited for; matrix products, arithmetic and copies ran while one was open for 2% of the time, Pallas kernels for 10%

profile of v6, /device:TPU:1, one launch (start us, length us, event | category | flops | bytes accessed | tf_op | source)
XLA Modules:
  0.0 282.2 jit_solution(16003481485397178442)
XLA Ops:
  6.6 6.8 %all-to-all-start = ((bf16[16,2,32,128]{3,2,1,0:T(8,128)(2,1)}), bf16[16,2,32,128]{3,2,1,0:T(8,128)(2,1)S(1)}, u32[]{:S(2)}, u32[]{:S(2)}) async-start(bf16[16,2,32,128]{3,2,1,0:T(8,128)(2,1)} %broadcast_in_dim.54), calls=%async_computation | async-start | bytes 524288 | tf_op jit(solution)/shard_map/all_to_all | solution.py:194
  14.7 6.1 %all-to-all-done = bf16[16,2,32,128]{3,2,1,0:T(8,128)(2,1)S(1)} async-done(((bf16[16,2,32,128]{3,2,1,0:T(8,128)(2,1)}), bf16[16,2,32,128]{3,2,1,0:T(8,128)(2,1)S(1)}, u32[]{:S(2)}, u32[]{:S(2)}) %all-to-all-start) | async-done | bytes 262176 | tf_op jit(solution)/shard_map/all_to_all | solution.py:194
  22.7 4.6 %collective-permute-start.6 = (bf16[2,32,128]{2,1,0:T(8,128)(2,1)S(1)}, bf16[2,32,128]{2,1,0:T(8,128)(2,1)S(1)}, u32[]{:S(2)}, u32[]{:S(2)}) collective-permute-start(bf16[2,32,128]{2,1,0:T(8,128)(2,1)S(1)} %get-tuple-element.358), channel_id=1, source_target_pairs={{0,2},{1,7},{2,0},{3,5},{4,6},{5,3},{6,4},{7,1},{8,10},{9,15},{10,... | collective-permute-start | bytes 49160 | tf_op jit(solution)/shard_map/ppermute | solution.py:170
  28.7 2.7 collective-permute-done.7
  31.4 1.8 shard_map.87
  33.7 11.2 %all_to_all.70 = bf16[16,2,32,128]{3,2,1,0:T(8,128)(2,1)S(1)} all-to-all(bf16[16,2,32,128]{3,2,1,0:T(8,128)(2,1)S(1)} %broadcast_in_dim.55), channel_id=1, replica_groups={{1,9,17,25,33,41,49,57,65,73,81,89,97,105,113,121},{3,11,19,27,35,43,51..., dimensions={0} | all-to-all | bytes 524288 | tf_op jit(solution)/shard_map/all_to_all | solution.py:194
  46.9 1.9 collective-permute-start.10
  49.6 1.9 shard_map.89
  52.2 10.9 %all_to_all.71 = bf16[16,2,32,128]{3,2,1,0:T(8,128)(2,1)S(1)} all-to-all(bf16[16,2,32,128]{3,2,1,0:T(8,128)(2,1)S(1)} %broadcast_in_dim.56), channel_id=1, replica_groups={{1,9,17,25,33,41,49,57,65,73,81,89,97,105,113,121},{3,11,19,27,35,43,51..., dimensions={0} | all-to-all | bytes 524288 | tf_op jit(solution)/shard_map/all_to_all | solution.py:194
  64.4 2.1 collective-permute-start.12
  71.1 11.1 %all_to_all.72 = bf16[16,2,32,128]{3,2,1,0:T(8,128)(2,1)S(1)} all-to-all(bf16[16,2,32,128]{3,2,1,0:T(8,128)(2,1)S(1)} %broadcast_in_dim.57), channel_id=1, replica_groups={{1,9,17,25,33,41,49,57,65,73,81,89,97,105,113,121},{3,11,19,27,35,43,51..., dimensions={0} | all-to-all | bytes 524288 | tf_op jit(solution)/shard_map/all_to_all | solution.py:194
  83.5 1.8 collective-permute-start.15
  89.9 11.3 %all_to_all.73 = bf16[16,2,32,128]{3,2,1,0:T(8,128)(2,1)S(1)} all-to-all(bf16[16,2,32,128]{3,2,1,0:T(8,128)(2,1)S(1)} %broadcast_in_dim.58), channel_id=1, replica_groups={{1,9,17,25,33,41,49,57,65,73,81,89,97,105,113,121},{3,11,19,27,35,43,51..., dimensions={0} | all-to-all | bytes 524288 | tf_op jit(solution)/shard_map/all_to_all | solution.py:194
  105.9 1.8 shard_map.95
  108.6 11.6 %all_to_all.74 = bf16[16,2,32,128]{3,2,1,0:T(8,128)(2,1)S(1)} all-to-all(bf16[16,2,32,128]{3,2,1,0:T(8,128)(2,1)S(1)} %broadcast_in_dim.59), channel_id=1, replica_groups={{1,9,17,25,33,41,49,57,65,73,81,89,97,105,113,121},{3,11,19,27,35,43,51..., dimensions={0} | all-to-all | bytes 524288 | tf_op jit(solution)/shard_map/all_to_all | solution.py:194
  127.8 11.5 %all_to_all.75 = bf16[16,2,32,128]{3,2,1,0:T(8,128)(2,1)S(1)} all-to-all(bf16[16,2,32,128]{3,2,1,0:T(8,128)(2,1)S(1)} %broadcast_in_dim.60), channel_id=1, replica_groups={{1,9,17,25,33,41,49,57,65,73,81,89,97,105,113,121},{3,11,19,27,35,43,51..., dimensions={0} | all-to-all | bytes 524288 | tf_op jit(solution)/shard_map/all_to_all | solution.py:194
  143.9 1.8 shard_map.99
  147.0 11.5 %all_to_all.76 = bf16[16,2,32,128]{3,2,1,0:T(8,128)(2,1)S(1)} all-to-all(bf16[16,2,32,128]{3,2,1,0:T(8,128)(2,1)S(1)} %broadcast_in_dim.61), channel_id=1, replica_groups={{1,9,17,25,33,41,49,57,65,73,81,89,97,105,113,121},{3,11,19,27,35,43,51..., dimensions={0} | all-to-all | bytes 524288 | tf_op jit(solution)/shard_map/all_to_all | solution.py:194
  166.0 11.7 %all_to_all.77 = bf16[16,2,32,128]{3,2,1,0:T(8,128)(2,1)S(1)} all-to-all(bf16[16,2,32,128]{3,2,1,0:T(8,128)(2,1)S(1)} %broadcast_in_dim.62), channel_id=1, replica_groups={{1,9,17,25,33,41,49,57,65,73,81,89,97,105,113,121},{3,11,19,27,35,43,51..., dimensions={0} | all-to-all | bytes 524288 | tf_op jit(solution)/shard_map/all_to_all | solution.py:194
  185.0 11.7 %all_to_all.78 = bf16[16,2,32,128]{3,2,1,0:T(8,128)(2,1)S(1)} all-to-all(bf16[16,2,32,128]{3,2,1,0:T(8,128)(2,1)S(1)} %broadcast_in_dim.63), channel_id=1, replica_groups={{1,9,17,25,33,41,49,57,65,73,81,89,97,105,113,121},{3,11,19,27,35,43,51..., dimensions={0} | all-to-all | bytes 524288 | tf_op jit(solution)/shard_map/all_to_all | solution.py:194
  204.0 11.8 %all_to_all.79 = bf16[16,2,32,128]{3,2,1,0:T(8,128)(2,1)S(1)} all-to-all(bf16[16,2,32,128]{3,2,1,0:T(8,128)(2,1)S(1)} %broadcast_in_dim.64), channel_id=1, replica_groups={{1,9,17,25,33,41,49,57,65,73,81,89,97,105,113,121},{3,11,19,27,35,43,51..., dimensions={0} | all-to-all | bytes 524288 | tf_op jit(solution)/shard_map/all_to_all | solution.py:194
  223.1 11.7 %all_to_all.80 = bf16[16,2,32,128]{3,2,1,0:T(8,128)(2,1)S(1)} all-to-all(bf16[16,2,32,128]{3,2,1,0:T(8,128)(2,1)S(1)} %broadcast_in_dim.65), channel_id=1, replica_groups={{1,9,17,25,33,41,49,57,65,73,81,89,97,105,113,121},{3,11,19,27,35,43,51..., dimensions={0} | all-to-all | bytes 524288 | tf_op jit(solution)/shard_map/all_to_all | solution.py:194
  242.2 11.8 %all_to_all.81 = bf16[16,2,32,128]{3,2,1,0:T(8,128)(2,1)S(1)} all-to-all(bf16[16,2,32,128]{3,2,1,0:T(8,128)(2,1)S(1)} %broadcast_in_dim.66), channel_id=1, replica_groups={{1,9,17,25,33,41,49,57,65,73,81,89,97,105,113,121},{3,11,19,27,35,43,51..., dimensions={0} | all-to-all | bytes 524288 | tf_op jit(solution)/shard_map/all_to_all | solution.py:194
  261.3 11.7 %all_to_all.82 = bf16[16,2,32,128]{3,2,1,0:T(8,128)(2,1)S(1)} all-to-all(bf16[16,2,32,128]{3,2,1,0:T(8,128)(2,1)S(1)} %broadcast_in_dim.67), channel_id=1, replica_groups={{1,9,17,25,33,41,49,57,65,73,81,89,97,105,113,121},{3,11,19,27,35,43,51..., dimensions={0} | all-to-all | bytes 524288 | tf_op jit(solution)/shard_map/all_to_all | solution.py:194
  (266 shorter events, 97.5 us)
Async XLA Ops:
  4.5 26.9 %collective-permute-start.5 = (bf16[7,8,4,128,128]{4,3,2,1,0:T(8,128)(2,1)}, bf16[7,8,4,128,128]{4,3,2,1,0:T(8,128)(2,1)}, u32[]{:S(2)}, u32[]{:S(2)}) collective-permute-start(bf16[7,8,4,128,128]{4,3,2,1,0:T(8,128)(2,1)} %bitcast.300), channel_id=1, source_target_pairs={{0,1},{1,0},{2,3},{3,2},{4,5},{5,4},{6,7},{7,6},{8,9},{9,8},{10,11... | collective-permute-start | bytes 22020104 | tf_op jit(solution)/shard_map/ppermute | solution.py:162
  4.6 16.7 %collective-permute-start.2 = (bf16[8,4,128,128]{3,2,1,0:T(8,128)(2,1)S(1)}, bf16[8,4,128,128]{3,2,1,0:T(8,128)(2,1)S(1)}, u32[]{:S(2)}, u32[]{:S(2)}) collective-permute-start(bf16[8,4,128,128]{3,2,1,0:T(8,128)(2,1)S(1)} %slice_bitcast_fusion.odd_ref), channel_id=1, source_target_pairs={{0,1},{1,0},{2,3},{3,2},{4,5},{5,4},{6,7},{7,6},{8,9},{9,8},{10,11... | collective-permute-start | bytes 3145736 | tf_op jit(solution)/shard_map/ppermute | solution.py:162
  5.7 8.9 %collective-permute-start = (s32[448]{0:T(512)S(1)}, s32[448]{0:T(512)S(1)}, u32[]{:S(2)}, u32[]{:S(2)}) collective-permute-start(s32[448]{0:T(512)S(1)} %pad_add_fusion), channel_id=1, source_target_pairs={{0,1},{1,0},{2,3},{3,2},{4,5},{5,4},{6,7},{7,6},{8,9},{9,8},{10,11... | collective-permute-start | bytes 5384 | tf_op jit(solution)/shard_map/ppermute | solution.py:162
  6.6 14.2 %all-to-all-start = ((bf16[16,2,32,128]{3,2,1,0:T(8,128)(2,1)}), bf16[16,2,32,128]{3,2,1,0:T(8,128)(2,1)S(1)}, u32[]{:S(2)}, u32[]{:S(2)}) async-start(bf16[16,2,32,128]{3,2,1,0:T(8,128)(2,1)} %broadcast_in_dim.54), calls=%async_computation | async-start | bytes 524288 | tf_op jit(solution)/shard_map/all_to_all | solution.py:194
  13.4 18.0 %collective-permute-start.3 = (f32[8,128,128]{2,1,0:T(8,128)S(1)}, f32[8,128,128]{2,1,0:T(8,128)S(1)}, u32[]{:S(2)}, u32[]{:S(2)}) collective-permute-start(f32[8,128,128]{2,1,0:T(8,128)S(1)} %bitcast.271), channel_id=1, source_target_pairs={{0,1},{1,0},{2,3},{3,2},{4,5},{5,4},{6,7},{7,6},{8,9},{9,8},{10,11... | collective-permute-start | bytes 1572872 | tf_op jit(solution)/shard_map/ppermute | solution.py:162
  22.7 5.7 %collective-permute-start.6 = (bf16[2,32,128]{2,1,0:T(8,128)(2,1)S(1)}, bf16[2,32,128]{2,1,0:T(8,128)(2,1)S(1)}, u32[]{:S(2)}, u32[]{:S(2)}) collective-permute-start(bf16[2,32,128]{2,1,0:T(8,128)(2,1)S(1)} %get-tuple-element.358), channel_id=1, source_target_pairs={{0,2},{1,7},{2,0},{3,5},{4,6},{5,3},{6,4},{7,1},{8,10},{9,15},{10,... | collective-permute-start | bytes 49160 | tf_op jit(solution)/shard_map/ppermute | solution.py:170
  46.3 5.2 %collective-permute-start.9 = (bf16[2,32,128]{2,1,0:T(8,128)(2,1)S(1)}, bf16[2,32,128]{2,1,0:T(8,128)(2,1)S(1)}, u32[]{:S(2)}, u32[]{:S(2)}) collective-permute-start(bf16[2,32,128]{2,1,0:T(8,128)(2,1)S(1)} %get-tuple-element.370), channel_id=1, source_target_pairs={{0,2},{1,7},{2,0},{3,5},{4,6},{5,3},{6,4},{7,1},{8,10},{9,15},{10,... | collective-permute-start | bytes 49160 | tf_op jit(solution)/shard_map/ppermute | solution.py:170
  46.9 4.6 %collective-permute-start.10 = (bf16[2,32,128]{2,1,0:T(8,128)(2,1)S(1)}, bf16[2,32,128]{2,1,0:T(8,128)(2,1)S(1)}, u32[]{:S(2)}, u32[]{:S(2)}) collective-permute-start(bf16[2,32,128]{2,1,0:T(8,128)(2,1)S(1)} %get-tuple-element.371), channel_id=1, source_target_pairs={{0,2},{1,5},{2,0},{3,7},{4,6},{5,1},{6,4},{7,3},{8,10},{9,13},{10,... | collective-permute-start | bytes 49160 | tf_op jit(solution)/shard_map/ppermute | solution.py:170
  52.1 56.4 %collective-permute-start.21 = (bf16[7,8,4,128,128]{4,3,2,1,0:T(8,128)(2,1)S(1)}, bf16[7,8,4,128,128]{4,3,2,1,0:T(8,128)(2,1)S(1)}, u32[]{:S(2)}, u32[]{:S(2)}) collective-permute-start(bf16[7,8,4,128,128]{4,3,2,1,0:T(8,128)(2,1)S(1)} %bitcast.298), channel_id=1, source_target_pairs={{0,1},{1,0},{2,3},{3,2},{4,5},{5,4},{6,7},{7,6},{8,9},{9,8},{10,11... | collective-permute-start | bytes 22020104 | tf_op jit(solution)/shard_map/ppermute | solution.py:162
  64.4 5.1 %collective-permute-start.12 = (bf16[2,32,128]{2,1,0:T(8,128)(2,1)S(1)}, bf16[2,32,128]{2,1,0:T(8,128)(2,1)S(1)}, u32[]{:S(2)}, u32[]{:S(2)}) collective-permute-start(bf16[2,32,128]{2,1,0:T(8,128)(2,1)S(1)} %get-tuple-element.386), channel_id=1, source_target_pairs={{0,2},{1,7},{2,0},{3,5},{4,6},{5,3},{6,4},{7,1},{8,10},{9,15},{10,... | collective-permute-start | bytes 49160 | tf_op jit(solution)/shard_map/ppermute | solution.py:170
  66.5 4.1 %collective-permute-start.13 = (bf16[2,32,128]{2,1,0:T(8,128)(2,1)S(1)}, bf16[2,32,128]{2,1,0:T(8,128)(2,1)S(1)}, u32[]{:S(2)}, u32[]{:S(2)}) collective-permute-start(bf16[2,32,128]{2,1,0:T(8,128)(2,1)S(1)} %get-tuple-element.387), channel_id=1, source_target_pairs={{0,2},{1,5},{2,0},{3,7},{4,6},{5,1},{6,4},{7,3},{8,10},{9,13},{10,... | collective-permute-start | bytes 49160 | tf_op jit(solution)/shard_map/ppermute | solution.py:170
  83.5 5.1 %collective-permute-start.15 = (bf16[2,32,128]{2,1,0:T(8,128)(2,1)S(1)}, bf16[2,32,128]{2,1,0:T(8,128)(2,1)S(1)}, u32[]{:S(2)}, u32[]{:S(2)}) collective-permute-start(bf16[2,32,128]{2,1,0:T(8,128)(2,1)S(1)} %get-tuple-element.398), channel_id=1, source_target_pairs={{0,2},{1,7},{2,0},{3,5},{4,6},{5,3},{6,4},{7,1},{8,10},{9,15},{10,... | collective-permute-start | bytes 49160 | tf_op jit(solution)/shard_map/ppermute | solution.py:170
  85.3 4.1 %collective-permute-start.16 = (bf16[2,32,128]{2,1,0:T(8,128)(2,1)S(1)}, bf16[2,32,128]{2,1,0:T(8,128)(2,1)S(1)}, u32[]{:S(2)}, u32[]{:S(2)}) collective-permute-start(bf16[2,32,128]{2,1,0:T(8,128)(2,1)S(1)} %get-tuple-element.399), channel_id=1, source_target_pairs={{0,2},{1,5},{2,0},{3,7},{4,6},{5,1},{6,4},{7,3},{8,10},{9,13},{10,... | collective-permute-start | bytes 49160 | tf_op jit(solution)/shard_map/ppermute | solution.py:170
  102.5 5.1 %collective-permute-start.18 = (bf16[2,32,128]{2,1,0:T(8,128)(2,1)S(1)}, bf16[2,32,128]{2,1,0:T(8,128)(2,1)S(1)}, u32[]{:S(2)}, u32[]{:S(2)}) collective-permute-start(bf16[2,32,128]{2,1,0:T(8,128)(2,1)S(1)} %get-tuple-element.410), channel_id=1, source_target_pairs={{0,2},{1,7},{2,0},{3,5},{4,6},{5,3},{6,4},{7,1},{8,10},{9,15},{10,... | collective-permute-start | bytes 49160 | tf_op jit(solution)/shard_map/ppermute | solution.py:170
  104.0 4.1 %collective-permute-start.19 = (bf16[2,32,128]{2,1,0:T(8,128)(2,1)S(1)}, bf16[2,32,128]{2,1,0:T(8,128)(2,1)S(1)}, u32[]{:S(2)}, u32[]{:S(2)}) collective-permute-start(bf16[2,32,128]{2,1,0:T(8,128)(2,1)S(1)} %get-tuple-element.411), channel_id=1, source_target_pairs={{0,2},{1,5},{2,0},{3,7},{4,6},{5,1},{6,4},{7,3},{8,10},{9,13},{10,... | collective-permute-start | bytes 49160 | tf_op jit(solution)/shard_map/ppermute | solution.py:170
  121.6 5.1 %collective-permute-start.23 = (bf16[2,32,128]{2,1,0:T(8,128)(2,1)S(1)}, bf16[2,32,128]{2,1,0:T(8,128)(2,1)S(1)}, u32[]{:S(2)}, u32[]{:S(2)}) collective-permute-start(bf16[2,32,128]{2,1,0:T(8,128)(2,1)S(1)} %get-tuple-element.426), channel_id=1, source_target_pairs={{0,2},{1,7},{2,0},{3,5},{4,6},{5,3},{6,4},{7,1},{8,10},{9,15},{10,... | collective-permute-start | bytes 49160 | tf_op jit(solution)/shard_map/ppermute | solution.py:170
  140.6 5.1 %collective-permute-start.26 = (bf16[2,32,128]{2,1,0:T(8,128)(2,1)S(1)}, bf16[2,32,128]{2,1,0:T(8,128)(2,1)S(1)}, u32[]{:S(2)}, u32[]{:S(2)}) collective-permute-start(bf16[2,32,128]{2,1,0:T(8,128)(2,1)S(1)} %get-tuple-element.440), channel_id=1, source_target_pairs={{0,2},{1,7},{2,0},{3,5},{4,6},{5,3},{6,4},{7,1},{8,10},{9,15},{10,... | collective-permute-start | bytes 49160 | tf_op jit(solution)/shard_map/ppermute | solution.py:170
  159.8 5.0 %collective-permute-start.29 = (bf16[2,32,128]{2,1,0:T(8,128)(2,1)S(1)}, bf16[2,32,128]{2,1,0:T(8,128)(2,1)S(1)}, u32[]{:S(2)}, u32[]{:S(2)}) collective-permute-start(bf16[2,32,128]{2,1,0:T(8,128)(2,1)S(1)} %get-tuple-element.455), channel_id=1, source_target_pairs={{0,2},{1,7},{2,0},{3,5},{4,6},{5,3},{6,4},{7,1},{8,10},{9,15},{10,... | collective-permute-start | bytes 49160 | tf_op jit(solution)/shard_map/ppermute | solution.py:170
  179.1 5.0 %collective-permute-start.32 = (bf16[2,32,128]{2,1,0:T(8,128)(2,1)S(1)}, bf16[2,32,128]{2,1,0:T(8,128)(2,1)S(1)}, u32[]{:S(2)}, u32[]{:S(2)}) collective-permute-start(bf16[2,32,128]{2,1,0:T(8,128)(2,1)S(1)} %get-tuple-element.465), channel_id=1, source_target_pairs={{0,2},{1,7},{2,0},{3,5},{4,6},{5,3},{6,4},{7,1},{8,10},{9,15},{10,... | collective-permute-start | bytes 49160 | tf_op jit(solution)/shard_map/ppermute | solution.py:170
  198.1 5.0 %collective-permute-start.35 = (bf16[2,32,128]{2,1,0:T(8,128)(2,1)S(1)}, bf16[2,32,128]{2,1,0:T(8,128)(2,1)S(1)}, u32[]{:S(2)}, u32[]{:S(2)}) collective-permute-start(bf16[2,32,128]{2,1,0:T(8,128)(2,1)S(1)} %get-tuple-element.475), channel_id=1, source_target_pairs={{0,2},{1,7},{2,0},{3,5},{4,6},{5,3},{6,4},{7,1},{8,10},{9,15},{10,... | collective-permute-start | bytes 49160 | tf_op jit(solution)/shard_map/ppermute | solution.py:170
  217.2 5.0 %collective-permute-start.38 = (bf16[2,32,128]{2,1,0:T(8,128)(2,1)S(1)}, bf16[2,32,128]{2,1,0:T(8,128)(2,1)S(1)}, u32[]{:S(2)}, u32[]{:S(2)}) collective-permute-start(bf16[2,32,128]{2,1,0:T(8,128)(2,1)S(1)} %get-tuple-element.485), channel_id=1, source_target_pairs={{0,2},{1,7},{2,0},{3,5},{4,6},{5,3},{6,4},{7,1},{8,10},{9,15},{10,... | collective-permute-start | bytes 49160 | tf_op jit(solution)/shard_map/ppermute | solution.py:170
  236.2 5.0 %collective-permute-start.41 = (bf16[2,32,128]{2,1,0:T(8,128)(2,1)S(1)}, bf16[2,32,128]{2,1,0:T(8,128)(2,1)S(1)}, u32[]{:S(2)}, u32[]{:S(2)}) collective-permute-start(bf16[2,32,128]{2,1,0:T(8,128)(2,1)S(1)} %get-tuple-element.495), channel_id=1, source_target_pairs={{0,2},{1,7},{2,0},{3,5},{4,6},{5,3},{6,4},{7,1},{8,10},{9,15},{10,... | collective-permute-start | bytes 49160 | tf_op jit(solution)/shard_map/ppermute | solution.py:170
  237.6 4.1 %collective-permute-start.42 = (bf16[2,32,128]{2,1,0:T(8,128)(2,1)S(1)}, bf16[2,32,128]{2,1,0:T(8,128)(2,1)S(1)}, u32[]{:S(2)}, u32[]{:S(2)}) collective-permute-start(bf16[2,32,128]{2,1,0:T(8,128)(2,1)S(1)} %get-tuple-element.496), channel_id=1, source_target_pairs={{0,2},{1,5},{2,0},{3,7},{4,6},{5,1},{6,4},{7,3},{8,10},{9,13},{10,... | collective-permute-start | bytes 49160 | tf_op jit(solution)/shard_map/ppermute | solution.py:170
  255.3 5.0 %collective-permute-start.44 = (bf16[2,32,128]{2,1,0:T(8,128)(2,1)S(1)}, bf16[2,32,128]{2,1,0:T(8,128)(2,1)S(1)}, u32[]{:S(2)}, u32[]{:S(2)}) collective-permute-start(bf16[2,32,128]{2,1,0:T(8,128)(2,1)S(1)} %get-tuple-element.505), channel_id=1, source_target_pairs={{0,2},{1,7},{2,0},{3,5},{4,6},{5,3},{6,4},{7,1},{8,10},{9,15},{10,... | collective-permute-start | bytes 49160 | tf_op jit(solution)/shard_map/ppermute | solution.py:170
  (37 other events, 156.1 us)

commit v7 on v6

--- a/solution.py
+++ b/solution.py
@@ -9,7 +9,7 @@
 
 BLOCKS_LAST = (((1,), (1,)), ((), ()))
 AXES = ("col", "row")
-PARTIAL_TYPE = jnp.bfloat16
+PARTIAL_TYPE = jnp.float32
 VLIM = 12
 SLIM = 12
 TURN = 2

time: 283 us -> 286 us (1.011)
  waiting for transfers between devices: 18.3 us -> 22.4 us
    ppermute x42, waiting for transfers between devices: 11.6 us -> 15.9 us  [reduce_rows(): total = total + lax.ppermute(parts[step], 'row', pairs).astype(jnp.float32)]
  transfers between devices with their start and end apart: 53 -> 53, of which waited for: 18 -> 19; matrix products, arithmetic and copies ran while one was open for 2% -> 2% of each run, Pallas kernels for 10% -> 10%
where the time goes in v7:
time: 286 us; the launch traced here: 285 us
  blocking collectives  148 us (52%)
  starting transfers between devices  59.2 us (21%)
  Pallas kernels  42.7 us (15%)
  waiting for transfers between devices  22.4 us (8%)
  matrix products  5.82 us (2%)
  local copies, waits for them, and re-layouts  4.36 us (2%)
    all_to_all x13, blocking collectives, share_solved(): lax.all_to_all(copies, AXES, 0, 0, tiled=True, axis_index_groups=gather_g...  148 us
    ppermute x42, starting transfers between devices, reduce_rows(): total = total + lax.ppermute(parts[step], 'row', pairs).astype(jnp.float32)  48.4 us
    pallas_call x14, Pallas kernels, stage(): pl.pallas_call(functools.partial(stage_kernel, places), out_shape=out_sha...  23 us
    pallas_call x14, Pallas kernels, level_terms(): pl.pallas_call(functools.partial(product_kernel, level), out_shape=out_sh...  18.2 us
    ppermute x42, waiting for transfers between devices, reduce_rows(): total = total + lax.ppermute(parts[step], 'row', pairs).astype(jnp.float32)  15.9 us
    all_to_all x1, starting transfers between devices, share_solved(): lax.all_to_all(copies, AXES, 0, 0, tiled=True, axis_index_groups=gather_g...  6.84 us
    all_to_all x1, waiting for transfers between devices, share_solved(): lax.all_to_all(copies, AXES, 0, 0, tiled=True, axis_index_groups=gather_g...  6.1 us
    dot_general x31, matrix products, apply_inverse(): jnp.einsum('xi,oi->xo', vectors, inverse, precision=lax.Precision.HIGH)  5.82 us
  transfers between devices with their start and end apart: 53, of which 19 were waited for; matrix products, arithmetic and copies ran while one was open for 2% of the time, Pallas kernels for 10%

profile of v7, /device:TPU:1, one launch (start us, length us, event | category | flops | bytes accessed | tf_op | source)
XLA Modules:
  0.0 285.4 jit_solution(14426837661574264634)
XLA Ops:
  6.6 6.8 %all-to-all-start = ((bf16[16,2,32,128]{3,2,1,0:T(8,128)(2,1)}), bf16[16,2,32,128]{3,2,1,0:T(8,128)(2,1)S(1)}, u32[]{:S(2)}, u32[]{:S(2)}) async-start(bf16[16,2,32,128]{3,2,1,0:T(8,128)(2,1)} %broadcast_in_dim.54), calls=%async_computation | async-start | bytes 524288 | tf_op jit(solution)/shard_map/all_to_all | solution.py:194
  14.7 6.1 %all-to-all-done = bf16[16,2,32,128]{3,2,1,0:T(8,128)(2,1)S(1)} async-done(((bf16[16,2,32,128]{3,2,1,0:T(8,128)(2,1)}), bf16[16,2,32,128]{3,2,1,0:T(8,128)(2,1)S(1)}, u32[]{:S(2)}, u32[]{:S(2)}) %all-to-all-start) | async-done | bytes 262176 | tf_op jit(solution)/shard_map/all_to_all | solution.py:194
  22.7 4.6 %collective-permute-start.6 = (f32[2,32,128]{2,1,0:T(8,128)S(1)}, f32[2,32,128]{2,1,0:T(8,128)S(1)}, u32[]{:S(2)}, u32[]{:S(2)}) collective-permute-start(f32[2,32,128]{2,1,0:T(8,128)S(1)} %get-tuple-element.358), channel_id=1, source_target_pairs={{0,2},{1,7},{2,0},{3,5},{4,6},{5,3},{6,4},{7,1},{8,10},{9,15},{10,... | collective-permute-start | bytes 98312 | tf_op jit(solution)/shard_map/ppermute | solution.py:170
  28.8 2.7 collective-permute-done.7
  31.6 1.8 shard_map.87
  33.9 11.2 %all_to_all.70 = bf16[16,2,32,128]{3,2,1,0:T(8,128)(2,1)S(1)} all-to-all(bf16[16,2,32,128]{3,2,1,0:T(8,128)(2,1)S(1)} %broadcast_in_dim.55), channel_id=1, replica_groups={{1,9,17,25,33,41,49,57,65,73,81,89,97,105,113,121},{3,11,19,27,35,43,51..., dimensions={0} | all-to-all | bytes 524288 | tf_op jit(solution)/shard_map/all_to_all | solution.py:194
  49.8 1.9 shard_map.89
  52.4 11.4 %all_to_all.71 = bf16[16,2,32,128]{3,2,1,0:T(8,128)(2,1)S(1)} all-to-all(bf16[16,2,32,128]{3,2,1,0:T(8,128)(2,1)S(1)} %broadcast_in_dim.56), channel_id=1, replica_groups={{1,9,17,25,33,41,49,57,65,73,81,89,97,105,113,121},{3,11,19,27,35,43,51..., dimensions={0} | all-to-all | bytes 524288 | tf_op jit(solution)/shard_map/all_to_all | solution.py:194
  71.6 11.2 %all_to_all.72 = bf16[16,2,32,128]{3,2,1,0:T(8,128)(2,1)S(1)} all-to-all(bf16[16,2,32,128]{3,2,1,0:T(8,128)(2,1)S(1)} %broadcast_in_dim.57), channel_id=1, replica_groups={{1,9,17,25,33,41,49,57,65,73,81,89,97,105,113,121},{3,11,19,27,35,43,51..., dimensions={0} | all-to-all | bytes 524288 | tf_op jit(solution)/shard_map/all_to_all | solution.py:194
  90.8 11.3 %all_to_all.73 = bf16[16,2,32,128]{3,2,1,0:T(8,128)(2,1)S(1)} all-to-all(bf16[16,2,32,128]{3,2,1,0:T(8,128)(2,1)S(1)} %broadcast_in_dim.58), channel_id=1, replica_groups={{1,9,17,25,33,41,49,57,65,73,81,89,97,105,113,121},{3,11,19,27,35,43,51..., dimensions={0} | all-to-all | bytes 524288 | tf_op jit(solution)/shard_map/all_to_all | solution.py:194
  109.7 11.4 %all_to_all.74 = bf16[16,2,32,128]{3,2,1,0:T(8,128)(2,1)S(1)} all-to-all(bf16[16,2,32,128]{3,2,1,0:T(8,128)(2,1)S(1)} %broadcast_in_dim.59), channel_id=1, replica_groups={{1,9,17,25,33,41,49,57,65,73,81,89,97,105,113,121},{3,11,19,27,35,43,51..., dimensions={0} | all-to-all | bytes 524288 | tf_op jit(solution)/shard_map/all_to_all | solution.py:194
  122.4 2.1 collective-permute-start.23
  129.2 11.4 %all_to_all.75 = bf16[16,2,32,128]{3,2,1,0:T(8,128)(2,1)S(1)} all-to-all(bf16[16,2,32,128]{3,2,1,0:T(8,128)(2,1)S(1)} %broadcast_in_dim.60), channel_id=1, replica_groups={{1,9,17,25,33,41,49,57,65,73,81,89,97,105,113,121},{3,11,19,27,35,43,51..., dimensions={0} | all-to-all | bytes 524288 | tf_op jit(solution)/shard_map/all_to_all | solution.py:194
  148.4 11.8 %all_to_all.76 = bf16[16,2,32,128]{3,2,1,0:T(8,128)(2,1)S(1)} all-to-all(bf16[16,2,32,128]{3,2,1,0:T(8,128)(2,1)S(1)} %broadcast_in_dim.61), channel_id=1, replica_groups={{1,9,17,25,33,41,49,57,65,73,81,89,97,105,113,121},{3,11,19,27,35,43,51..., dimensions={0} | all-to-all | bytes 524288 | tf_op jit(solution)/shard_map/all_to_all | solution.py:194
  168.0 11.3 %all_to_all.77 = bf16[16,2,32,128]{3,2,1,0:T(8,128)(2,1)S(1)} all-to-all(bf16[16,2,32,128]{3,2,1,0:T(8,128)(2,1)S(1)} %broadcast_in_dim.62), channel_id=1, replica_groups={{1,9,17,25,33,41,49,57,65,73,81,89,97,105,113,121},{3,11,19,27,35,43,51..., dimensions={0} | all-to-all | bytes 524288 | tf_op jit(solution)/shard_map/all_to_all | solution.py:194
  180.6 2.0 collective-permute-start.32
  187.4 11.4 %all_to_all.78 = bf16[16,2,32,128]{3,2,1,0:T(8,128)(2,1)S(1)} all-to-all(bf16[16,2,32,128]{3,2,1,0:T(8,128)(2,1)S(1)} %broadcast_in_dim.63), channel_id=1, replica_groups={{1,9,17,25,33,41,49,57,65,73,81,89,97,105,113,121},{3,11,19,27,35,43,51..., dimensions={0} | all-to-all | bytes 524288 | tf_op jit(solution)/shard_map/all_to_all | solution.py:194
  206.5 11.3 %all_to_all.79 = bf16[16,2,32,128]{3,2,1,0:T(8,128)(2,1)S(1)} all-to-all(bf16[16,2,32,128]{3,2,1,0:T(8,128)(2,1)S(1)} %broadcast_in_dim.64), channel_id=1, replica_groups={{1,9,17,25,33,41,49,57,65,73,81,89,97,105,113,121},{3,11,19,27,35,43,51..., dimensions={0} | all-to-all | bytes 524288 | tf_op jit(solution)/shard_map/all_to_all | solution.py:194
  219.2 1.9 collective-permute-start.38
  225.9 11.4 %all_to_all.80 = bf16[16,2,32,128]{3,2,1,0:T(8,128)(2,1)S(1)} all-to-all(bf16[16,2,32,128]{3,2,1,0:T(8,128)(2,1)S(1)} %broadcast_in_dim.65), channel_id=1, replica_groups={{1,9,17,25,33,41,49,57,65,73,81,89,97,105,113,121},{3,11,19,27,35,43,51..., dimensions={0} | all-to-all | bytes 524288 | tf_op jit(solution)/shard_map/all_to_all | solution.py:194
  244.9 11.5 %all_to_all.81 = bf16[16,2,32,128]{3,2,1,0:T(8,128)(2,1)S(1)} all-to-all(bf16[16,2,32,128]{3,2,1,0:T(8,128)(2,1)S(1)} %broadcast_in_dim.66), channel_id=1, replica_groups={{1,9,17,25,33,41,49,57,65,73,81,89,97,105,113,121},{3,11,19,27,35,43,51..., dimensions={0} | all-to-all | bytes 524288 | tf_op jit(solution)/shard_map/all_to_all | solution.py:194
  257.7 1.9 collective-permute-start.44
  264.4 11.4 %all_to_all.82 = bf16[16,2,32,128]{3,2,1,0:T(8,128)(2,1)S(1)} all-to-all(bf16[16,2,32,128]{3,2,1,0:T(8,128)(2,1)S(1)} %broadcast_in_dim.67), channel_id=1, replica_groups={{1,9,17,25,33,41,49,57,65,73,81,89,97,105,113,121},{3,11,19,27,35,43,51..., dimensions={0} | all-to-all | bytes 524288 | tf_op jit(solution)/shard_map/all_to_all | solution.py:194
  281.3 1.9 collective-permute-done.49
  (266 shorter events, 101.4 us)
Async XLA Ops:
  4.5 27.0 %collective-permute-start.5 = (bf16[7,8,4,128,128]{4,3,2,1,0:T(8,128)(2,1)}, bf16[7,8,4,128,128]{4,3,2,1,0:T(8,128)(2,1)}, u32[]{:S(2)}, u32[]{:S(2)}) collective-permute-start(bf16[7,8,4,128,128]{4,3,2,1,0:T(8,128)(2,1)} %bitcast.300), channel_id=1, source_target_pairs={{0,1},{1,0},{2,3},{3,2},{4,5},{5,4},{6,7},{7,6},{8,9},{9,8},{10,11... | collective-permute-start | bytes 22020104 | tf_op jit(solution)/shard_map/ppermute | solution.py:162
  4.6 16.7 %collective-permute-start.2 = (bf16[8,4,128,128]{3,2,1,0:T(8,128)(2,1)S(1)}, bf16[8,4,128,128]{3,2,1,0:T(8,128)(2,1)S(1)}, u32[]{:S(2)}, u32[]{:S(2)}) collective-permute-start(bf16[8,4,128,128]{3,2,1,0:T(8,128)(2,1)S(1)} %slice_bitcast_fusion.odd_ref), channel_id=1, source_target_pairs={{0,1},{1,0},{2,3},{3,2},{4,5},{5,4},{6,7},{7,6},{8,9},{9,8},{10,11... | collective-permute-start | bytes 3145736 | tf_op jit(solution)/shard_map/ppermute | solution.py:162
  5.7 8.9 %collective-permute-start = (s32[448]{0:T(512)S(1)}, s32[448]{0:T(512)S(1)}, u32[]{:S(2)}, u32[]{:S(2)}) collective-permute-start(s32[448]{0:T(512)S(1)} %pad_add_fusion), channel_id=1, source_target_pairs={{0,1},{1,0},{2,3},{3,2},{4,5},{5,4},{6,7},{7,6},{8,9},{9,8},{10,11... | collective-permute-start | bytes 5384 | tf_op jit(solution)/shard_map/ppermute | solution.py:162
  6.6 14.2 %all-to-all-start = ((bf16[16,2,32,128]{3,2,1,0:T(8,128)(2,1)}), bf16[16,2,32,128]{3,2,1,0:T(8,128)(2,1)S(1)}, u32[]{:S(2)}, u32[]{:S(2)}) async-start(bf16[16,2,32,128]{3,2,1,0:T(8,128)(2,1)} %broadcast_in_dim.54), calls=%async_computation | async-start | bytes 524288 | tf_op jit(solution)/shard_map/all_to_all | solution.py:194
  13.4 18.2 %collective-permute-start.3 = (f32[8,128,128]{2,1,0:T(8,128)S(1)}, f32[8,128,128]{2,1,0:T(8,128)S(1)}, u32[]{:S(2)}, u32[]{:S(2)}) collective-permute-start(f32[8,128,128]{2,1,0:T(8,128)S(1)} %bitcast.271), channel_id=1, source_target_pairs={{0,1},{1,0},{2,3},{3,2},{4,5},{5,4},{6,7},{7,6},{8,9},{9,8},{10,11... | collective-permute-start | bytes 1572872 | tf_op jit(solution)/shard_map/ppermute | solution.py:162
  22.7 5.9 %collective-permute-start.6 = (f32[2,32,128]{2,1,0:T(8,128)S(1)}, f32[2,32,128]{2,1,0:T(8,128)S(1)}, u32[]{:S(2)}, u32[]{:S(2)}) collective-permute-start(f32[2,32,128]{2,1,0:T(8,128)S(1)} %get-tuple-element.358), channel_id=1, source_target_pairs={{0,2},{1,7},{2,0},{3,5},{4,6},{5,3},{6,4},{7,1},{8,10},{9,15},{10,... | collective-permute-start | bytes 98312 | tf_op jit(solution)/shard_map/ppermute | solution.py:170
  27.3 4.3 %collective-permute-start.7 = (f32[2,32,128]{2,1,0:T(8,128)S(1)}, f32[2,32,128]{2,1,0:T(8,128)S(1)}, u32[]{:S(2)}, u32[]{:S(2)}) collective-permute-start(f32[2,32,128]{2,1,0:T(8,128)S(1)} %get-tuple-element.359), channel_id=1, source_target_pairs={{0,2},{1,5},{2,0},{3,7},{4,6},{5,1},{6,4},{7,3},{8,10},{9,13},{10,... | collective-permute-start | bytes 98312 | tf_op jit(solution)/shard_map/ppermute | solution.py:170
  46.5 5.2 %collective-permute-start.9 = (f32[2,32,128]{2,1,0:T(8,128)S(1)}, f32[2,32,128]{2,1,0:T(8,128)S(1)}, u32[]{:S(2)}, u32[]{:S(2)}) collective-permute-start(f32[2,32,128]{2,1,0:T(8,128)S(1)} %get-tuple-element.370), channel_id=1, source_target_pairs={{0,2},{1,7},{2,0},{3,5},{4,6},{5,3},{6,4},{7,1},{8,10},{9,15},{10,... | collective-permute-start | bytes 98312 | tf_op jit(solution)/shard_map/ppermute | solution.py:170
  47.5 4.3 %collective-permute-start.10 = (f32[2,32,128]{2,1,0:T(8,128)S(1)}, f32[2,32,128]{2,1,0:T(8,128)S(1)}, u32[]{:S(2)}, u32[]{:S(2)}) collective-permute-start(f32[2,32,128]{2,1,0:T(8,128)S(1)} %get-tuple-element.371), channel_id=1, source_target_pairs={{0,2},{1,5},{2,0},{3,7},{4,6},{5,1},{6,4},{7,3},{8,10},{9,13},{10,... | collective-permute-start | bytes 98312 | tf_op jit(solution)/shard_map/ppermute | solution.py:170
  52.3 57.2 %collective-permute-start.21 = (bf16[7,8,4,128,128]{4,3,2,1,0:T(8,128)(2,1)S(1)}, bf16[7,8,4,128,128]{4,3,2,1,0:T(8,128)(2,1)S(1)}, u32[]{:S(2)}, u32[]{:S(2)}) collective-permute-start(bf16[7,8,4,128,128]{4,3,2,1,0:T(8,128)(2,1)S(1)} %bitcast.298), channel_id=1, source_target_pairs={{0,1},{1,0},{2,3},{3,2},{4,5},{5,4},{6,7},{7,6},{8,9},{9,8},{10,11... | collective-permute-start | bytes 22020104 | tf_op jit(solution)/shard_map/ppermute | solution.py:162
  65.2 5.1 %collective-permute-start.12 = (f32[2,32,128]{2,1,0:T(8,128)S(1)}, f32[2,32,128]{2,1,0:T(8,128)S(1)}, u32[]{:S(2)}, u32[]{:S(2)}) collective-permute-start(f32[2,32,128]{2,1,0:T(8,128)S(1)} %get-tuple-element.386), channel_id=1, source_target_pairs={{0,2},{1,7},{2,0},{3,5},{4,6},{5,3},{6,4},{7,1},{8,10},{9,15},{10,... | collective-permute-start | bytes 98312 | tf_op jit(solution)/shard_map/ppermute | solution.py:170
  66.9 4.3 %collective-permute-start.13 = (f32[2,32,128]{2,1,0:T(8,128)S(1)}, f32[2,32,128]{2,1,0:T(8,128)S(1)}, u32[]{:S(2)}, u32[]{:S(2)}) collective-permute-start(f32[2,32,128]{2,1,0:T(8,128)S(1)} %get-tuple-element.387), channel_id=1, source_target_pairs={{0,2},{1,5},{2,0},{3,7},{4,6},{5,1},{6,4},{7,3},{8,10},{9,13},{10,... | collective-permute-start | bytes 98312 | tf_op jit(solution)/shard_map/ppermute | solution.py:170
  84.2 5.1 %collective-permute-start.15 = (f32[2,32,128]{2,1,0:T(8,128)S(1)}, f32[2,32,128]{2,1,0:T(8,128)S(1)}, u32[]{:S(2)}, u32[]{:S(2)}) collective-permute-start(f32[2,32,128]{2,1,0:T(8,128)S(1)} %get-tuple-element.398), channel_id=1, source_target_pairs={{0,2},{1,7},{2,0},{3,5},{4,6},{5,3},{6,4},{7,1},{8,10},{9,15},{10,... | collective-permute-start | bytes 98312 | tf_op jit(solution)/shard_map/ppermute | solution.py:170
  103.5 5.1 %collective-permute-start.18 = (f32[2,32,128]{2,1,0:T(8,128)S(1)}, f32[2,32,128]{2,1,0:T(8,128)S(1)}, u32[]{:S(2)}, u32[]{:S(2)}) collective-permute-start(f32[2,32,128]{2,1,0:T(8,128)S(1)} %get-tuple-element.410), channel_id=1, source_target_pairs={{0,2},{1,7},{2,0},{3,5},{4,6},{5,3},{6,4},{7,1},{8,10},{9,15},{10,... | collective-permute-start | bytes 98312 | tf_op jit(solution)/shard_map/ppermute | solution.py:170
  104.9 4.3 %collective-permute-start.19 = (f32[2,32,128]{2,1,0:T(8,128)S(1)}, f32[2,32,128]{2,1,0:T(8,128)S(1)}, u32[]{:S(2)}, u32[]{:S(2)}) collective-permute-start(f32[2,32,128]{2,1,0:T(8,128)S(1)} %get-tuple-element.411), channel_id=1, source_target_pairs={{0,2},{1,5},{2,0},{3,7},{4,6},{5,1},{6,4},{7,3},{8,10},{9,13},{10,... | collective-permute-start | bytes 98312 | tf_op jit(solution)/shard_map/ppermute | solution.py:170
  122.4 5.1 %collective-permute-start.23 = (f32[2,32,128]{2,1,0:T(8,128)S(1)}, f32[2,32,128]{2,1,0:T(8,128)S(1)}, u32[]{:S(2)}, u32[]{:S(2)}) collective-permute-start(f32[2,32,128]{2,1,0:T(8,128)S(1)} %get-tuple-element.426), channel_id=1, source_target_pairs={{0,2},{1,7},{2,0},{3,5},{4,6},{5,3},{6,4},{7,1},{8,10},{9,15},{10,... | collective-permute-start | bytes 98312 | tf_op jit(solution)/shard_map/ppermute | solution.py:170
  142.0 5.1 %collective-permute-start.26 = (f32[2,32,128]{2,1,0:T(8,128)S(1)}, f32[2,32,128]{2,1,0:T(8,128)S(1)}, u32[]{:S(2)}, u32[]{:S(2)}) collective-permute-start(f32[2,32,128]{2,1,0:T(8,128)S(1)} %get-tuple-element.440), channel_id=1, source_target_pairs={{0,2},{1,7},{2,0},{3,5},{4,6},{5,3},{6,4},{7,1},{8,10},{9,15},{10,... | collective-permute-start | bytes 98312 | tf_op jit(solution)/shard_map/ppermute | solution.py:170
  161.6 5.0 %collective-permute-start.29 = (f32[2,32,128]{2,1,0:T(8,128)S(1)}, f32[2,32,128]{2,1,0:T(8,128)S(1)}, u32[]{:S(2)}, u32[]{:S(2)}) collective-permute-start(f32[2,32,128]{2,1,0:T(8,128)S(1)} %get-tuple-element.455), channel_id=1, source_target_pairs={{0,2},{1,7},{2,0},{3,5},{4,6},{5,3},{6,4},{7,1},{8,10},{9,15},{10,... | collective-permute-start | bytes 98312 | tf_op jit(solution)/shard_map/ppermute | solution.py:170
  180.6 5.0 %collective-permute-start.32 = (f32[2,32,128]{2,1,0:T(8,128)S(1)}, f32[2,32,128]{2,1,0:T(8,128)S(1)}, u32[]{:S(2)}, u32[]{:S(2)}) collective-permute-start(f32[2,32,128]{2,1,0:T(8,128)S(1)} %get-tuple-element.465), channel_id=1, source_target_pairs={{0,2},{1,7},{2,0},{3,5},{4,6},{5,3},{6,4},{7,1},{8,10},{9,15},{10,... | collective-permute-start | bytes 98312 | tf_op jit(solution)/shard_map/ppermute | solution.py:170
  200.2 5.0 %collective-permute-start.35 = (f32[2,32,128]{2,1,0:T(8,128)S(1)}, f32[2,32,128]{2,1,0:T(8,128)S(1)}, u32[]{:S(2)}, u32[]{:S(2)}) collective-permute-start(f32[2,32,128]{2,1,0:T(8,128)S(1)} %get-tuple-element.475), channel_id=1, source_target_pairs={{0,2},{1,7},{2,0},{3,5},{4,6},{5,3},{6,4},{7,1},{8,10},{9,15},{10,... | collective-permute-start | bytes 98312 | tf_op jit(solution)/shard_map/ppermute | solution.py:170
  219.2 5.0 %collective-permute-start.38 = (f32[2,32,128]{2,1,0:T(8,128)S(1)}, f32[2,32,128]{2,1,0:T(8,128)S(1)}, u32[]{:S(2)}, u32[]{:S(2)}) collective-permute-start(f32[2,32,128]{2,1,0:T(8,128)S(1)} %get-tuple-element.485), channel_id=1, source_target_pairs={{0,2},{1,7},{2,0},{3,5},{4,6},{5,3},{6,4},{7,1},{8,10},{9,15},{10,... | collective-permute-start | bytes 98312 | tf_op jit(solution)/shard_map/ppermute | solution.py:170
  238.7 5.0 %collective-permute-start.41 = (f32[2,32,128]{2,1,0:T(8,128)S(1)}, f32[2,32,128]{2,1,0:T(8,128)S(1)}, u32[]{:S(2)}, u32[]{:S(2)}) collective-permute-start(f32[2,32,128]{2,1,0:T(8,128)S(1)} %get-tuple-element.495), channel_id=1, source_target_pairs={{0,2},{1,7},{2,0},{3,5},{4,6},{5,3},{6,4},{7,1},{8,10},{9,15},{10,... | collective-permute-start | bytes 98312 | tf_op jit(solution)/shard_map/ppermute | solution.py:170
  240.1 4.3 %collective-permute-start.42 = (f32[2,32,128]{2,1,0:T(8,128)S(1)}, f32[2,32,128]{2,1,0:T(8,128)S(1)}, u32[]{:S(2)}, u32[]{:S(2)}) collective-permute-start(f32[2,32,128]{2,1,0:T(8,128)S(1)} %get-tuple-element.496), channel_id=1, source_target_pairs={{0,2},{1,5},{2,0},{3,7},{4,6},{5,1},{6,4},{7,3},{8,10},{9,13},{10,... | collective-permute-start | bytes 98312 | tf_op jit(solution)/shard_map/ppermute | solution.py:170
  257.7 5.0 %collective-permute-start.44 = (f32[2,32,128]{2,1,0:T(8,128)S(1)}, f32[2,32,128]{2,1,0:T(8,128)S(1)}, u32[]{:S(2)}, u32[]{:S(2)}) collective-permute-start(f32[2,32,128]{2,1,0:T(8,128)S(1)} %get-tuple-element.505), channel_id=1, source_target_pairs={{0,2},{1,7},{2,0},{3,5},{4,6},{5,3},{6,4},{7,1},{8,10},{9,15},{10,... | collective-permute-start | bytes 98312 | tf_op jit(solution)/shard_map/ppermute | solution.py:170
  (37 other events, 163.3 us)
